TPU v7x, 256 devices: a whole 4x4x8 slice. The times are simulated.
256 devices in a mesh: ctx: 64 (over z, y, core), tp: 4 (over x).
Axes of the slice: x: 4, y: 4, z: 8, core: 2. Of those that a mesh axis runs over, the one named last changes fastest.
Arguments:
- tokens: bfloat16 [65536, 4096], P('ctx', 'tp'), may hold values from -6 to 6
- chosen: int32 [4096], P('ctx'), may hold values from 0 to 65535, as said below
- router: bfloat16 [4096], replicated, may hold values from -0.09375 to 0.09375
- w_query: bfloat16 [4096, 2048], P(None, 'tp')
- w_key: bfloat16 [4096, 512], P(None, 'tp')
- w_value: bfloat16 [4096, 512], P(None, 'tp'), may hold values from -0.09375 to 0.09375
- w_out: bfloat16 [2048, 4096], P('tp'), may hold values from -0.5 to 0.5
- cotangent: bfloat16 [65536, 4096], P('ctx', 'tp'), may hold values from -6 to 6
Outputs:
- mixed: bfloat16 [65536, 4096], P('ctx', 'tp')
- input_grad: bfloat16 [65536, 4096], P('ctx', 'tp')
Inputs may be any that keep to these rules, and one draw needn't show every extreme that they name: Entries 64 * b to 64 * (b + 1) - 1 hold, in increasing order, 64 different positions of block b, which is positions 1024 * b to 1024 * (b + 1) - 1. The first and the last position of the sequence are always chosen.
All inputs are finite; a program needn't handle non-finite values.
Results may differ from a plain program's by a relative error of at most 0.011.
Values may be sent and summed in bfloat16 or wider, within the bound.
No kernel may reach another device: no remote copies, remote signals or barrier semaphores. Data moves between devices by JAX's collectives and lax.ppermute only.
A program may use at most 128 MiB of HBM per device.

v0:
```python
import math

import jax
import jax.numpy as jnp
from jax import lax
from jax.sharding import PartitionSpec as P

HEAD_DIM = 128


EPS = 1e-05
FLOOR = -1e30


def times_transposed(left_rows, weight_matrix):
    return lax.dot_general(
        left_rows, weight_matrix, (((1,), (1,)), ((), ())), preferred_element_type=jnp.float32
    )


def on_device(tokens, chosen, router, w_query, w_key, w_value, w_out, cotangent):
    picked = chosen.shape[0]
    tok_rows = tokens.shape[0]
    part_width = tokens.shape[1]
    devices = lax.axis_size("ctx")
    ctx_index = lax.axis_index("ctx")
    tp_index = lax.axis_index("tp")
    local_rows = chosen - ctx_index * tok_rows
    rows_in = tokens[local_rows]
    rows_grad = cotangent[local_rows]
    full_in, full_grad = (
        lax.all_gather(rows_in, "tp", axis=1, tiled=True),
        lax.all_gather(rows_grad, "tp", axis=1, tiled=True),
    )
    wide_in = full_in.astype(jnp.float32)
    gating = jax.nn.sigmoid(jnp.dot(full_in, router, preferred_element_type=jnp.float32))
    inverse = lax.rsqrt(jnp.mean(wide_in * wide_in, axis=1) + EPS)
    normed = (wide_in * inverse[:, None]).astype(jnp.bfloat16)
    queries = jnp.dot(normed, w_query, preferred_element_type=jnp.float32).astype(jnp.bfloat16)
    keys_own = jnp.dot(normed, w_key, preferred_element_type=jnp.float32).astype(jnp.bfloat16)
    values_own = jnp.dot(normed, w_value, preferred_element_type=jnp.float32).astype(jnp.bfloat16)
    kv_width = keys_own.shape[1]
    kv_count = kv_width // HEAD_DIM
    head_count = queries.shape[1] // HEAD_DIM
    group_size = head_count // kv_count
    logit_scale = 1.0 / math.sqrt(HEAD_DIM)
    gathered = lax.all_gather(
        jnp.concatenate([keys_own, values_own], axis=1), "ctx", axis=0, tiled=True
    )
    chosen_total = gathered.shape[0]
    key_all = gathered[:, :kv_width].reshape(chosen_total, kv_count, HEAD_DIM)
    value_all = gathered[:, kv_width:].reshape(chosen_total, kv_count, HEAD_DIM)
    shard_group = 1
    while shard_group * 2 <= devices and shard_group * 2 * picked <= 512:
        shard_group = shard_group * 2
    block_rows = shard_group * picked
    block_count = devices // shard_group
    half_rows = picked // 2
    offsets = jnp.arange(picked, dtype=jnp.int32)
    query_ranks = jnp.where(
        offsets < half_rows, ctx_index * picked + offsets, ctx_index * picked + offsets
    )
    spans = [(0, picked)]
    query_proc = jnp.concatenate([queries[:half_rows], queries[half_rows:]], axis=0)
    query_heads = query_proc.reshape(picked, kv_count, group_size, HEAD_DIM)

    def block_scores(query_rows, ranks, start):
        key_block = lax.dynamic_slice_in_dim(key_all, start, block_rows, 0)
        value_block = lax.dynamic_slice_in_dim(value_all, start, block_rows, 0)
        logits = (
            jnp.einsum("rkgd,ckd->kgrc", query_rows, key_block, preferred_element_type=jnp.float32)
            * logit_scale
        )
        block_ranks = start + jnp.arange(block_rows, dtype=jnp.int32)
        allowed = block_ranks[None, :] <= ranks[:, None]
        return (jnp.where(allowed[None, None], logits, -jnp.inf), key_block, value_block)

    def over_blocks(update, carry, top_rank):

        def turn(block_index, state):
            start = block_index * block_rows
            return lax.cond(
                start <= top_rank,
                lambda inner_state: update(inner_state, start),
                lambda inner_state: inner_state,
                state,
            )

        return lax.fori_loop(0, block_count, turn, carry)

    def forward_group(query_rows, ranks):
        rows = query_rows.shape[0]
        top_rank = jnp.max(ranks)

        def stats_step(state, start):
            running_top, running_sum = state
            scores, key_block, value_block = block_scores(query_rows, ranks, start)
            new_top = jnp.maximum(running_top, jnp.max(scores, axis=3, keepdims=True))
            new_sum = running_sum * jnp.exp(running_top - new_top) + jnp.sum(
                jnp.exp(scores - new_top), axis=3, keepdims=True
            )
            return (new_top, new_sum)

        start_top = jnp.full((kv_count, group_size, rows, 1), FLOOR, jnp.float32)
        start_sum = jnp.zeros((kv_count, group_size, rows, 1), jnp.float32)
        row_top, row_sum = over_blocks(stats_step, (start_top, start_sum), top_rank)

        def output_step(total, start):
            scores, key_block, value_block = block_scores(query_rows, ranks, start)
            probs_low = (jnp.exp(scores - row_top) / row_sum).astype(jnp.bfloat16)
            return total + jnp.einsum(
                "kgrc,ckd->rkgd", probs_low, value_block, preferred_element_type=jnp.float32
            )

        output = over_blocks(
            output_step, jnp.zeros((rows, kv_count, group_size, HEAD_DIM), jnp.float32), top_rank
        )
        return (output, row_top, row_sum)

    forward_parts = [forward_group(query_heads, query_ranks) for first, last in spans]
    attended = jnp.concatenate([part[0] for part in forward_parts], axis=0)
    row_top = jnp.concatenate([part[1] for part in forward_parts], axis=2)
    row_sum = jnp.concatenate([part[2] for part in forward_parts], axis=2)
    out_proc = attended.reshape(picked, head_count * HEAD_DIM).astype(jnp.bfloat16)
    out_home = jnp.concatenate([out_proc[:half_rows], out_proc[half_rows:]], axis=0)
    partial_branch = jnp.dot(out_home, w_out, preferred_element_type=jnp.float32)
    branch_full = lax.psum(partial_branch.astype(jnp.bfloat16), "tp").astype(jnp.float32)
    gate_dot = jnp.sum(full_grad.astype(jnp.float32) * branch_full, axis=1)
    branch_mine = lax.dynamic_slice_in_dim(branch_full, tp_index * part_width, part_width, 1)
    mixed_rows = (rows_in.astype(jnp.float32) + gating[:, None] * branch_mine).astype(jnp.bfloat16)
    mixed = tokens.at[local_rows].set(mixed_rows)
    logit_grad = gate_dot * gating * (1.0 - gating)
    branch_grad = (gating[:, None] * full_grad.astype(jnp.float32)).astype(jnp.bfloat16)
    attended_grad = times_transposed(branch_grad, w_out).astype(jnp.bfloat16)
    grad_proc = jnp.concatenate([attended_grad[:half_rows], attended_grad[half_rows:]], axis=0)
    grad_heads = grad_proc.reshape(picked, kv_count, group_size, HEAD_DIM)
    kv_buffer = jnp.zeros((chosen_total, 2 * kv_width), jnp.float32)
    group_top = row_top
    group_sum = row_sum
    rows = query_heads.shape[0]
    top_rank = jnp.max(query_ranks)

    def inner_step(total, start):
        scores, key_block, value_block = block_scores(query_heads, query_ranks, start)
        probabilities = jnp.exp(scores - group_top) / group_sum
        prob_grad = jnp.einsum(
            "rkgd,ckd->kgrc", grad_heads, value_block, preferred_element_type=jnp.float32
        )
        return total + jnp.sum(probabilities * prob_grad, axis=3, keepdims=True)

    row_inner = over_blocks(
        inner_step, jnp.zeros((kv_count, group_size, rows, 1), jnp.float32), top_rank
    )

    def grad_step(state, start):
        scores, key_block, value_block = block_scores(query_heads, query_ranks, start)
        probabilities = jnp.exp(scores - group_top) / group_sum
        prob_grad = jnp.einsum(
            "rkgd,ckd->kgrc", grad_heads, value_block, preferred_element_type=jnp.float32
        )
        score_low = (probabilities * (prob_grad - row_inner)).astype(jnp.bfloat16)
        query_total = state[0] + jnp.einsum(
            "kgrc,ckd->rkgd", score_low, key_block, preferred_element_type=jnp.float32
        )
        probs_low = probabilities.astype(jnp.bfloat16)
        key_block_grad = (
            jnp.einsum("kgrc,rkgd->ckd", score_low, query_heads, preferred_element_type=jnp.float32)
            * logit_scale
        )
        value_block_grad = jnp.einsum(
            "kgrc,rkgd->ckd", probs_low, grad_heads, preferred_element_type=jnp.float32
        )
        block_grad = jnp.concatenate(
            [
                key_block_grad.reshape(block_rows, kv_width),
                value_block_grad.reshape(block_rows, kv_width),
            ],
            axis=1,
        )
        previous = lax.dynamic_slice_in_dim(state[1], start, block_rows, 0)
        return (
            query_total,
            lax.dynamic_update_slice_in_dim(state[1], previous + block_grad, start, 0),
        )

    start_state = (jnp.zeros((rows, kv_count, group_size, HEAD_DIM), jnp.float32),)
    start_state = start_state + (kv_buffer,)
    final_state = over_blocks(grad_step, start_state, top_rank)
    query_piece = final_state[0]
    inner_piece = row_inner
    kv_buffer = final_state[-1]
    query_part = query_piece * logit_scale
    row_inner = inner_piece
    query_grad = query_part.reshape(picked, head_count * HEAD_DIM).astype(jnp.bfloat16)
    kv_grad = lax.psum_scatter(kv_buffer, "ctx", scatter_dimension=0, tiled=True)
    key_grad = kv_grad[:, :kv_width].astype(jnp.bfloat16)
    value_grad = kv_grad[:, kv_width:].astype(jnp.bfloat16)
    query_home = jnp.concatenate([query_grad[:half_rows], query_grad[half_rows:]], axis=0)
    hidden_part = times_transposed(query_home, w_query)
    hidden_part = hidden_part + times_transposed(key_grad, w_key)
    hidden_part = hidden_part + times_transposed(value_grad, w_value)
    router_wide = router.astype(jnp.float32)
    hidden_full = lax.psum(hidden_part.astype(jnp.bfloat16), "tp").astype(jnp.float32)
    row_stat = jnp.mean(hidden_full * wide_in, axis=1)
    delta_full = (
        inverse[:, None] * hidden_full - wide_in * (inverse**3)[:, None] * row_stat[:, None]
    )
    delta_full = delta_full + logit_grad[:, None] * router_wide[None, :]
    rows_delta = lax.dynamic_slice_in_dim(delta_full, tp_index * part_width, part_width, 1)
    grad_rows = (rows_grad.astype(jnp.float32) + rows_delta).astype(jnp.bfloat16)
    input_grad = cotangent.at[local_rows].set(grad_rows)
    return (mixed, input_grad)


def solution(mesh):
    placed = (
        P("ctx", "tp"),
        P("ctx"),
        P(),
        P(None, "tp"),
        P(None, "tp"),
        P(None, "tp"),
        P("tp", None),
        P("ctx", "tp"),
    )
    return jax.shard_map(
        on_device,
        mesh=mesh,
        in_specs=placed,
        out_specs=(P("ctx", "tp"), P("ctx", "tp")),
        check_vma=False,
    )
```

profile of v0, /device:TPU:2, one launch (start us, length us, event | category | flops | bytes accessed | tf_op | source)
XLA Modules:
  0.0 429.8 jit_solution(1125308111125658600)
XLA Ops:
  7.2 3.2 copy.99
  10.5 1.3 copy.100
  12.3 2.7 gather_fusion
  15.0 13.5 %all-gather = bf16[64,4096]{1,0:T(8,128)(2,1)S(1)} all-gather(bf16[64,1024]{1,0:T(8,128)(2,1)S(1)} %gather_fusion), channel_id=2, replica_groups=mesh['ctx'=64,'tp'=4] {'tp'}, dimensions={1}, use_global_device_ids=true | all-gather | bytes 655360 | tf_op jit(solution)/shard_map/all_gather | solution.py:32
  30.6 3.1 convolution_convert_fusion.2
  34.5 2.7 gather_fusion.1
  37.1 12.8 %all-gather.1 = bf16[64,4096]{1,0:T(8,128)(2,1)S(1)} all-gather(bf16[64,1024]{1,0:T(8,128)(2,1)S(1)} %gather_fusion.1), channel_id=3, replica_groups=mesh['ctx'=64,'tp'=4] {'tp'}, dimensions={1}, use_global_device_ids=true | all-gather | bytes 655360 | tf_op jit(solution)/shard_map/all_gather | solution.py:33
  50.2 3.6 convolution_convert_fusion.1
  53.9 56.8 %all-gather.4.cloned.1.call-done = bf16[4096,256]{1,0:T(8,128)(2,1)} async-done(((bf16[64,256]{1,0:T(8,128)(2,1)}), bf16[4096,256]{1,0:T(8,128)(2,1)}) %all-gather.4.cloned.1.call-update) | async-done | bytes 2097168 | tf_op jit(solution)/shard_map/all_gather | solution.py:47
  110.7 2.7 slice_bitcast_fusion
  113.4 7.1 %while.66 = (s32[]{:T(128)}, f32[1,4,64,1]{2,1,3,0:T(4,128)S(1)}, f32[1,4,64,1]{2,1,3,0:T(4,128)S(1)}, s32[]{:T(128)}, bf16[4096,1,128]{2,0,1:T(8,128)(2,1)}, /*...) while((s32[]{:T(128)}, f32[1,4,64,1]{2,1,3,0:T(4,128)S(1)}, ...), condition=%wide.region_7.8_spmd.clone, body=%wide.region_2.7_spmd.clone.sunk | while | flops 34243656 | bytes 1329413 | solution.py:89
  114.0 1.6 conditional.12
  120.5 7.1 %while.68 = (s32[]{:T(128)}, f32[1,4,64,1]{2,3,1,0:T(1,128)S(1)}, s32[]{:T(128)}, bf16[4096,1,128]{2,0,1:T(8,128)(2,1)}, bf16[64,1,4,128]{3,0,2,1:T(8,128)(2,1)S...) while((s32[]{:T(128)}, f32[1,4,64,1]{2,3,1,0:T(1,128)S(1)}, ...), condition=%wide.region_18.19_spmd.clone, body=%wide.region_14.18_spmd.clone.sunk | while | flops 67928640 | bytes 1518873 | solution.py:89
  121.1 1.7 conditional.14
  127.6 2.5 broadcast_in_dim.79
  130.1 16.0 %while.69 = (s32[]{:T(128)}, f32[64,1,4,128]{3,0,2,1:T(8,128)S(1)}, f32[4096,256]{0,1:T(8,128)}, s32[]{:T(128)}, bf16[4096,1,128]{2,0,1:T(8,128)(2,1)}, /*index=...) while((s32[]{:T(128)}, f32[64,1,4,128]{3,0,2,1:T(8,128)S(1)}, ...), condition=%wide.region_22.23_spmd.clone, body=%wide.region_19.22_spmd.clone.sunk | while | flops 169214528 | bytes 5449057 | solution.py:89
  131.3 5.8 %conditional.15 = ((f32[64,1,4,128]{3,0,2,1:T(8,128)S(1)}, f32[4096,256]{0,1:T(8,128)})) conditional(s32[]{:T(128)} %convert_element_type.183, (f32[64,1,4,128]{3,0,2,1:T(8,128)S(1)}, f32[4096,256]{0,1:T(8,128)}) %tuple.179, (s32[]{:T(128)}, bf16[4096,1,128]{2,0,1:T(8,128)(2,1)}, s32[]{:T(128)}, bf16[64,1,4,128]{3,0,2,1:T(8,128)(2,1)S(1)}, ...), branch_computations={%region_20.20_spmd, %region_21.21_spmd} | conditional | flops 169214528 | bytes 5448530 | solution.py:82
  134.1 2.0 fusion.65
  146.1 5.6 %copy.38 = f32[4096,256]{1,0:T(8,128)} copy(f32[4096,256]{0,1:T(8,128)} %get-tuple-element.793) | data formatting | bytes 8388608
  152.5 6.9 %while.67 = (s32[]{:T(128)}, f32[64,1,4,128]{3,0,2,1:T(8,128)S(1)}, s32[]{:T(128)}, bf16[4096,1,128]{2,0,1:T(8,128)(2,1)S(1)}, bf16[4096,1,128]{2,0,1:T(8,128)(2...) while((s32[]{:T(128)}, f32[64,1,4,128]{3,0,2,1:T(8,128)S(1)}, ...), condition=%wide.region_11.12_spmd.clone, body=%wide.region_8.11_spmd.clone.sunk | while | flops 67830336 | bytes 665857 | solution.py:89
  153.2 1.5 conditional.13
  153.3 1.3 fusion.21
  159.5 4.0 convolution_convert_fusion
  163.5 1.4 fusion.104
  164.9 190.6 %reduce-scatter.4.cloned.1.call-done = f32[64,256]{1,0:T(8,128)} async-done(((f32[4096,256]{1,0:T(8,128)}), f32[64,256]{1,0:T(8,128)}) %reduce-scatter.4.cloned.1.call-update) | async-done | bytes 65552
  356.9 2.5 fusion.81
  359.6 48.4 %all-reduce.3.cloned.1.call-done = (bf16[64,4096]{1,0:T(8,128)(2,1)}, bf16[64,4096]{1,0:T(8,128)(2,1)}) async-done(((bf16[64,4096]{1,0:T(8,128)(2,1)}, bf16[64,4096]{1,0:T(8,128)(2,1)}), (bf16[64,4096]{1,0:T(8,128)(2,1)}, bf16[64,4096]{1,0:T(8,128)(2,1)})) %all-reduce.3.cloned.1.call-update) | async-done | bytes 1048592 | tf_op jit(solution)/shard_map/psum | solution.py:127
  408.1 2.1 convert_element_type.121
  410.2 1.6 fusion.87
  411.7 2.1 convert_element_type.112
  413.9 4.6 %scatter_custom_fusion = bf16[1024,1024]{1,0:T(8,128)(2,1)} fusion(bf16[1024,1024]{1,0:T(8,128)(2,1)} %copy.99, s32[64]{0:T(128)} %copy-done.12, f32[64,4096]{1,0:T(8,128)} %convert_element_type.112, s32[]{:T(128)} %constant.129.clone.1, s32[]{:T(128)S(6)} %select_n.43, bf16[64,1024]{1,0:T(8,128)(2,1)S(1)} %gather_fusion, f32[64]{0:T(128)S(1)} %copy-done.10), kind=kCustom, calls=%fused_computation.134 | custom fusion | flops 262144 | bytes 2491140 | tf_op jit(solution)/shard_map/scatter | solution.py:131
  418.5 4.7 %scatter_custom_fusion.1 = bf16[1024,1024]{1,0:T(8,128)(2,1)} fusion(bf16[1024,1024]{1,0:T(8,128)(2,1)} %copy.100, s32[64]{0:T(128)} %copy-done.12, f32[64,4096]{1,0:T(8,128)} %convert_element_type.121, s32[]{:T(128)} %constant.129.clone.1, s32[]{:T(128)S(6)} %select_n.43, f32[64,4096]{1,0:T(8,128)S(1)} %convert_element_type.104, ...), kind=kCustom, calls=%fused_computation.135 | custom fusion | flops 589824 | bytes 2759172 | tf_op jit(solution)/shard_map/scatter | solution.py:211
  (148 shorter events, 18.4 us)
Async XLA Ops:
  7.2 22.1 %copy-start = (bf16[4096,128]{1,0:T(8,128)(2,1)S(1)}, bf16[4096,128]{1,0:T(8,128)(2,1)}, u32[]{:S(2)}) copy-start(bf16[4096,128]{1,0:T(8,128)(2,1)} %param.28) | copy-start | bytes 3145732
  7.2 4.6 %copy-start.13 = (s32[64]{0:T(128)S(1)}, s32[64]{0:T(128)}, u32[]{:S(2)}) copy-start(s32[64]{0:T(128)} %param.25) | copy-start | bytes 772
  7.2 103.5 %all-gather.4.cloned.1.call-start = ((), (), s32[]{:S(2)}) async-start(), calls=%async_computation.1 | async-start | bytes 2129920 | tf_op jit(solution)/shard_map/all_gather | solution.py:47
  7.2 3.2 copy-start.3
  10.5 19.1 %copy-start.2 = (bf16[4096,128]{1,0:T(8,128)(2,1)S(1)}, bf16[4096,128]{1,0:T(8,128)(2,1)}, u32[]{:S(2)}) copy-start(bf16[4096,128]{1,0:T(8,128)(2,1)} %param.29) | copy-start | bytes 3145732
  11.8 0.5 copy-start.12
  28.7 5.8 %copy-start.7 = (bf16[4096]{0:T(1024)(128)(2,1)S(1)}, bf16[4096]{0:T(1024)(128)(2,1)}, u32[]{:S(2)}) copy-start(bf16[4096]{0:T(1024)(128)(2,1)} %param.26) | copy-start | bytes 24580
  30.6 324.9 %reduce-scatter.4.cloned.1.call-start = ((), (), s32[]{:S(2)}) async-start(), calls=%async_computation.2 | async-start | bytes 4259840
  37.1 16.7 %copy-start.4 = (bf16[64,1024]{1,0:T(8,128)(2,1)}, bf16[64,1024]{1,0:T(8,128)(2,1)S(1)}, u32[]{:S(2)}) copy-start(bf16[64,1024]{1,0:T(8,128)(2,1)S(1)} %gather_fusion.1) | copy-start | bytes 393220
  50.2 63.2 %copy-start.9 = (f32[64]{0:T(128)}, f32[64]{0:T(128)S(1)}, u32[]{:S(2)}) copy-start(f32[64]{0:T(128)S(1)} %fusion.85) | copy-start | bytes 772
  151.7 256.3 %all-reduce.3.cloned.1.call-start = ((), (), s32[]{:S(2)}) async-start(), calls=%async_computation.3 | async-start | bytes 2097152 | tf_op jit(solution)/shard_map/psum | solution.py:127
  159.4 4.1 copy-start.1
  159.4 4.1 copy-start.6
  356.4 3.2 copy-start.8
  359.5 54.4 %copy-start.10 = (f32[64]{0:T(128)S(1)}, f32[64]{0:T(128)}, u32[]{:S(2)}) copy-start(f32[64]{0:T(128)} %copy-done.9) | copy-start | bytes 772
  359.6 58.9 %copy-start.5 = (bf16[64,1024]{1,0:T(8,128)(2,1)S(1)}, bf16[64,1024]{1,0:T(8,128)(2,1)}, u32[]{:S(2)}) copy-start(bf16[64,1024]{1,0:T(8,128)(2,1)} %copy-done.4) | copy-start | bytes 393220
  359.6 58.9 %copy-start.11 = (f32[64]{0:T(128)S(1)}, f32[64]{0:T(128)}, u32[]{:S(2)}) copy-start(f32[64]{0:T(128)} %get-tuple-element.1094) | copy-start | bytes 772
Sparse Core Ops, SparseCore 0:
  30.7 79.8 all-gather.3
  151.9 203.5 reduce-scatter.3
  359.6 48.4 all-reduce.2
where the time goes:
time: 433 us; the launch traced here: 430 us
  waiting for transfers between devices  296 us (68%)
  local copies, waits for them, and re-layouts  27.8 us (6%)
  blocking collectives  26.2 us (6%)
  matrix products  23.1 us (5%)
  loops' own time  22 us (5%)
  other arithmetic  20.6 us (5%)
  between operations  14 us (3%)
    unnamed x4, waiting for transfers between devices  191 us
    all_gather x1, waiting for transfers between devices, on_device(): lax.all_gather(jnp.concatenate([keys_own, values_own], axis=1), 'ctx', ax...  56.8 us
    psum x1, waiting for transfers between devices, on_device(): lax.psum(partial_branch.astype(jnp.bfloat16), 'tp').astype(jnp.float32)  48.4 us
    another operation x4, loops' own time, over_blocks(): return lax.fori_loop(0, block_count, turn, carry)  21.4 us
    all_gather x1, blocking collectives, on_device(): lax.all_gather(rows_in, 'tp', axis=1, tiled=True)  13.5 us
    all_gather x1, blocking collectives, on_device(): lax.all_gather(rows_grad, 'tp', axis=1, tiled=True)  12.8 us
    unnamed x36, local copies, waits for them, and re-layouts  11.7 us
  transfers between devices with their start and end apart: 3, of which 3 were waited for; matrix products, arithmetic and copies ran while one was open for 4% of the time, Pallas kernels for 0%

commit v1 on v0

v1 whole, which is shorter than its diff:
```python
import math

import jax
import jax.numpy as jnp
from jax import lax
from jax.experimental import pallas as pl
from jax.experimental.pallas import tpu as pltpu
from jax.sharding import Mesh
from jax.sharding import PartitionSpec as P

HEAD_DIM = 128
EPS = 1e-05
FLOOR = -1e30
LOG2E = 1.0 / math.log(2.0)
BF = jnp.bfloat16
F32 = jnp.float32
VMEM = pltpu.VMEM
NT = (((1,), (1,)), ((), ()))
NN = (((1,), (0,)), ((), ()))


def mm(left, right, dims):
    return lax.dot_general(left, right, dims, preferred_element_type=F32)


def whole():
    return pl.BlockSpec(memory_space=VMEM)


def pick_rows(array, positions):
    picked, (total, width) = positions.shape[0], array.shape
    block = min(256, total)
    steps = total // block

    def kernel(pos_ref, block_ref, out_ref, acc_ref):
        step = pl.program_id(0)
        column = lax.broadcasted_iota(jnp.int32, (picked, block), 1) + step * block
        chosen_here = jnp.where(column == pos_ref[...], 1.0, 0.0).astype(BF)
        part = mm(chosen_here, block_ref[...], NN)

        @pl.when(step == 0)
        def _():
            acc_ref[...] = part

        @pl.when(step > 0)
        def _():
            acc_ref[...] += part

        @pl.when(step == steps - 1)
        def _():
            out_ref[...] = acc_ref[...].astype(BF)

    return pl.pallas_call(
        kernel,
        grid=(steps,),
        in_specs=[
            pl.BlockSpec((picked, 1), lambda i: (0, 0)),
            pl.BlockSpec((block, width), lambda i: (i, 0)),
        ],
        out_specs=pl.BlockSpec((picked, width), lambda i: (0, 0)),
        out_shape=jax.ShapeDtypeStruct((picked, width), BF),
        scratch_shapes=[pltpu.VMEM((picked, width), F32)],
        name="pick_rows",
    )(positions[:, None], array)


def put_rows(array, positions, rows):
    picked, (total, width) = positions.shape[0], array.shape
    block = min(256, total)

    def kernel(pos_ref, rows_ref, block_ref, out_ref):
        row = lax.broadcasted_iota(jnp.int32, (block, picked), 0) + pl.program_id(0) * block
        here = jnp.where(row == pos_ref[...], 1.0, 0.0)
        value = mm(here.astype(BF), rows_ref[...], NN)
        hit = jnp.max(here, axis=1, keepdims=True) > 0.5
        out_ref[...] = jnp.where(hit, value, block_ref[...].astype(F32)).astype(BF)

    return pl.pallas_call(
        kernel,
        grid=(total // block,),
        in_specs=[
            pl.BlockSpec((1, picked), lambda i: (0, 0)),
            pl.BlockSpec((picked, width), lambda i: (0, 0)),
            pl.BlockSpec((block, width), lambda i: (i, 0)),
        ],
        out_specs=pl.BlockSpec((block, width), lambda i: (i, 0)),
        out_shape=jax.ShapeDtypeStruct((total, width), BF),
        name="put_rows",
    )(positions[None, :], rows, array)


class Tiles:
    def __init__(self, picked, planes, columns, cores, heads):
        self.picked, self.planes, self.columns, self.cores, self.heads = (
            picked, planes, columns, cores, heads,
        )
        self.group = cores * picked
        self.lanes = heads * self.group
        self.keys = planes * picked
        self.half = heads * HEAD_DIM

    def fill(self, place, own, other, group_ref):
        core = place[2]
        mine = pl.ds(pl.multiple_of(core * self.picked, self.picked), self.picked)
        theirs = pl.ds(pl.multiple_of((1 - core) * self.picked, self.picked), self.picked)
        for s in range(self.columns):
            group_ref[s, mine, :] = own[s][...]
            group_ref[s, theirs, :] = other[s][...]

    def stacked(self, group_ref, s, first):
        parts = [
            group_ref[s, :, first + h * HEAD_DIM : first + (h + 1) * HEAD_DIM]
            for h in range(self.heads)
        ]
        return jnp.concatenate(parts, axis=0)

    def y_of(self, place, s):
        return lax.rem(place[1] + self.columns - s, self.columns)

    def scores(self, place, keys, queries, s):
        z, y, core = place[0], place[1], place[2]
        plane_rows = self.columns * self.group
        logits = mm(keys, queries, NT) * (LOG2E / math.sqrt(HEAD_DIM))
        key = lax.broadcasted_iota(jnp.int32, (self.keys, 1), 0)
        key_rank = (
            lax.div(key, self.picked) * plane_rows
            + (y * self.cores + core) * self.picked
            + lax.rem(key, self.picked)
        )
        lane = lax.broadcasted_iota(jnp.int32, (1, self.lanes), 1)
        query_rank = z * plane_rows + self.y_of(place, s) * self.group + lax.rem(lane, self.group)
        return jnp.where(key_rank <= query_rank, logits, FLOOR)


def softmax_parts(tiles, place, own, other, key_values):
    n = tiles.columns

    def kernel(place_ref, kv_ref, *refs):
        own_refs, other_refs, out_ref, group_ref = refs[:n], refs[n : 2 * n], refs[2 * n], refs[-1]
        at = (place_ref[0], place_ref[1], place_ref[2])
        tiles.fill(at, own_refs, other_refs, group_ref)
        keys, values = kv_ref[:, :HEAD_DIM], kv_ref[:, HEAD_DIM:]
        for s in range(n):
            queries = tiles.stacked(group_ref, s, 0)
            grads = tiles.stacked(group_ref, s, tiles.half)
            logits = tiles.scores(at, keys, queries, s)
            top = jnp.max(logits, axis=0, keepdims=True)
            weights = jnp.exp2(logits - top)
            prob_grad = mm(values, grads, NT)
            total = jnp.sum(weights, axis=0, keepdims=True)
            inner = jnp.sum(weights * prob_grad, axis=0, keepdims=True)
            some = top > 0.5 * FLOOR
            slot = tiles.y_of(at, s)
            out_ref[slot, 0:1, :] = top
            out_ref[slot, 1:2, :] = jnp.where(some, total, 0.0)
            out_ref[slot, 2:3, :] = jnp.where(some, inner, 0.0)
            out_ref[slot, 3:4, :] = jnp.zeros_like(top)

    return pl.pallas_call(
        kernel,
        in_specs=[pl.BlockSpec(memory_space=pltpu.SMEM)] + [whole()] * (1 + 2 * n),
        out_specs=whole(),
        out_shape=jax.ShapeDtypeStruct((n, 4, tiles.lanes), F32),
        scratch_shapes=[pltpu.VMEM((n, tiles.group, 2 * tiles.half), BF)],
        compiler_params=pltpu.CompilerParams(vmem_limit_bytes=24 * 2**20),
        name="softmax_parts",
    )(place, key_values, *own, *other)


def attention_parts(tiles, place, own, other, key_values, parts):
    n = tiles.columns
    scale = 1.0 / math.sqrt(HEAD_DIM)

    def kernel(place_ref, kv_ref, parts_ref, *refs):
        own_refs, other_refs = refs[:n], refs[n : 2 * n]
        mine_ref, theirs_ref, kv_grad_ref, group_ref, result_ref = refs[2 * n :]
        at = (place_ref[0], place_ref[1], place_ref[2])
        tiles.fill(at, own_refs, other_refs, group_ref)
        keys, values = kv_ref[:, :HEAD_DIM], kv_ref[:, HEAD_DIM:]
        keys_t, values_t = keys.T, values.T
        key_grad = jnp.zeros((tiles.keys, HEAD_DIM), F32)
        value_grad = jnp.zeros((tiles.keys, HEAD_DIM), F32)
        core = at[2]
        mine = pl.ds(pl.multiple_of(core * tiles.picked, tiles.picked), tiles.picked)
        theirs = pl.ds(pl.multiple_of((1 - core) * tiles.picked, tiles.picked), tiles.picked)
        for s in range(n):
            slot = tiles.y_of(at, s)
            tops = [parts_ref[b, slot, 0:1, :] for b in range(n * tiles.cores)]
            top = tops[0]
            for one in tops[1:]:
                top = jnp.maximum(top, one)
            total, inner = jnp.zeros_like(top), jnp.zeros_like(top)
            for b in range(n * tiles.cores):
                weight = jnp.exp2(tops[b] - top)
                total += weight * parts_ref[b, slot, 1:2, :]
                inner += weight * parts_ref[b, slot, 2:3, :]
            shift = top + jnp.log(total) * LOG2E
            row_inner = inner / total
            queries = tiles.stacked(group_ref, s, 0)
            grads = tiles.stacked(group_ref, s, tiles.half)
            probs = jnp.exp2(tiles.scores(at, keys, queries, s) - shift)
            prob_grad = mm(values, grads, NT)
            score_low = (probs * (prob_grad - row_inner)).astype(BF)
            probs_low = probs.astype(BF)
            key_grad += mm(score_low, queries, NN)
            value_grad += mm(probs_low, grads, NN)
            query_t = mm(keys_t, score_low, NN) * scale
            output_t = mm(values_t, probs_low, NN)
            for h in range(tiles.heads):
                lanes = slice(h * tiles.group, (h + 1) * tiles.group)
                columns = slice(h * HEAD_DIM, (h + 1) * HEAD_DIM)
                shifted = slice(tiles.half + h * HEAD_DIM, tiles.half + (h + 1) * HEAD_DIM)
                result_ref[s, :, columns] = query_t[:, lanes].T.astype(BF)
                result_ref[s, :, shifted] = output_t[:, lanes].T.astype(BF)
            mine_ref[s, :, :] = result_ref[s, mine, :]
            theirs_ref[s, :, :] = result_ref[s, theirs, :]
        kv_grad_ref[:, :HEAD_DIM] = (key_grad * scale).astype(BF)
        kv_grad_ref[:, HEAD_DIM:] = value_grad.astype(BF)

    rows = jax.ShapeDtypeStruct((n, tiles.picked, 2 * tiles.half), BF)
    return pl.pallas_call(
        kernel,
        in_specs=[pl.BlockSpec(memory_space=pltpu.SMEM)] + [whole()] * (2 + 2 * n),
        out_specs=[whole()] * 3,
        out_shape=[rows, rows, jax.ShapeDtypeStruct((tiles.keys, 2 * HEAD_DIM), BF)],
        scratch_shapes=[pltpu.VMEM((n, tiles.group, 2 * tiles.half), BF)] * 2,
        compiler_params=pltpu.CompilerParams(vmem_limit_bytes=24 * 2**20),
        name="attention_parts",
    )(place, key_values, parts, *own, *other)


def copies(array, count):
    return jnp.broadcast_to(array[None], (count,) + array.shape)


def exchange(array, axis):
    return lax.all_to_all(array, axis, 0, 0, tiled=True)


def shifted(array, axis, count, step):
    return lax.ppermute(array, axis, [(i, (i + step) % count) for i in range(count)])


def on_device(sizes, tokens, chosen, router, w_query, w_key, w_value, w_out, cotangent):
    planes, columns, cores, parts_tp = sizes
    picked = chosen.shape[0]
    tok_rows, part_width = tokens.shape
    width = part_width * parts_tp
    z, y, core, tp = (lax.axis_index(name) for name in ("z", "y", "core", "tp"))
    local_rows = chosen - ((z * columns + y) * cores + core) * tok_rows
    heads = w_query.shape[1] // HEAD_DIM
    tiles = Tiles(picked, planes, columns, cores, heads)
    half = tiles.half

    rows_in = pick_rows(tokens, local_rows)
    rows_grad = pick_rows(cotangent, local_rows)
    in_parts = exchange(copies(rows_in, parts_tp), "tp")
    full_in = jnp.transpose(in_parts, (1, 0, 2)).reshape(picked, width)
    full_grad = jnp.zeros((picked, width), BF)
    for s in range(parts_tp):
        piece = rows_grad if s == 0 else shifted(rows_grad, "tp", parts_tp, s)
        owner = lax.rem(tp + parts_tp - s, parts_tp)
        full_grad = lax.dynamic_update_slice(full_grad, piece, (0, owner * part_width))

    wide_in = full_in.astype(F32)
    inverse = lax.rsqrt(jnp.mean(wide_in * wide_in, axis=1) + EPS)
    gating = jax.nn.sigmoid(jnp.dot(full_in, router, preferred_element_type=F32))
    normed = (wide_in * inverse[:, None]).astype(BF)
    keys_own = mm(normed, w_key, NN).astype(BF)
    values_own = mm(normed, w_value, NN).astype(BF)
    key_values = exchange(copies(jnp.concatenate([keys_own, values_own], axis=1), planes), "z")
    key_values = key_values.reshape(planes * picked, 2 * HEAD_DIM)
    queries = mm(normed, w_query, NN).astype(BF)
    branch_grad = (gating[:, None] * full_grad.astype(F32)).astype(BF)
    attended_grad = mm(branch_grad, w_out, NT).astype(BF)

    own = [jnp.concatenate([queries, attended_grad], axis=1)]
    own = own + [shifted(own[0], "y", columns, s) for s in range(1, columns)]
    other = [shifted(piece, "core", cores, 1) for piece in own]
    place = jnp.stack([z, y, core]).astype(jnp.int32)
    parts = softmax_parts(tiles, place, own, other, key_values)
    parts = exchange(copies(parts, columns * cores), ("y", "core"))
    mine, theirs, kv_grads = attention_parts(tiles, place, own, other, key_values, parts)

    kv_grads = exchange(kv_grads.reshape(planes, picked, 2 * HEAD_DIM), "z")
    received = shifted(theirs, "core", cores, 1)
    chip = (mine.astype(F32) + received.astype(F32)).astype(BF)
    total = chip[0].astype(F32)
    for s in range(1, columns):
        total = total + shifted(chip[s], "y", columns, columns - s).astype(F32)
    total = total.astype(BF)
    query_grad, attended = total[:, :half], total[:, half:]
    kv_grad = jnp.sum(kv_grads.astype(F32), axis=0).astype(BF)

    branch_part = mm(attended, w_out, NN)
    hidden_part = mm(query_grad, w_query, NT)
    hidden_part = hidden_part + mm(kv_grad[:, :HEAD_DIM], w_key, NT)
    hidden_part = hidden_part + mm(kv_grad[:, HEAD_DIM:], w_value, NT)
    stat_part = jnp.sum(hidden_part * wide_in, axis=1) * (1.0 / width)
    gate_part = jnp.sum(attended.astype(F32) * attended_grad.astype(F32), axis=1)
    scalars = jnp.stack([stat_part, gate_part], axis=1)
    high = scalars.astype(BF)
    low = (scalars - high.astype(F32)).astype(BF)
    extra = jnp.concatenate([high, low, jnp.zeros((picked, 124), BF)], axis=1)

    def by_owner(array):
        pieces = array.astype(BF).reshape(picked, parts_tp, part_width)
        return jnp.transpose(pieces, (1, 0, 2))

    sent = jnp.concatenate(
        [by_owner(hidden_part), by_owner(branch_part), copies(extra, parts_tp)], axis=2
    )
    summed = jnp.sum(exchange(sent, "tp").astype(F32), axis=0)
    hidden = summed[:, :part_width]
    branch = summed[:, part_width : 2 * part_width]
    row_stat = summed[:, 2 * part_width] + summed[:, 2 * part_width + 2]
    gate_sum = summed[:, 2 * part_width + 1] + summed[:, 2 * part_width + 3]

    wide_own = rows_in.astype(F32)
    mixed_rows = (wide_own + gating[:, None] * branch).astype(BF)
    mixed = put_rows(tokens, local_rows, mixed_rows)
    logit_grad = gate_sum * (1.0 - gating)
    router_own = lax.dynamic_slice_in_dim(router, tp * part_width, part_width, 0).astype(F32)
    delta = inverse[:, None] * hidden - wide_own * (inverse**3 * row_stat)[:, None]
    delta = delta + logit_grad[:, None] * router_own[None, :]
    grad_rows = (rows_grad.astype(F32) + delta).astype(BF)
    input_grad = put_rows(cotangent, local_rows, grad_rows)
    return mixed, input_grad


def solution(mesh):
    sizes = (8, 4, 2, 4)
    return build(mesh, sizes)


def build(mesh, sizes):
    fine = Mesh(mesh.devices.reshape(sizes), ("z", "y", "core", "tp"))
    ctx = ("z", "y", "core")

    def step(*arrays):
        return on_device(sizes, *arrays)

    placed = (
        P(ctx, "tp"), P(ctx), P(), P(None, "tp"), P(None, "tp"), P(None, "tp"), P("tp", None), P(ctx, "tp"),
    )
    return jax.shard_map(
        step,
        mesh=fine,
        in_specs=placed,
        out_specs=(P(ctx, "tp"), P(ctx, "tp")),
        check_vma=False,
    )
```

time: 433 us -> 143 us (0.33)
  waiting for transfers between devices: 296 us -> 45.3 us
  starting transfers between devices: 0.12 us -> 38.2 us
  Pallas kernels: 0 us -> 22.6 us
  loops' own time: 22 us -> 0 us
  local copies, waits for them, and re-layouts: 27.8 us -> 8.33 us
  blocking collectives: 26.2 us -> 9.95 us
  matrix products: 23.1 us -> 8.72 us
  between operations: 14 us -> 1.07 us
  other arithmetic: 20.6 us -> 7.81 us
    unnamed x4 -> x0, waiting for transfers between devices: 191 us -> none
    all_gather x1 -> x0, waiting for transfers between devices: 56.8 us -> none  [on_device(): lax.all_gather(jnp.concatenate([keys_own, values_own], axis=1), 'ctx', ax...]
    psum x1 -> x0, waiting for transfers between devices: 48.4 us -> none  [on_device(): lax.psum(partial_branch.astype(jnp.bfloat16), 'tp').astype(jnp.float32)]
    all_to_all x0 -> x4, waiting for transfers between devices: none -> 30.7 us  [exchange(): return lax.all_to_all(array, axis, 0, 0, tiled=True)]
    all_to_all x0 -> x4, starting transfers between devices: none -> 26.4 us  [exchange(): return lax.all_to_all(array, axis, 0, 0, tiled=True)]
    all_gather x2 -> x0, blocking collectives: 26.2 us -> none  [the longest x1 13.5 us: on_device(): lax.all_gather(rows_in, 'tp', axis=1, tiled=True)]
    pallas_call x0 -> x6, Pallas kernels: none -> 22.6 us  [the longest x2 8.58 us: put_rows(): pl.pallas_call(kernel, grid=(total // block,), in_specs=[pl.BlockSpec((1,...]
    another operation x36 -> x0, loops' own time: 22 us -> none  [the longest x4 21.4 us: over_blocks(): return lax.fori_loop(0, block_count, turn, carry)]
  transfers between devices with their start and end apart: 3 -> 18, of which waited for: 3 -> 9; matrix products, arithmetic and copies ran while one was open for 4% -> 6% of each run, Pallas kernels for 0% -> 3%
where the time goes in v1:
time: 143 us; the launch traced here: 142 us
  waiting for transfers between devices  45.3 us (32%)
  starting transfers between devices  38.2 us (27%)
  Pallas kernels  22.6 us (16%)
  blocking collectives  9.95 us (7%)
  matrix products  8.72 us (6%)
  local copies, waits for them, and re-layouts  8.33 us (6%)
  other arithmetic  7.81 us (5%)
    all_to_all x4, waiting for transfers between devices, exchange(): return lax.all_to_all(array, axis, 0, 0, tiled=True)  30.7 us
    all_to_all x4, starting transfers between devices, exchange(): return lax.all_to_all(array, axis, 0, 0, tiled=True)  26.4 us
    ppermute x14, waiting for transfers between devices, shifted(): lax.ppermute(array, axis, [(i, (i + step) % count) for i in range(count)])  14.6 us
    ppermute x14, starting transfers between devices, shifted(): lax.ppermute(array, axis, [(i, (i + step) % count) for i in range(count)])  11.9 us
    all_to_all x1, blocking collectives, exchange(): return lax.all_to_all(array, axis, 0, 0, tiled=True)  9.95 us
    pallas_call x2, Pallas kernels, put_rows(): pl.pallas_call(kernel, grid=(total // block,), in_specs=[pl.BlockSpec((1,...  8.58 us
    dot_general x8, matrix products, mm(): return lax.dot_general(left, right, dims, preferred_element_type=F32)  8.47 us
    pallas_call x2, Pallas kernels, pick_rows(): pl.pallas_call(kernel, grid=(steps,), in_specs=[pl.BlockSpec((picked, 1),...  7.2 us
  transfers between devices with their start and end apart: 18, of which 9 were waited for; matrix products, arithmetic and copies ran while one was open for 6% of the time, Pallas kernels for 3%

profile of v1, /device:TPU:2, one launch (start us, length us, event | category | flops | bytes accessed | tf_op | source)
XLA Modules:
  0.0 142.0 jit_solution(11801635569207327224)
XLA Ops:
  0.7 1.3 subtract_bitcast_fusion
  2.6 3.6 %pick_rows.3 = bf16[64,1024]{1,0:T(8,128)(2,1)} custom-call(s32[64,1]{1,0:T(8,128)} %copy.34.pos_ref, bf16[1024,1024]{1,0:T(8,128)(2,1)} %block_ref.7), custom_call_target="tpu_custom_call" | custom-call | tf_op jit(solution)/shard_map/pick_rows/pallas_call | solution.py:53
  6.3 1.5 %collective-permute-start = (bf16[64,1024]{1,0:T(8,128)(2,1)}, bf16[64,1024]{1,0:T(8,128)(2,1)S(1)}, u32[]{:S(2)}, u32[]{:S(2)}) collective-permute-start(bf16[64,1024]{1,0:T(8,128)(2,1)} %pick_rows.3), channel_id=1, source_target_pairs={{0,1},{1,2},{2,3},{3,0},{4,5},{5,6},{6,7},{7,4},{8,9},{9,10},{10,1... | collective-permute-start | bytes 393224 | tf_op jit(solution)/shard_map/ppermute | solution.py:241
  8.6 2.0 %collective-permute-start.1 = (bf16[64,1024]{1,0:T(8,128)(2,1)}, bf16[64,1024]{1,0:T(8,128)(2,1)}, u32[]{:S(2)}, u32[]{:S(2)}) collective-permute-start(bf16[64,1024]{1,0:T(8,128)(2,1)} %pick_rows.3), channel_id=1, source_target_pairs={{0,2},{1,3},{2,0},{3,1},{4,6},{5,7},{6,4},{7,5},{8,10},{9,11},{10,... | collective-permute-start | bytes 393224 | tf_op jit(solution)/shard_map/ppermute | solution.py:241
  10.6 3.6 %pick_rows.2 = bf16[64,1024]{1,0:T(8,128)(2,1)} custom-call(s32[64,1]{1,0:T(8,128)} %copy.34.pos_ref, bf16[1024,1024]{1,0:T(8,128)(2,1)} %block_ref.6), custom_call_target="tpu_custom_call" | custom-call | tf_op jit(solution)/shard_map/pick_rows/pallas_call | solution.py:53
  14.2 1.8 %broadcast_in_dim.18 = bf16[4,64,1024]{2,1,0:T(8,128)(2,1)} broadcast(bf16[64,1024]{1,0:T(8,128)(2,1)} %pick_rows.2), dimensions={1,2} | broadcast | bytes 655360 | tf_op jit(solution)/shard_map/broadcast_in_dim | solution.py:233
  15.9 6.0 %all-to-all-start = ((bf16[4,64,1024]{2,1,0:T(8,128)(2,1)}), bf16[4,64,1024]{2,1,0:T(8,128)(2,1)S(1)}, u32[]{:S(2)}, u32[]{:S(2)}) async-start(bf16[4,64,1024]{2,1,0:T(8,128)(2,1)} %broadcast_in_dim.18), calls=%async_computation | async-start | bytes 1048576 | tf_op jit(solution)/shard_map/all_to_all | solution.py:237
  23.1 5.4 %all-to-all-done = bf16[4,64,1024]{2,1,0:T(8,128)(2,1)S(1)} async-done(((bf16[4,64,1024]{2,1,0:T(8,128)(2,1)}), bf16[4,64,1024]{2,1,0:T(8,128)(2,1)S(1)}, u32[]{:S(2)}, u32[]{:S(2)}) %all-to-all-start) | async-done | bytes 524320 | tf_op jit(solution)/shard_map/all_to_all | solution.py:237
  30.4 1.3 copy-done.2
  33.4 8.0 %all-to-all-start.1 = ((bf16[8,64,256]{2,1,0:T(8,128)(2,1)}), bf16[8,64,256]{2,1,0:T(8,128)(2,1)S(1)}, u32[]{:S(2)}, u32[]{:S(2)}) async-start(bf16[8,64,256]{2,1,0:T(8,128)(2,1)} %broadcast_in_dim.19), calls=%async_computation.1 | async-start | bytes 524288 | tf_op jit(solution)/shard_map/all_to_all | solution.py:237
  41.4 3.6 %convolution_convert_fusion.1 = bf16[64,512]{1,0:T(8,128)(2,1)S(1)} fusion(bf16[512,4096]{1,0:T(8,128)(2,1)} %param.14, bf16[64,4096]{1,0:T(8,128)(2,1)S(1)} %constant_dynamic-update-slice_fusion, f32[64]{0:T(128)S(1)} %fusion.3), kind=kOutput, calls=%fused_computation.6 | convolution fusion | flops 269254656 | bytes 4784384 | tf_op jit(solution)/shard_map/dot_general | solution.py:23
  45.6 3.1 %collective-permute-start.5 = (bf16[64,1024]{1,0:T(8,128)(2,1)S(1)}, bf16[64,1024]{1,0:T(8,128)(2,1)S(1)}, u32[]{:S(2)}, u32[]{:S(2)}) collective-permute-start(bf16[64,1024]{1,0:T(8,128)(2,1)S(1)} %pad_maximum_fusion.1.refs_0_), channel_id=1, source_target_pairs={{0,24},{8,0},{16,8},{24,16},{1,25},{9,1},{17,9},{25,17},{2,26},{10... | collective-permute-start | bytes 393224 | tf_op jit(solution)/shard_map/ppermute | solution.py:241
  50.3 2.3 %collective-permute-done.5.refs_3_ = bf16[64,1024]{1,0:T(8,128)(2,1)S(1)} collective-permute-done((bf16[64,1024]{1,0:T(8,128)(2,1)S(1)}, bf16[64,1024]{1,0:T(8,128)(2,1)S(1)}, u32[]{:S(2)}, u32[]{:S(2)}) %collective-permute-start.5) | collective-permute-done | bytes 131104 | tf_op jit(solution)/shard_map/ppermute | solution.py:241
  52.6 2.6 %collective-permute-done.4.refs_2_ = bf16[64,1024]{1,0:T(8,128)(2,1)S(1)} collective-permute-done((bf16[64,1024]{1,0:T(8,128)(2,1)S(1)}, bf16[64,1024]{1,0:T(8,128)(2,1)S(1)}, u32[]{:S(2)}, u32[]{:S(2)}) %collective-permute-start.4) | collective-permute-done | bytes 131104 | tf_op jit(solution)/shard_map/ppermute | solution.py:241
  55.3 1.3 collective-permute-done.3.refs_1_
  56.7 1.3 collective-permute-done.7.refs_5_
  57.9 2.4 %softmax_parts.1 = f32[4,4,512]{2,1,0:T(4,128)S(1)} custom-call(s32[3]{0:T(128)S(1)} %pad_add_fusion.place_ref, bf16[512,256]{1,0:T(8,128)(2,1)S(1)} %bitcast.59, bf16[64,1024]{1,0:T(8,128)(2,1)S(1)} %pad_maximum_fusion.1.refs_0_, bf16[64,1024]{1,0:T(8,128)(2,1)S(1)} %collective-permute-done.3.refs_1_, bf16[64,1024]{1,0:T(8,128)(2,1)S(1)} %collective-permute-done.4.refs_2_, ...), custom_call_target="tpu_custom_call" | custom-call | tf_op jit(solution)/shard_map/softmax_parts/pallas_call | solution.py:159
  60.4 9.9 %all_to_all.25.parts_ref = f32[8,4,4,512]{3,2,1,0:T(4,128)S(1)} all-to-all(f32[8,4,4,512]{3,2,1,0:T(4,128)S(1)} %broadcast_in_dim.21), channel_id=1, replica_groups=mesh['z'=8,'y'=4,'core'=2,'tp'=4] {'y','core'}, dimensions={0} | all-to-all | bytes 524288 | tf_op jit(solution)/shard_map/all_to_all | solution.py:237
  70.3 4.5 %attention_parts.1 = (bf16[4,64,1024]{2,1,0:T(8,128)(2,1)S(1)}, bf16[4,64,1024]{2,1,0:T(8,128)(2,1)S(1)}, bf16[512,256]{1,0:T(8,128)(2,1)}) custom-call(s32[3]{0:T(128)S(1)} %pad_add_fusion.place_ref, bf16[512,256]{1,0:T(8,128)(2,1)S(1)} %bitcast.60, f32[8,4,4,512]{3,2,1,0:T(4,128)S(1)} %all_to_all.25.parts_ref, ...), custom_call_target="tpu_custom_call" | custom-call | tf_op jit(solution)/shard_map/attention_parts/pallas_call | solution.py:221
  74.8 7.3 %all-to-all-start.3 = ((bf16[8,64,256]{2,1,0:T(8,128)(2,1)}), bf16[8,64,256]{2,1,0:T(8,128)(2,1)}, u32[]{:S(2)}, u32[]{:S(2)}) async-start(bf16[8,64,256]{2,1,0:T(8,128)(2,1)} %bitcast.12), calls=%async_computation.3 | async-start | bytes 524288 | tf_op jit(solution)/shard_map/all_to_all | solution.py:237
  82.2 12.4 %all-to-all-done.3 = bf16[8,64,256]{2,1,0:T(8,128)(2,1)} async-done(((bf16[8,64,256]{2,1,0:T(8,128)(2,1)}), bf16[8,64,256]{2,1,0:T(8,128)(2,1)}, u32[]{:S(2)}, u32[]{:S(2)}) %all-to-all-start.3) | async-done | bytes 262176 | tf_op jit(solution)/shard_map/all_to_all | solution.py:237
  95.7 1.4 add_convert_fusion
  97.1 1.3 collective-permute-start.11
  100.4 2.2 %collective-permute-done.11 = bf16[64,1024]{1,0:T(8,128)(2,1)S(1)} collective-permute-done((bf16[64,1024]{1,0:T(8,128)(2,1)S(1)}, bf16[64,1024]{1,0:T(8,128)(2,1)S(1)}, u32[]{:S(2)}, u32[]{:S(2)}) %collective-permute-start.11) | collective-permute-done | bytes 131104 | tf_op jit(solution)/shard_map/ppermute | solution.py:241
  102.6 4.9 %collective-permute-done.13 = bf16[64,1024]{1,0:T(8,128)(2,1)S(1)} collective-permute-done((bf16[64,1024]{1,0:T(8,128)(2,1)S(1)}, bf16[64,1024]{1,0:T(8,128)(2,1)S(1)}, u32[]{:S(2)}, u32[]{:S(2)}) %collective-permute-start.13) | collective-permute-done | bytes 131104 | tf_op jit(solution)/shard_map/ppermute | solution.py:241
  108.5 1.3 copy-done.3
  109.8 1.4 convolution_add_fusion.1
  112.3 1.1 pad_maximum_fusion
  113.4 5.1 %all-to-all-start.4 = ((bf16[4,64,2176]{2,1,0:T(8,128)(2,1)}), bf16[4,64,2176]{2,1,0:T(8,128)(2,1)S(1)}, u32[]{:S(2)}, u32[]{:S(2)}) async-start(bf16[4,64,2176]{2,1,0:T(8,128)(2,1)} %pad_maximum_fusion), calls=%async_computation.4 | async-start | bytes 2228224 | tf_op jit(solution)/shard_map/all_to_all | solution.py:237
  119.4 12.9 %all-to-all-done.4 = bf16[4,64,2176]{2,1,0:T(8,128)(2,1)S(1)} async-done(((bf16[4,64,2176]{2,1,0:T(8,128)(2,1)}), bf16[4,64,2176]{2,1,0:T(8,128)(2,1)S(1)}, u32[]{:S(2)}, u32[]{:S(2)}) %all-to-all-start.4) | async-done | bytes 1114144 | tf_op jit(solution)/shard_map/all_to_all | solution.py:237
  133.4 4.3 %put_rows.3 = bf16[1024,1024]{1,0:T(8,128)(2,1)} custom-call(s32[1,64]{1,0:T(1,128)} %get-tuple-element.20.pos_ref, bf16[64,1024]{1,0:T(8,128)(2,1)} %get-tuple-element.14.rows_ref, bf16[1024,1024]{1,0:T(8,128)(2,1)} %block_ref.7), custom_call_target="tpu_custom_call" | custom-call | tf_op jit(solution)/shard_map/put_rows/pallas_call | solution.py:78
  137.7 4.3 %put_rows.2 = bf16[1024,1024]{1,0:T(8,128)(2,1)} custom-call(s32[1,64]{1,0:T(1,128)} %get-tuple-element.20.pos_ref, bf16[64,1024]{1,0:T(8,128)(2,1)} %get-tuple-element.15.rows_ref, bf16[1024,1024]{1,0:T(8,128)(2,1)} %block_ref.6), custom_call_target="tpu_custom_call" | custom-call | tf_op jit(solution)/shard_map/put_rows/pallas_call | solution.py:78
  (96 shorter events, 15.8 us)
Async XLA Ops:
  0.6 29.0 %copy-start = (bf16[4096,128]{1,0:T(8,128)(2,1)S(1)}, bf16[4096,128]{1,0:T(8,128)(2,1)}, u32[]{:S(2)}) copy-start(bf16[4096,128]{1,0:T(8,128)(2,1)} %param.13) | copy-start | bytes 3145732
  6.3 15.7 %copy-start.9 = (bf16[64,1024]{1,0:T(8,128)(2,1)S(1)}, bf16[64,1024]{1,0:T(8,128)(2,1)}, u32[]{:S(2)}) copy-start(bf16[64,1024]{1,0:T(8,128)(2,1)} %pick_rows.3) | copy-start | bytes 393220
  6.3 15.7 %copy-start.14 = (bf16[4096]{0:T(1024)(128)(2,1)S(1)}, bf16[4096]{0:T(1024)(128)(2,1)}, u32[]{:S(2)}) copy-start(bf16[4096]{0:T(1024)(128)(2,1)} %param.10) | copy-start | bytes 24580
  6.3 15.8 %collective-permute-start = (bf16[64,1024]{1,0:T(8,128)(2,1)}, bf16[64,1024]{1,0:T(8,128)(2,1)S(1)}, u32[]{:S(2)}, u32[]{:S(2)}) collective-permute-start(bf16[64,1024]{1,0:T(8,128)(2,1)} %pick_rows.3), channel_id=1, source_target_pairs={{0,1},{1,2},{2,3},{3,0},{4,5},{5,6},{6,7},{7,4},{8,9},{9,10},{10,1... | collective-permute-start | bytes 393224 | tf_op jit(solution)/shard_map/ppermute | solution.py:241
  7.7 15.4 %collective-permute-start.2 = (bf16[64,1024]{1,0:T(8,128)(2,1)}, bf16[64,1024]{1,0:T(8,128)(2,1)S(1)}, u32[]{:S(2)}, u32[]{:S(2)}) collective-permute-start(bf16[64,1024]{1,0:T(8,128)(2,1)} %pick_rows.3), channel_id=1, source_target_pairs={{0,3},{1,0},{2,1},{3,2},{4,7},{5,4},{6,5},{7,6},{8,11},{9,8},{10,9... | collective-permute-start | bytes 393224 | tf_op jit(solution)/shard_map/ppermute | solution.py:241
  8.6 13.5 %collective-permute-start.1 = (bf16[64,1024]{1,0:T(8,128)(2,1)}, bf16[64,1024]{1,0:T(8,128)(2,1)}, u32[]{:S(2)}, u32[]{:S(2)}) collective-permute-start(bf16[64,1024]{1,0:T(8,128)(2,1)} %pick_rows.3), channel_id=1, source_target_pairs={{0,2},{1,3},{2,0},{3,1},{4,6},{5,7},{6,4},{7,5},{8,10},{9,11},{10,... | collective-permute-start | bytes 393224 | tf_op jit(solution)/shard_map/ppermute | solution.py:241
  15.9 12.6 %all-to-all-start = ((bf16[4,64,1024]{2,1,0:T(8,128)(2,1)}), bf16[4,64,1024]{2,1,0:T(8,128)(2,1)S(1)}, u32[]{:S(2)}, u32[]{:S(2)}) async-start(bf16[4,64,1024]{2,1,0:T(8,128)(2,1)} %broadcast_in_dim.18), calls=%async_computation | async-start | bytes 1048576 | tf_op jit(solution)/shard_map/all_to_all | solution.py:237
  22.0 8.0 %copy-start.6 = (bf16[4096,128]{1,0:T(8,128)(2,1)S(1)}, bf16[4096,128]{1,0:T(8,128)(2,1)}, u32[]{:S(2)}) copy-start(bf16[4096,128]{1,0:T(8,128)(2,1)} %param.12) | copy-start | bytes 3145732
  29.3 2.4 %copy-start.2 = (bf16[4096,512]{1,0:T(8,128)(2,1)S(1)}, bf16[4096,512]{1,0:T(8,128)(2,1)}, u32[]{:S(2)}) copy-start(bf16[4096,512]{1,0:T(8,128)(2,1)} %param.11) | copy-start | bytes 12582916
  29.4 3.2 %copy-start.4 = (bf16[4,8,8,1024]{3,2,0,1:T(8,128)(2,1)}, bf16[4,8,8,1024]{3,2,0,1:T(8,128)(2,1)S(1)}, u32[]{:S(2)}) copy-start(bf16[4,8,8,1024]{3,2,0,1:T(8,128)(2,1)S(1)} %copy.45) | copy-start | bytes 1572868
  29.6 11.8 %copy-start.15 = (f32[64]{0:T(128)}, f32[64]{0:T(128)S(1)}, u32[]{:S(2)}) copy-start(f32[64]{0:T(128)S(1)} %fusion.3) | copy-start | bytes 772
  33.4 24.6 %all-to-all-start.1 = ((bf16[8,64,256]{2,1,0:T(8,128)(2,1)}), bf16[8,64,256]{2,1,0:T(8,128)(2,1)S(1)}, u32[]{:S(2)}, u32[]{:S(2)}) async-start(bf16[8,64,256]{2,1,0:T(8,128)(2,1)} %broadcast_in_dim.19), calls=%async_computation.1 | async-start | bytes 524288 | tf_op jit(solution)/shard_map/all_to_all | solution.py:237
  45.6 7.0 %collective-permute-start.5 = (bf16[64,1024]{1,0:T(8,128)(2,1)S(1)}, bf16[64,1024]{1,0:T(8,128)(2,1)S(1)}, u32[]{:S(2)}, u32[]{:S(2)}) collective-permute-start(bf16[64,1024]{1,0:T(8,128)(2,1)S(1)} %pad_maximum_fusion.1.refs_0_), channel_id=1, source_target_pairs={{0,24},{8,0},{16,8},{24,16},{1,25},{9,1},{17,9},{25,17},{2,26},{10... | collective-permute-start | bytes 393224 | tf_op jit(solution)/shard_map/ppermute | solution.py:241
  48.7 6.6 %collective-permute-start.4 = (bf16[64,1024]{1,0:T(8,128)(2,1)S(1)}, bf16[64,1024]{1,0:T(8,128)(2,1)S(1)}, u32[]{:S(2)}, u32[]{:S(2)}) collective-permute-start(bf16[64,1024]{1,0:T(8,128)(2,1)S(1)} %pad_maximum_fusion.1.refs_0_), channel_id=1, source_target_pairs={{0,16},{8,24},{16,0},{24,8},{1,17},{9,25},{17,1},{25,9},{2,18},{10... | collective-permute-start | bytes 393224 | tf_op jit(solution)/shard_map/ppermute | solution.py:241
  49.3 7.2 %collective-permute-start.3 = (bf16[64,1024]{1,0:T(8,128)(2,1)S(1)}, bf16[64,1024]{1,0:T(8,128)(2,1)S(1)}, u32[]{:S(2)}, u32[]{:S(2)}) collective-permute-start(bf16[64,1024]{1,0:T(8,128)(2,1)S(1)} %pad_maximum_fusion.1.refs_0_), channel_id=1, source_target_pairs={{0,8},{8,16},{16,24},{24,0},{1,9},{9,17},{17,25},{25,1},{2,10},{10... | collective-permute-start | bytes 393224 | tf_op jit(solution)/shard_map/ppermute | solution.py:241
  50.3 6.4 %collective-permute-start.6 = (bf16[64,1024]{1,0:T(8,128)(2,1)S(1)}, bf16[64,1024]{1,0:T(8,128)(2,1)S(1)}, u32[]{:S(2)}, u32[]{:S(2)}) collective-permute-start(bf16[64,1024]{1,0:T(8,128)(2,1)S(1)} %pad_maximum_fusion.1.refs_0_), channel_id=1, source_target_pairs={{0,4},{4,0},{1,5},{5,1},{2,6},{6,2},{3,7},{7,3},{8,12},{12,8},{9,1... | collective-permute-start | bytes 393224 | tf_op jit(solution)/shard_map/ppermute | solution.py:241
  52.6 4.0 %collective-permute-start.9 = (bf16[64,1024]{1,0:T(8,128)(2,1)S(1)}, bf16[64,1024]{1,0:T(8,128)(2,1)S(1)}, u32[]{:S(2)}, u32[]{:S(2)}) collective-permute-start(bf16[64,1024]{1,0:T(8,128)(2,1)S(1)} %collective-permute-done.5.refs_3_), channel_id=1, source_target_pairs={{0,4},{4,0},{1,5},{5,1},{2,6},{6,2},{3,7},{7,3},{8,12},{12,8},{9,1... | collective-permute-start | bytes 393224 | tf_op jit(solution)/shard_map/ppermute | solution.py:241
  55.3 1.4 collective-permute-start.8
  56.6 1.3 collective-permute-start.7
  74.8 25.1 %copy-start.7 = (bf16[4096,128]{1,0:T(8,128)(2,1)S(1)}, bf16[4096,128]{1,0:T(8,128)(2,1)}, u32[]{:S(2)}) copy-start(bf16[4096,128]{1,0:T(8,128)(2,1)} %param.12) | copy-start | bytes 3145732
  74.8 20.9 %collective-permute-start.10 = (bf16[4,64,1024]{2,1,0:T(8,128)(2,1)S(1)}, bf16[4,64,1024]{2,1,0:T(8,128)(2,1)}, u32[]{:S(2)}, u32[]{:S(2)}) collective-permute-start(bf16[4,64,1024]{2,1,0:T(8,128)(2,1)S(1)} %get-tuple-element.6), channel_id=1, source_target_pairs={{0,4},{4,0},{1,5},{5,1},{2,6},{6,2},{3,7},{7,3},{8,12},{12,8},{9,1... | collective-permute-start | bytes 1572872 | tf_op jit(solution)/shard_map/ppermute | solution.py:241
  74.8 19.9 %all-to-all-start.3 = ((bf16[8,64,256]{2,1,0:T(8,128)(2,1)}), bf16[8,64,256]{2,1,0:T(8,128)(2,1)}, u32[]{:S(2)}, u32[]{:S(2)}) async-start(bf16[8,64,256]{2,1,0:T(8,128)(2,1)} %bitcast.12), calls=%async_computation.3 | async-start | bytes 524288 | tf_op jit(solution)/shard_map/all_to_all | solution.py:237
  95.6 11.9 %copy-start.11 = (bf16[64,512]{1,0:T(8,128)(2,1)S(1)}, bf16[64,512]{1,0:T(8,128)(2,1)}, u32[]{:S(2)}) copy-start(bf16[64,512]{1,0:T(8,128)(2,1)} %copy-done.10) | copy-start | bytes 196612
  95.6 12.0 %copy-start.1 = (bf16[512,4096]{1,0:T(8,128)(2,1)S(1)}, bf16[512,4096]{1,0:T(8,128)(2,1)}, u32[]{:S(2)}) copy-start(bf16[512,4096]{1,0:T(8,128)(2,1)} %param.14) | copy-start | bytes 12582916
  97.1 5.5 %collective-permute-start.11 = (bf16[64,1024]{1,0:T(8,128)(2,1)S(1)}, bf16[64,1024]{1,0:T(8,128)(2,1)S(1)}, u32[]{:S(2)}, u32[]{:S(2)}) collective-permute-start(bf16[64,1024]{1,0:T(8,128)(2,1)S(1)} %get-tuple-element.16), channel_id=1, source_target_pairs={{0,24},{8,0},{16,8},{24,16},{1,25},{9,1},{17,9},{25,17},{2,26},{10... | collective-permute-start | bytes 393224 | tf_op jit(solution)/shard_map/ppermute | solution.py:241
  98.3 9.1 %collective-permute-start.13 = (bf16[64,1024]{1,0:T(8,128)(2,1)S(1)}, bf16[64,1024]{1,0:T(8,128)(2,1)S(1)}, u32[]{:S(2)}, u32[]{:S(2)}) collective-permute-start(bf16[64,1024]{1,0:T(8,128)(2,1)S(1)} %get-tuple-element.17), channel_id=1, source_target_pairs={{0,8},{8,16},{16,24},{24,0},{1,9},{9,17},{17,25},{25,1},{2,10},{10... | collective-permute-start | bytes 393224 | tf_op jit(solution)/shard_map/ppermute | solution.py:241
  99.2 8.3 %collective-permute-start.12 = (bf16[64,1024]{1,0:T(8,128)(2,1)S(1)}, bf16[64,1024]{1,0:T(8,128)(2,1)S(1)}, u32[]{:S(2)}, u32[]{:S(2)}) collective-permute-start(bf16[64,1024]{1,0:T(8,128)(2,1)S(1)} %get-tuple-element.18), channel_id=1, source_target_pairs={{0,16},{8,24},{16,0},{24,8},{1,17},{9,25},{17,1},{25,9},{2,18},{10... | collective-permute-start | bytes 393224 | tf_op jit(solution)/shard_map/ppermute | solution.py:241
  112.3 6.9 %copy-start.17 = (f32[64,1]{0,1:T(1,128)S(1)}, f32[64,1]{0,1:T(1,128)}, u32[]{:S(2)}) copy-start(f32[64,1]{0,1:T(1,128)} %get-tuple-element.10) | copy-start | bytes 772
  112.3 7.0 %copy-start.13 = (f32[64]{0:T(128)S(1)}, f32[64]{0:T(128)}, u32[]{:S(2)}) copy-start(f32[64]{0:T(128)} %copy-done.12) | copy-start | bytes 772
  113.4 19.2 %copy-start.16 = (f32[64]{0:T(128)S(1)}, f32[64]{0:T(128)}, u32[]{:S(2)}) copy-start(f32[64]{0:T(128)} %copy-done.15) | copy-start | bytes 772
  113.4 19.2 %copy-start.8 = (bf16[64,1024]{1,0:T(8,128)(2,1)S(1)}, bf16[64,1024]{1,0:T(8,128)(2,1)}, u32[]{:S(2)}) copy-start(bf16[64,1024]{1,0:T(8,128)(2,1)} %pick_rows.2) | copy-start | bytes 393220
  113.4 18.8 %all-to-all-start.4 = ((bf16[4,64,2176]{2,1,0:T(8,128)(2,1)}), bf16[4,64,2176]{2,1,0:T(8,128)(2,1)S(1)}, u32[]{:S(2)}, u32[]{:S(2)}) async-start(bf16[4,64,2176]{2,1,0:T(8,128)(2,1)} %pad_maximum_fusion), calls=%async_computation.4 | async-start | bytes 2228224 | tf_op jit(solution)/shard_map/all_to_all | solution.py:237
  (4 other events, 5.3 us)

commit v2 on v1

v2 whole, which is shorter than its diff:
```python
import math

import jax
import jax.numpy as jnp
from jax import lax
from jax.experimental import pallas as pl
from jax.experimental.pallas import tpu as pltpu
from jax.sharding import Mesh
from jax.sharding import PartitionSpec as P

HEAD_DIM = 128
EPS = 1e-05
FLOOR = -1e30
LOG2E = 1.0 / math.log(2.0)
BF = jnp.bfloat16
F32 = jnp.float32
VMEM = pltpu.VMEM
NT = (((1,), (1,)), ((), ()))
NN = (((1,), (0,)), ((), ()))


def mm(left, right, dims):
    return lax.dot_general(left, right, dims, preferred_element_type=F32)


def whole():
    return pl.BlockSpec(memory_space=VMEM)


def far():
    return pl.BlockSpec(memory_space=pl.ANY)


def like(shape, dtype=BF):
    return jax.ShapeDtypeStruct(tuple(shape), dtype)


def params(mib):
    return pltpu.CompilerParams(vmem_limit_bytes=mib * 2**20)


def my_place():
    return lax.axis_index("z"), lax.axis_index("y"), lax.axis_index("core")


def my_first_row(sizes, tok_rows):
    z, y, core = my_place()
    return ((z * sizes[1] + y) * sizes[2] + core) * tok_rows


def pick_rows(sizes, array, chosen):
    picked = chosen.shape[1]
    total, width = array.shape
    rows = min(256, total)

    def kernel(chosen_ref, array_ref, out_ref):
        square = (picked, picked)
        eye = lax.broadcasted_iota(jnp.int32, square, 0) == lax.broadcasted_iota(jnp.int32, square, 1)
        local = (chosen_ref[...] - my_first_row(sizes, total)).astype(F32)
        spot = jnp.sum(jnp.where(eye, jnp.broadcast_to(local, square), 0.0), axis=1, keepdims=True)
        column = lax.broadcasted_iota(jnp.int32, (picked, total), 1)
        here = jnp.where(column == spot.astype(jnp.int32), 1.0, 0.0).astype(BF)
        out_ref[...] = mm(here, array_ref[...], NN).astype(BF)

    return pl.pallas_call(
        kernel,
        in_specs=[whole()] * 2,
        out_specs=whole(),
        out_shape=like((picked, width)),
        compiler_params=params(8),
        name="pick_rows",
    )(chosen, array)


def project(sizes, in_pieces, grad_pieces, router, w_query, w_key, w_value, w_out, after):
    parts = len(in_pieces)
    picked, part = in_pieces[0].shape
    width = part * parts
    half = w_query.shape[1]

    def kernel(*refs):
        in_refs, grad_refs = refs[:parts], refs[parts : 2 * parts]
        router_ref, query_ref, key_ref, value_ref, out_w_ref = refs[2 * parts : 2 * parts + 5]
        kv_ref, own_ref, scales_ref = refs[2 * parts + 6 :]
        tp = lax.axis_index("tp")

        def span(s):
            owner = lax.rem(tp + parts - s, parts)
            return pl.ds(pl.multiple_of(owner * part, part), part)

        squares = jnp.zeros((picked, 1), F32)
        logit = jnp.zeros((picked, 1), F32)
        for s in range(parts):
            rows = in_refs[s][...].astype(F32)
            squares += jnp.sum(rows * rows, axis=1, keepdims=True)
            weights = router_ref[:, span(s)].astype(F32)
            logit += jnp.sum(rows * weights, axis=1, keepdims=True)
        inverse = lax.rsqrt(squares * (1.0 / width) + EPS)
        gate = 1.0 / (1.0 + jnp.exp(-logit))
        lane = lax.broadcasted_iota(jnp.int32, (picked, 128), 1)
        scales_ref[...] = jnp.where(lane == 0, gate, inverse)
        keys = jnp.zeros((picked, HEAD_DIM), F32)
        values = jnp.zeros((picked, HEAD_DIM), F32)
        queries = jnp.zeros((picked, half), F32)
        grads = jnp.zeros((picked, half), F32)
        for s in range(parts):
            rows = span(s)
            normed = (in_refs[s][...].astype(F32) * inverse).astype(BF)
            keys += mm(normed, key_ref[rows, :], NN)
            values += mm(normed, value_ref[rows, :], NN)
            queries += mm(normed, query_ref[rows, :], NN)
            grads += mm(grad_refs[s][...], out_w_ref[:, rows], NT)
        own_ref[:, :half] = queries.astype(BF)
        own_ref[:, half:] = (gate * grads).astype(BF)
        low = jnp.concatenate([keys, values], axis=1).astype(BF)
        for b in range(sizes[0]):
            kv_ref[b] = low

    ins = (*in_pieces, *grad_pieces, router, w_query, w_key, w_value, w_out)
    outs = [
        like((sizes[0], picked, 2 * HEAD_DIM)),
        like((picked, 2 * half)),
        like((picked, 128), F32),
    ]
    return pl.pallas_call(
        kernel,
        in_specs=[whole()] * len(ins) + [far()],
        out_specs=[whole()] * len(outs),
        out_shape=outs,
        compiler_params=params(16),
        name="project",
    )(*ins, after)


def add_pieces(mine, received):
    count = mine.shape[0]

    def kernel(mine_ref, received_ref, *out_refs):
        for s in range(count):
            out_refs[s][...] = (mine_ref[s].astype(F32) + received_ref[s].astype(F32)).astype(BF)

    outs = [like(mine.shape[1:])] * count
    return pl.pallas_call(
        kernel,
        in_specs=[whole()] * 2,
        out_specs=[whole()] * len(outs),
        out_shape=outs,
        compiler_params=params(8),
        name="add_pieces",
    )(mine, received)


def touch(arrays, after):
    def kernel(*refs):
        refs[-1][...] = jnp.zeros_like(refs[-1])

    return pl.pallas_call(
        kernel,
        in_specs=[whole()] * len(arrays) + [far()],
        out_specs=whole(),
        out_shape=like((8, 128), F32),
        compiler_params=params(4),
        name="touch",
    )(*arrays, after)


def final_shares(pieces, kv_grads, in_pieces, own, w_query, w_key, w_value, w_out, after):
    count, parts = len(pieces), len(in_pieces)
    picked, part = in_pieces[0].shape
    half = w_query.shape[1]

    def kernel(*refs):
        piece_refs, in_refs = refs[:count], refs[count : count + parts]
        kv_ref, own_ref, query_ref, key_ref, value_ref, out_w_ref, _ = refs[
            count + parts : count + parts + 7
        ]
        out_refs = refs[count + parts + 7 :]
        tp = lax.axis_index("tp")
        total = piece_refs[0][...].astype(F32)
        for ref in piece_refs[1:]:
            total += ref[...].astype(F32)
        total = total.astype(BF)
        query_grad, attended = total[:, :half], total[:, half:]
        kv_sum = kv_ref[0].astype(F32)
        for b in range(1, kv_ref.shape[0]):
            kv_sum += kv_ref[b].astype(F32)
        kv_sum = kv_sum.astype(BF)
        key_grad, value_grad = kv_sum[:, :HEAD_DIM], kv_sum[:, HEAD_DIM:]
        stat = jnp.zeros((picked, 1), F32)
        for s in range(parts):
            owner = lax.rem(tp + s, parts)
            rows = pl.ds(pl.multiple_of(owner * part, part), part)
            hidden = mm(query_grad, query_ref[rows, :], NT)
            hidden += mm(key_grad, key_ref[rows, :], NT)
            hidden += mm(value_grad, value_ref[rows, :], NT)
            rows_in = in_refs[(parts - s) % parts][...].astype(F32)
            stat += jnp.sum(hidden * rows_in, axis=1, keepdims=True)
            out_refs[s][:, :part] = hidden.astype(BF)
            out_refs[s][:, part : 2 * part] = mm(attended, out_w_ref[:, rows], NN).astype(BF)
        stat = stat * (1.0 / (part * parts))
        grads = own_ref[:, half:].astype(F32)
        gate_sum = jnp.sum(attended.astype(F32) * grads, axis=1, keepdims=True)
        stat_high, gate_high = stat.astype(BF).astype(F32), gate_sum.astype(BF).astype(F32)
        lane = lax.broadcasted_iota(jnp.int32, (picked, 128), 1)
        extra = jnp.where(lane == 0, stat_high, 0.0)
        extra = jnp.where(lane == 1, gate_high, extra)
        extra = jnp.where(lane == 2, stat - stat_high, extra)
        extra = jnp.where(lane == 3, gate_sum - gate_high, extra).astype(BF)
        for s in range(parts):
            out_refs[s][:, 2 * part :] = extra

    ins = (*pieces, *in_pieces, kv_grads, own, w_query, w_key, w_value, w_out)
    outs = [like((picked, 2 * part + 128))] * parts
    return pl.pallas_call(
        kernel,
        in_specs=[whole()] * len(ins) + [far()],
        out_specs=[whole()] * parts,
        out_shape=outs,
        compiler_params=params(16),
        name="final_shares",
    )(*ins, after)


def put_block(base, spot, new, i, rows):
    row = lax.broadcasted_iota(jnp.int32, (rows, spot.shape[1]), 0)
    here = jnp.where(row + i * rows == spot, 1.0, 0.0)
    hit = jnp.max(here, axis=1, keepdims=True) > 0.5
    return jnp.where(hit, mm(here.astype(BF), new, NN), base.astype(F32)).astype(BF)


def put_rows(sizes, tokens, cotangent, chosen, rows_in, rows_grad, shares, scales, router):
    (total, width), parts = cotangent.shape, sizes[3]
    rows = min(128, total)
    steps = total // rows

    def kernel(chosen_ref, in_ref, grad_ref, scales_ref, router_ref, tokens_ref, cotangent_ref, *refs):
        share_refs = refs[:parts]
        mixed_ref, input_grad_ref, block_ref, sems = refs[parts:]
        tp = lax.axis_index("tp")
        gating, inverse_rows = scales_ref[:, 0:1], scales_ref[:, 1:2]
        wide_in = in_ref[...].astype(F32)
        summed = share_refs[0][...].astype(F32)
        for ref in share_refs[1:]:
            summed += ref[...].astype(F32)
        hidden, branch, extra = summed[:, :width], summed[:, width : 2 * width], summed[:, 2 * width :]
        row_stat = extra[:, 0:1] + extra[:, 2:3]
        logit_grad = (extra[:, 1:2] + extra[:, 3:4]) * (1.0 - gating)
        router_own = router_ref[:, pl.ds(pl.multiple_of(tp * width, width), width)].astype(F32)
        delta = inverse_rows * hidden - wide_in * (inverse_rows**3 * row_stat)
        delta = delta + logit_grad * router_own
        grad_rows = (grad_ref[...].astype(F32) + delta).astype(BF)
        mixed_rows = (wide_in + gating * branch).astype(BF)
        spot = chosen_ref[...] - my_first_row(sizes, total)
        started = []
        pairs = ((tokens_ref, mixed_rows, mixed_ref), (cotangent_ref, grad_rows, input_grad_ref))
        for i in range(steps):
            part = slice(i * rows, (i + 1) * rows)
            for a, (base_ref, new, out_ref) in enumerate(pairs):
                block_ref[a, part, :] = put_block(base_ref[part, :], spot, new, i, rows)
                copy = pltpu.make_async_copy(block_ref.at[a, part], out_ref.at[part], sems.at[a, i])
                copy.start()
                started.append(copy)
        for copy in started:
            copy.wait()

    ins = (chosen, rows_in, rows_grad, scales, router, tokens, cotangent, *shares)
    return pl.pallas_call(
        kernel,
        in_specs=[whole()] * len(ins),
        out_specs=[far()] * 2,
        out_shape=[like((total, width))] * 2,
        scratch_shapes=[pltpu.VMEM((2, total, width), BF), pltpu.SemaphoreType.DMA((2, steps))],
        compiler_params=params(16),
        name="put_rows",
    )(*ins)


class Tiles:
    def __init__(self, picked, planes, columns, cores, heads):
        self.picked, self.planes, self.columns, self.cores, self.heads = (
            picked, planes, columns, cores, heads,
        )
        self.group = cores * picked
        self.lanes = heads * self.group
        self.keys = planes * picked
        self.half = heads * HEAD_DIM

    def fill(self, place, own, other, group_ref):
        core = place[2]
        mine = pl.ds(pl.multiple_of(core * self.picked, self.picked), self.picked)
        theirs = pl.ds(pl.multiple_of((1 - core) * self.picked, self.picked), self.picked)
        for s in range(self.columns):
            group_ref[s, mine, :] = own[s][...]
            group_ref[s, theirs, :] = other[s][...]

    def stacked(self, group_ref, s, first):
        parts = [
            group_ref[s, :, first + h * HEAD_DIM : first + (h + 1) * HEAD_DIM]
            for h in range(self.heads)
        ]
        return jnp.concatenate(parts, axis=0)

    def y_of(self, place, s):
        return lax.rem(place[1] + self.columns - s, self.columns)

    def scores(self, place, keys, queries, s):
        z, y, core = place[0], place[1], place[2]
        plane_rows = self.columns * self.group
        logits = mm(keys, queries, NT) * (LOG2E / math.sqrt(HEAD_DIM))
        key = lax.broadcasted_iota(jnp.int32, (self.keys, 1), 0)
        key_rank = (
            lax.div(key, self.picked) * plane_rows
            + (y * self.cores + core) * self.picked
            + lax.rem(key, self.picked)
        )
        lane = lax.broadcasted_iota(jnp.int32, (1, self.lanes), 1)
        query_rank = z * plane_rows + self.y_of(place, s) * self.group + lax.rem(lane, self.group)
        return jnp.where(key_rank <= query_rank, logits, FLOOR)


def softmax_parts(tiles, own, other, key_values):
    n = tiles.columns

    def kernel(kv_ref, *refs):
        own_refs, other_refs, out_ref, group_ref = refs[:n], refs[n : 2 * n], refs[2 * n], refs[-1]
        at = my_place()
        tiles.fill(at, own_refs, other_refs, group_ref)
        keys, values = kv_ref[:, :HEAD_DIM], kv_ref[:, HEAD_DIM:]
        for s in range(n):
            queries = tiles.stacked(group_ref, s, 0)
            grads = tiles.stacked(group_ref, s, tiles.half)
            logits = tiles.scores(at, keys, queries, s)
            top = jnp.max(logits, axis=0, keepdims=True)
            weights = jnp.exp2(logits - top)
            prob_grad = mm(values, grads, NT)
            total = jnp.sum(weights, axis=0, keepdims=True)
            inner = jnp.sum(weights * prob_grad, axis=0, keepdims=True)
            some = top > 0.5 * FLOOR
            slot = tiles.y_of(at, s)
            out_ref[slot, 0:1, :] = jnp.where(some, top + jnp.log(total) * LOG2E, FLOOR)
            out_ref[slot, 1:2, :] = jnp.where(some, inner / total, 0.0)

    return pl.pallas_call(
        kernel,
        in_specs=[whole()] * (1 + 2 * n),
        out_specs=whole(),
        out_shape=jax.ShapeDtypeStruct((n, 2, tiles.lanes), F32),
        scratch_shapes=[pltpu.VMEM((n, tiles.group, 2 * tiles.half), BF)],
        compiler_params=params(24),
        name="softmax_parts",
    )(key_values, *own, *other)


def attention_parts(tiles, own, other, key_values, parts):
    n = tiles.columns
    scale = 1.0 / math.sqrt(HEAD_DIM)

    def kernel(kv_ref, parts_ref, *refs):
        own_refs, other_refs = refs[:n], refs[n : 2 * n]
        mine_ref, theirs_ref, kv_grad_ref, group_ref, result_ref = refs[2 * n :]
        at = my_place()
        tiles.fill(at, own_refs, other_refs, group_ref)
        keys, values = kv_ref[:, :HEAD_DIM], kv_ref[:, HEAD_DIM:]
        keys_t, values_t = keys.T, values.T
        key_grad = jnp.zeros((tiles.keys, HEAD_DIM), F32)
        value_grad = jnp.zeros((tiles.keys, HEAD_DIM), F32)
        core = at[2]
        mine = pl.ds(pl.multiple_of(core * tiles.picked, tiles.picked), tiles.picked)
        theirs = pl.ds(pl.multiple_of((1 - core) * tiles.picked, tiles.picked), tiles.picked)
        for s in range(n):
            slot = tiles.y_of(at, s)
            tops = [parts_ref[b, slot, 0:1, :] for b in range(n * tiles.cores)]
            top = tops[0]
            for one in tops[1:]:
                top = jnp.maximum(top, one)
            total, inner = jnp.zeros_like(top), jnp.zeros_like(top)
            for b in range(n * tiles.cores):
                weight = jnp.exp2(tops[b] - top)
                total += weight
                inner += weight * parts_ref[b, slot, 1:2, :]
            shift = top + jnp.log(total) * LOG2E
            row_inner = inner / total
            queries = tiles.stacked(group_ref, s, 0)
            grads = tiles.stacked(group_ref, s, tiles.half)
            probs = jnp.exp2(tiles.scores(at, keys, queries, s) - shift)
            prob_grad = mm(values, grads, NT)
            score_low = (probs * (prob_grad - row_inner)).astype(BF)
            probs_low = probs.astype(BF)
            key_grad += mm(score_low, queries, NN)
            value_grad += mm(probs_low, grads, NN)
            query_t = mm(keys_t, score_low, NN) * scale
            output_t = mm(values_t, probs_low, NN)
            for h in range(tiles.heads):
                lanes = slice(h * tiles.group, (h + 1) * tiles.group)
                columns = slice(h * HEAD_DIM, (h + 1) * HEAD_DIM)
                shifted = slice(tiles.half + h * HEAD_DIM, tiles.half + (h + 1) * HEAD_DIM)
                result_ref[s, :, columns] = query_t[:, lanes].T.astype(BF)
                result_ref[s, :, shifted] = output_t[:, lanes].T.astype(BF)
            mine_ref[s, :, :] = result_ref[s, mine, :]
            theirs_ref[s, :, :] = result_ref[s, theirs, :]
        kv_grad_ref[:, :HEAD_DIM] = (key_grad * scale).astype(BF)
        kv_grad_ref[:, HEAD_DIM:] = value_grad.astype(BF)

    rows = like((n, tiles.picked, 2 * tiles.half))
    outs = [rows, rows, like((tiles.keys, 2 * HEAD_DIM))]
    return pl.pallas_call(
        kernel,
        in_specs=[whole()] * (2 + 2 * n),
        out_specs=[whole()] * 3,
        out_shape=outs,
        scratch_shapes=[pltpu.VMEM((n, tiles.group, 2 * tiles.half), BF)] * 2,
        compiler_params=params(24),
        name="attention_parts",
    )(key_values, parts, *own, *other)


def copies(array, count):
    return jnp.broadcast_to(array[None], (count,) + array.shape)


def exchange(array, axis):
    return lax.all_to_all(array, axis, 0, 0, tiled=True)


def shifted(array, axis, count, step):
    return lax.ppermute(array, axis, [(i, (i + step) % count) for i in range(count)])


def on_device(sizes, tokens, chosen, router, w_query, w_key, w_value, w_out, cotangent):
    planes, columns, cores, parts_tp = sizes
    picked = chosen.shape[0]
    chosen, router = chosen[None, :], router[None, :]
    tiles = Tiles(picked, planes, columns, cores, w_query.shape[1] // HEAD_DIM)

    rows_in = pick_rows(sizes, tokens, chosen)
    inputs = [rows_in] + [shifted(rows_in, "tp", parts_tp, s) for s in range(1, parts_tp)]
    rows_grad = pick_rows(sizes, cotangent, chosen)
    grads = [rows_grad] + [shifted(rows_grad, "tp", parts_tp, s) for s in range(1, parts_tp)]
    near = touch((w_out, w_key, w_value), rows_in)
    key_values, mine, scales = project(
        sizes, inputs, grads, router, w_query, w_key, w_value, w_out, near
    )
    own = [mine] + [shifted(mine, "y", columns, s) for s in range(1, columns)]
    key_values = exchange(key_values, "z").reshape(tiles.keys, 2 * HEAD_DIM)
    key_values, *own = lax.optimization_barrier((key_values, *own))
    other = [shifted(piece, "core", cores, 1) for piece in own]
    parts = softmax_parts(tiles, own, other, key_values)
    parts = exchange(copies(parts, columns * cores), ("y", "core"))
    mine, theirs, kv_grads = attention_parts(tiles, own, other, key_values, parts)

    kv_grads = exchange(kv_grads.reshape(planes, picked, 2 * HEAD_DIM), "z")
    chip = add_pieces(mine, shifted(theirs, "core", cores, 1))
    pieces = [chip[0]] + [shifted(chip[s], "y", columns, columns - s) for s in range(1, columns)]
    shares = final_shares(
        pieces, kv_grads, inputs, own[0], w_query, w_key, w_value, w_out, kv_grads
    )
    shares = [shares[0]] + [shifted(shares[s], "tp", parts_tp, s) for s in range(1, parts_tp)]
    mixed, input_grad = put_rows(
        sizes, tokens, cotangent, chosen, rows_in, rows_grad, shares, scales, router
    )
    return mixed, input_grad


def solution(mesh):
    sizes = (8, 4, 2, 4)
    return build(mesh, sizes)


def build(mesh, sizes):
    fine = Mesh(mesh.devices.reshape(sizes), ("z", "y", "core", "tp"))
    ctx = ("z", "y", "core")

    def step(*arrays):
        return on_device(sizes, *arrays)

    placed = (
        P(ctx, "tp"), P(ctx), P(), P(None, "tp"), P(None, "tp"), P(None, "tp"), P("tp", None), P(ctx, "tp"),
    )
    return jax.shard_map(
        step,
        mesh=fine,
        in_specs=placed,
        out_specs=(P(ctx, "tp"), P(ctx, "tp")),
        check_vma=False,
    )
```

time: 143 us -> 112 us (0.78)
  waiting for transfers between devices: 45.3 us -> 30.3 us
  matrix products: 8.72 us -> 0 us
  other arithmetic: 7.81 us -> 0 us
  local copies, waits for them, and re-layouts: 8.33 us -> 14.2 us
  Pallas kernels: 22.6 us -> 18.5 us
  starting transfers between devices: 38.2 us -> 36.3 us
    all_to_all x4 -> x2, waiting for transfers between devices: 30.7 us -> 7.05 us  [exchange(): return lax.all_to_all(array, axis, 0, 0, tiled=True)]
    all_to_all x4 -> x2, starting transfers between devices: 26.4 us -> 14.2 us  [exchange(): return lax.all_to_all(array, axis, 0, 0, tiled=True)]
    unnamed x37 -> x42, local copies, waits for them, and re-layouts: 3.37 us -> 14.2 us
    ppermute x14 -> x20, starting transfers between devices: 11.9 us -> 22.1 us  [shifted(): lax.ppermute(array, axis, [(i, (i + step) % count) for i in range(count)])]
    dot_general x9 -> x0, matrix products: 8.72 us -> none  [the longest x8 8.47 us: mm(): return lax.dot_general(left, right, dims, preferred_element_type=F32)]
    ppermute x14 -> x20, waiting for transfers between devices: 14.6 us -> 23.2 us  [shifted(): lax.ppermute(array, axis, [(i, (i + step) % count) for i in range(count)])]
    pallas_call x6 -> x9, Pallas kernels: 22.6 us -> 18.5 us  [the longest x1 4.38 us: attention_parts(): pl.pallas_call(kernel, in_specs=[whole()] * (2 + 2 * n), out_specs=[whole...]
    convert_element_type x6 -> x0, other arithmetic: 3 us -> none  [the longest x1 1.38 us: on_device(): chip = (mine.astype(F32) + received.astype(F32)).astype(BF)]
  transfers between devices with their start and end apart: 18 -> 22, of which waited for: 9 -> 14; matrix products, arithmetic and copies ran while one was open for 6% -> 0% of each run, Pallas kernels for 3% -> 2%
where the time goes in v2:
time: 112 us; the launch traced here: 110 us
  starting transfers between devices  36.3 us (32%)
  waiting for transfers between devices  30.3 us (27%)
  Pallas kernels  18.5 us (17%)
  local copies, waits for them, and re-layouts  14.2 us (13%)
  blocking collectives  10 us (9%)
    ppermute x20, waiting for transfers between devices, shifted(): lax.ppermute(array, axis, [(i, (i + step) % count) for i in range(count)])  23.2 us
    ppermute x20, starting transfers between devices, shifted(): lax.ppermute(array, axis, [(i, (i + step) % count) for i in range(count)])  22.1 us
    all_to_all x2, starting transfers between devices, exchange(): return lax.all_to_all(array, axis, 0, 0, tiled=True)  14.2 us
    unnamed x42, local copies, waits for them, and re-layouts  14.2 us
    all_to_all x1, blocking collectives, exchange(): return lax.all_to_all(array, axis, 0, 0, tiled=True)  10 us
    all_to_all x2, waiting for transfers between devices, exchange(): return lax.all_to_all(array, axis, 0, 0, tiled=True)  7.05 us
    pallas_call x1, Pallas kernels, attention_parts(): pl.pallas_call(kernel, in_specs=[whole()] * (2 + 2 * n), out_specs=[whole...  4.38 us
    pallas_call x1, Pallas kernels, final_shares(): pl.pallas_call(kernel, in_specs=[whole()] * len(ins) + [far()], out_specs...  3.9 us
  transfers between devices with their start and end apart: 22, of which 14 were waited for; matrix products, arithmetic and copies ran while one was open for 0% of the time, Pallas kernels for 2%

profile of v2, /device:TPU:2, one launch (start us, length us, event | category | flops | bytes accessed | tf_op | source)
XLA Modules:
  0.0 110.2 jit_solution(13883267517152560124)
XLA Ops:
  0.7 1.6 %copy-done.10 = bf16[1024,1024]{1,0:T(8,128)(2,1)S(1)} copy-done((bf16[1024,1024]{1,0:T(8,128)(2,1)S(1)}, bf16[1024,1024]{1,0:T(8,128)(2,1)}, u32[]{:S(2)}) %copy-start.10) | copy-done | bytes 2097176
  3.5 2.3 %collective-permute-start.5 = (bf16[64,1024]{1,0:T(8,128)(2,1)S(1)}, bf16[64,1024]{1,0:T(8,128)(2,1)S(1)}, u32[]{:S(2)}, u32[]{:S(2)}) collective-permute-start(bf16[64,1024]{1,0:T(8,128)(2,1)S(1)} %pick_rows.3.refs_4_.grad_ref), channel_id=1, source_target_pairs={{0,3},{1,0},{2,1},{3,2},{4,7},{5,4},{6,5},{7,6},{8,11},{9,8},{10,9... | collective-permute-start | bytes 393224 | tf_op jit(solution)/shard_map/ppermute | solution.py:426
  6.5 1.8 %collective-permute-start.3 = (bf16[64,1024]{1,0:T(8,128)(2,1)S(1)}, bf16[64,1024]{1,0:T(8,128)(2,1)S(1)}, u32[]{:S(2)}, u32[]{:S(2)}) collective-permute-start(bf16[64,1024]{1,0:T(8,128)(2,1)S(1)} %pick_rows.3.refs_4_.grad_ref), channel_id=1, source_target_pairs={{0,1},{1,2},{2,3},{3,0},{4,5},{5,6},{6,7},{7,4},{8,9},{9,10},{10,1... | collective-permute-start | bytes 393224 | tf_op jit(solution)/shard_map/ppermute | solution.py:426
  8.3 1.6 %copy-done.8 = bf16[1024,1024]{1,0:T(8,128)(2,1)S(1)} copy-done((bf16[1024,1024]{1,0:T(8,128)(2,1)S(1)}, bf16[1024,1024]{1,0:T(8,128)(2,1)}, u32[]{:S(2)}) %copy-start.8) | copy-done | bytes 2097176
  10.7 2.9 %collective-permute-start.1 = (bf16[64,1024]{1,0:T(8,128)(2,1)S(1)}, bf16[64,1024]{1,0:T(8,128)(2,1)S(1)}, u32[]{:S(2)}, u32[]{:S(2)}) collective-permute-start(bf16[64,1024]{1,0:T(8,128)(2,1)S(1)} %pick_rows.2.refs_3_.refs_0_.refs_4_.in_ref), channel_id=1, source_target_pairs={{0,2},{1,3},{2,0},{3,1},{4,6},{5,7},{6,4},{7,5},{8,10},{9,11},{10,... | collective-permute-start | bytes 393224 | tf_op jit(solution)/shard_map/ppermute | solution.py:426
  14.6 1.2 %copy-done.4 = bf16[4096,128]{1,0:T(8,128)(2,1)S(1)} copy-done((bf16[4096,128]{1,0:T(8,128)(2,1)S(1)}, bf16[4096,128]{1,0:T(8,128)(2,1)}, u32[]{:S(2)}) %copy-start.4) | copy-done | bytes 1048600
  15.8 1.2 %copy-done.6 = bf16[4096,128]{1,0:T(8,128)(2,1)S(1)} copy-done((bf16[4096,128]{1,0:T(8,128)(2,1)S(1)}, bf16[4096,128]{1,0:T(8,128)(2,1)}, u32[]{:S(2)}) %copy-start.6) | copy-done | bytes 1048600
  17.1 1.2 %collective-permute-done.1.refs_2_.refs_6_ = bf16[64,1024]{1,0:T(8,128)(2,1)S(1)} collective-permute-done((bf16[64,1024]{1,0:T(8,128)(2,1)S(1)}, bf16[64,1024]{1,0:T(8,128)(2,1)S(1)}, u32[]{:S(2)}, u32[]{:S(2)}) %collective-permute-start.1) | collective-permute-done | bytes 131104 | tf_op jit(solution)/shard_map/ppermute | solution.py:426
  18.3 1.2 %collective-permute-done.refs_1_.refs_5_ = bf16[64,1024]{1,0:T(8,128)(2,1)S(1)} collective-permute-done((bf16[64,1024]{1,0:T(8,128)(2,1)S(1)}, bf16[64,1024]{1,0:T(8,128)(2,1)S(1)}, u32[]{:S(2)}, u32[]{:S(2)}) %collective-permute-start) | collective-permute-done | bytes 131104 | tf_op jit(solution)/shard_map/ppermute | solution.py:426
  19.8 2.9 %project.1 = (bf16[8,64,256]{2,1,0:T(8,128)(2,1)}, bf16[64,1024]{1,0:T(8,128)(2,1)S(1)}, f32[64,128]{1,0:T(8,128)S(1)}) custom-call(bf16[64,1024]{1,0:T(8,128)(2,1)S(1)} %pick_rows.2.refs_3_.refs_0_.refs_4_.in_ref, bf16[64,1024]{1,0:T(8,128)(2,1)S(1)} %collective-permute-done.refs_1_.refs_5_, bf16[64,1024]{1,0:T(8,128)(2,1)S(1)} %collective-permute-done.1.refs_2_.refs_6_, ...), custom_call_target="tpu_custom_call" | custom-call | tf_op jit(solution)/shard_map/project/pallas_call | solution.py:125
  23.4 8.5 %all-to-all-start = ((bf16[8,64,256]{2,1,0:T(8,128)(2,1)}), bf16[8,64,256]{2,1,0:T(8,128)(2,1)S(1)}, u32[]{:S(2)}, u32[]{:S(2)}) async-start(bf16[8,64,256]{2,1,0:T(8,128)(2,1)} %get-tuple-element.22), calls=%async_computation | async-start | bytes 524288 | tf_op jit(solution)/shard_map/all_to_all | solution.py:422
  31.8 3.0 %collective-permute-start.8 = (bf16[64,1024]{1,0:T(8,128)(2,1)S(1)}, bf16[64,1024]{1,0:T(8,128)(2,1)S(1)}, u32[]{:S(2)}, u32[]{:S(2)}) collective-permute-start(bf16[64,1024]{1,0:T(8,128)(2,1)S(1)} %get-tuple-element.25.refs_0_.refs_9_), channel_id=1, source_target_pairs={{0,24},{8,0},{16,8},{24,16},{1,25},{9,1},{17,9},{25,17},{2,26},{10... | collective-permute-start | bytes 393224 | tf_op jit(solution)/shard_map/ppermute | solution.py:426
  36.5 2.3 %collective-permute-done.8.refs_3_ = bf16[64,1024]{1,0:T(8,128)(2,1)S(1)} collective-permute-done((bf16[64,1024]{1,0:T(8,128)(2,1)S(1)}, bf16[64,1024]{1,0:T(8,128)(2,1)S(1)}, u32[]{:S(2)}, u32[]{:S(2)}) %collective-permute-start.8) | collective-permute-done | bytes 131104 | tf_op jit(solution)/shard_map/ppermute | solution.py:426
  38.8 2.7 %collective-permute-done.7.refs_2_ = bf16[64,1024]{1,0:T(8,128)(2,1)S(1)} collective-permute-done((bf16[64,1024]{1,0:T(8,128)(2,1)S(1)}, bf16[64,1024]{1,0:T(8,128)(2,1)S(1)}, u32[]{:S(2)}, u32[]{:S(2)}) %collective-permute-start.7) | collective-permute-done | bytes 131104 | tf_op jit(solution)/shard_map/ppermute | solution.py:426
  41.4 1.3 %collective-permute-done.6.refs_1_ = bf16[64,1024]{1,0:T(8,128)(2,1)S(1)} collective-permute-done((bf16[64,1024]{1,0:T(8,128)(2,1)S(1)}, bf16[64,1024]{1,0:T(8,128)(2,1)S(1)}, u32[]{:S(2)}, u32[]{:S(2)}) %collective-permute-start.6) | collective-permute-done | bytes 131104 | tf_op jit(solution)/shard_map/ppermute | solution.py:426
  44.8 1.8 %softmax_parts.1 = f32[4,2,512]{2,1,0:T(2,128)S(1)} custom-call(bf16[512,256]{1,0:T(8,128)(2,1)S(1)} %bitcast.3, bf16[64,1024]{1,0:T(8,128)(2,1)S(1)} %get-tuple-element.25.refs_0_.refs_9_, bf16[64,1024]{1,0:T(8,128)(2,1)S(1)} %collective-permute-done.6.refs_1_, bf16[64,1024]{1,0:T(8,128)(2,1)S(1)} %collective-permute-done.7.refs_2_, ...), custom_call_target="tpu_custom_call" | custom-call | tf_op jit(solution)/shard_map/softmax_parts/pallas_call | solution.py:343
  46.6 10.0 %all_to_all.15.parts_ref = f32[8,4,2,512]{3,2,1,0:T(2,128)S(1)} all-to-all(f32[8,4,2,512]{3,2,1,0:T(2,128)S(1)} %broadcast_in_dim.14), channel_id=1, replica_groups=mesh['z'=8,'y'=4,'core'=2,'tp'=4] {'y','core'}, dimensions={0} | all-to-all | bytes 262144 | tf_op jit(solution)/shard_map/all_to_all | solution.py:422
  56.6 4.4 %attention_parts.1 = (bf16[4,64,1024]{2,1,0:T(8,128)(2,1)S(1)}, bf16[4,64,1024]{2,1,0:T(8,128)(2,1)}, bf16[512,256]{1,0:T(8,128)(2,1)S(1)}) custom-call(bf16[512,256]{1,0:T(8,128)(2,1)S(1)} %bitcast.4, f32[8,4,2,512]{3,2,1,0:T(2,128)S(1)} %all_to_all.15.parts_ref, bf16[64,1024]{1,0:T(8,128)(2,1)S(1)} %get-tuple-element.25.refs_0_.refs_9_, ...), custom_call_target="tpu_custom_call" | custom-call | tf_op jit(solution)/shard_map/attention_parts/pallas_call | solution.py:406
  62.5 5.7 %all-to-all-start.2 = ((bf16[8,64,256]{2,1,0:T(8,128)(2,1)}), bf16[8,64,256]{2,1,0:T(8,128)(2,1)S(1)}, u32[]{:S(2)}, u32[]{:S(2)}) async-start(bf16[8,64,256]{2,1,0:T(8,128)(2,1)} %bitcast.5), calls=%async_computation.2 | async-start | bytes 524288 | tf_op jit(solution)/shard_map/all_to_all | solution.py:422
  69.3 1.8 %add_pieces.1 = (bf16[64,1024]{1,0:T(8,128)(2,1)S(1)}, bf16[64,1024]{1,0:T(8,128)(2,1)}, bf16[64,1024]{1,0:T(8,128)(2,1)}, bf16[64,1024]{1,0:T(8,128)(2,1)}) custom-call(bf16[4,64,1024]{2,1,0:T(8,128)(2,1)S(1)} %copy-done.13, bf16[4,64,1024]{2,1,0:T(8,128)(2,1)} %collective-permute-done.13.received_ref), custom_call_target="tpu_custom_call" | custom-call | tf_op jit(solution)/shard_map/add_pieces/pallas_call | solution.py:143
  72.3 1.5 %collective-permute-start.15 = (bf16[64,1024]{1,0:T(8,128)(2,1)}, bf16[64,1024]{1,0:T(8,128)(2,1)S(1)}, u32[]{:S(2)}, u32[]{:S(2)}) collective-permute-start(bf16[64,1024]{1,0:T(8,128)(2,1)} %get-tuple-element.33), channel_id=1, source_target_pairs={{0,16},{8,24},{16,0},{24,8},{1,17},{9,25},{17,1},{25,9},{2,18},{10... | collective-permute-start | bytes 393224 | tf_op jit(solution)/shard_map/ppermute | solution.py:426
  73.8 7.0 %all-to-all-done.2.refs_8_.refs_14_ = bf16[8,64,256]{2,1,0:T(8,128)(2,1)S(1)} async-done(((bf16[8,64,256]{2,1,0:T(8,128)(2,1)}), bf16[8,64,256]{2,1,0:T(8,128)(2,1)S(1)}, u32[]{:S(2)}, u32[]{:S(2)}) %all-to-all-start.2) | async-done | bytes 262176 | tf_op jit(solution)/shard_map/all_to_all | solution.py:422
  80.8 1.4 %collective-permute-done.16.refs_3_ = bf16[64,1024]{1,0:T(8,128)(2,1)} collective-permute-done((bf16[64,1024]{1,0:T(8,128)(2,1)}, bf16[64,1024]{1,0:T(8,128)(2,1)}, u32[]{:S(2)}, u32[]{:S(2)}) %collective-permute-start.16) | collective-permute-done | bytes 131104 | tf_op jit(solution)/shard_map/ppermute | solution.py:426
  82.3 2.2 %copy-done.1 = bf16[512,4096]{1,0:T(8,128)(2,1)S(1)} copy-done((bf16[512,4096]{1,0:T(8,128)(2,1)S(1)}, bf16[512,4096]{1,0:T(8,128)(2,1)}, u32[]{:S(2)}) %copy-start.1) | copy-done | bytes 4194328
  84.5 2.2 %copy-done.3 = bf16[4096,512]{1,0:T(8,128)(2,1)S(1)} copy-done((bf16[4096,512]{1,0:T(8,128)(2,1)S(1)}, bf16[4096,512]{1,0:T(8,128)(2,1)}, u32[]{:S(2)}) %copy-start.3) | copy-done | bytes 4194328
  86.6 3.9 %final_shares.1 = (bf16[64,2176]{1,0:T(8,128)(2,1)S(1)}, bf16[64,2176]{1,0:T(8,128)(2,1)S(1)}, bf16[64,2176]{1,0:T(8,128)(2,1)S(1)}, bf16[64,2176]{1,0:T(8,128)(2,1)S(1)}) custom-call(bf16[64,1024]{1,0:T(8,128)(2,1)S(1)} %get-tuple-element.31.refs_0_, bf16[64,1024]{1,0:T(8,128)(2,1)S(1)} %collective-permute-done.14.refs_1_, ...), custom_call_target="tpu_custom_call" | custom-call | tf_op jit(solution)/shard_map/final_shares/pallas_call | solution.py:214
  90.6 1.2 %collective-permute-start.17 = (bf16[64,2176]{1,0:T(8,128)(2,1)S(1)}, bf16[64,2176]{1,0:T(8,128)(2,1)S(1)}, u32[]{:S(2)}, u32[]{:S(2)}) collective-permute-start(bf16[64,2176]{1,0:T(8,128)(2,1)S(1)} %get-tuple-element.37), channel_id=1, source_target_pairs={{0,1},{1,2},{2,3},{3,0},{4,5},{5,6},{6,7},{7,4},{8,9},{9,10},{10,1... | collective-permute-start | bytes 835592 | tf_op jit(solution)/shard_map/ppermute | solution.py:426
  91.8 2.8 %collective-permute-start.18 = (bf16[64,2176]{1,0:T(8,128)(2,1)S(1)}, bf16[64,2176]{1,0:T(8,128)(2,1)S(1)}, u32[]{:S(2)}, u32[]{:S(2)}) collective-permute-start(bf16[64,2176]{1,0:T(8,128)(2,1)S(1)} %get-tuple-element.38), channel_id=1, source_target_pairs={{0,2},{1,3},{2,0},{3,1},{4,6},{5,7},{6,4},{7,5},{8,10},{9,11},{10,... | collective-permute-start | bytes 835592 | tf_op jit(solution)/shard_map/ppermute | solution.py:426
  95.4 4.7 %collective-permute-done.17.refs_1_ = bf16[64,2176]{1,0:T(8,128)(2,1)S(1)} collective-permute-done((bf16[64,2176]{1,0:T(8,128)(2,1)S(1)}, bf16[64,2176]{1,0:T(8,128)(2,1)S(1)}, u32[]{:S(2)}, u32[]{:S(2)}) %collective-permute-start.17) | collective-permute-done | bytes 278560 | tf_op jit(solution)/shard_map/ppermute | solution.py:426
  100.1 2.8 %collective-permute-done.18.refs_2_ = bf16[64,2176]{1,0:T(8,128)(2,1)S(1)} collective-permute-done((bf16[64,2176]{1,0:T(8,128)(2,1)S(1)}, bf16[64,2176]{1,0:T(8,128)(2,1)S(1)}, u32[]{:S(2)}, u32[]{:S(2)}) %collective-permute-start.18) | collective-permute-done | bytes 278560 | tf_op jit(solution)/shard_map/ppermute | solution.py:426
  102.9 4.5 %collective-permute-done.19.refs_3_ = bf16[64,2176]{1,0:T(8,128)(2,1)S(1)} collective-permute-done((bf16[64,2176]{1,0:T(8,128)(2,1)S(1)}, bf16[64,2176]{1,0:T(8,128)(2,1)S(1)}, u32[]{:S(2)}, u32[]{:S(2)}) %collective-permute-start.19) | collective-permute-done | bytes 278560 | tf_op jit(solution)/shard_map/ppermute | solution.py:426
  107.5 2.6 %put_rows.1 = (bf16[1024,1024]{1,0:T(8,128)(2,1)}, bf16[1024,1024]{1,0:T(8,128)(2,1)}) custom-call(s32[1,64]{1,0:T(1,128)S(1)} %bitcast.8, bf16[64,1024]{1,0:T(8,128)(2,1)S(1)} %pick_rows.2.refs_3_.refs_0_.refs_4_.in_ref, bf16[64,1024]{1,0:T(8,128)(2,1)S(1)} %pick_rows.3.refs_4_.grad_ref, f32[64,128]{1,0:T(8,128)S(1)} %copy-done.16, ...), custom_call_target="tpu_custom_call" | custom-call | tf_op jit(solution)/shard_map/put_rows/pallas_call | solution.py:267
  (66 shorter events, 12.9 us)
Async XLA Ops:
  0.6 7.7 %copy-start.18 = (s32[64]{0:T(128)S(1)}, s32[64]{0:T(128)}, u32[]{:S(2)}) copy-start(s32[64]{0:T(128)} %param.9) | copy-start | bytes 772
  2.9 11.7 %copy-start = (bf16[512,4096]{1,0:T(8,128)(2,1)S(1)}, bf16[512,4096]{1,0:T(8,128)(2,1)}, u32[]{:S(2)}) copy-start(bf16[512,4096]{1,0:T(8,128)(2,1)} %refs_13_.1) | copy-start | bytes 12582916
  3.5 10.1 %collective-permute-start.5 = (bf16[64,1024]{1,0:T(8,128)(2,1)S(1)}, bf16[64,1024]{1,0:T(8,128)(2,1)S(1)}, u32[]{:S(2)}, u32[]{:S(2)}) collective-permute-start(bf16[64,1024]{1,0:T(8,128)(2,1)S(1)} %pick_rows.3.refs_4_.grad_ref), channel_id=1, source_target_pairs={{0,3},{1,0},{2,1},{3,2},{4,7},{5,4},{6,5},{7,6},{8,11},{9,8},{10,9... | collective-permute-start | bytes 393224 | tf_op jit(solution)/shard_map/ppermute | solution.py:426
  5.8 11.3 %collective-permute-start.4 = (bf16[64,1024]{1,0:T(8,128)(2,1)S(1)}, bf16[64,1024]{1,0:T(8,128)(2,1)S(1)}, u32[]{:S(2)}, u32[]{:S(2)}) collective-permute-start(bf16[64,1024]{1,0:T(8,128)(2,1)S(1)} %pick_rows.3.refs_4_.grad_ref), channel_id=1, source_target_pairs={{0,2},{1,3},{2,0},{3,1},{4,6},{5,7},{6,4},{7,5},{8,10},{9,11},{10,... | collective-permute-start | bytes 393224 | tf_op jit(solution)/shard_map/ppermute | solution.py:426
  6.5 10.6 %collective-permute-start.3 = (bf16[64,1024]{1,0:T(8,128)(2,1)S(1)}, bf16[64,1024]{1,0:T(8,128)(2,1)S(1)}, u32[]{:S(2)}, u32[]{:S(2)}) collective-permute-start(bf16[64,1024]{1,0:T(8,128)(2,1)S(1)} %pick_rows.3.refs_4_.grad_ref), channel_id=1, source_target_pairs={{0,1},{1,2},{2,3},{3,0},{4,5},{5,6},{6,7},{7,4},{8,9},{9,10},{10,1... | collective-permute-start | bytes 393224 | tf_op jit(solution)/shard_map/ppermute | solution.py:426
  9.9 4.7 %copy-start.20 = (bf16[4096]{0:T(1024)(128)(2,1)S(1)}, bf16[4096]{0:T(1024)(128)(2,1)}, u32[]{:S(2)}) copy-start(bf16[4096]{0:T(1024)(128)(2,1)} %param.10) | copy-start | bytes 24580
  10.4 6.6 %collective-permute-start.2 = (bf16[64,1024]{1,0:T(8,128)(2,1)S(1)}, bf16[64,1024]{1,0:T(8,128)(2,1)S(1)}, u32[]{:S(2)}, u32[]{:S(2)}) collective-permute-start(bf16[64,1024]{1,0:T(8,128)(2,1)S(1)} %pick_rows.2.refs_3_.refs_0_.refs_4_.in_ref), channel_id=1, source_target_pairs={{0,3},{1,0},{2,1},{3,2},{4,7},{5,4},{6,5},{7,6},{8,11},{9,8},{10,9... | collective-permute-start | bytes 393224 | tf_op jit(solution)/shard_map/ppermute | solution.py:426
  10.7 7.5 %collective-permute-start.1 = (bf16[64,1024]{1,0:T(8,128)(2,1)S(1)}, bf16[64,1024]{1,0:T(8,128)(2,1)S(1)}, u32[]{:S(2)}, u32[]{:S(2)}) collective-permute-start(bf16[64,1024]{1,0:T(8,128)(2,1)S(1)} %pick_rows.2.refs_3_.refs_0_.refs_4_.in_ref), channel_id=1, source_target_pairs={{0,2},{1,3},{2,0},{3,1},{4,6},{5,7},{6,4},{7,5},{8,10},{9,11},{10,... | collective-permute-start | bytes 393224 | tf_op jit(solution)/shard_map/ppermute | solution.py:426
  13.6 5.9 %collective-permute-start = (bf16[64,1024]{1,0:T(8,128)(2,1)S(1)}, bf16[64,1024]{1,0:T(8,128)(2,1)S(1)}, u32[]{:S(2)}, u32[]{:S(2)}) collective-permute-start(bf16[64,1024]{1,0:T(8,128)(2,1)S(1)} %pick_rows.2.refs_3_.refs_0_.refs_4_.in_ref), channel_id=1, source_target_pairs={{0,1},{1,2},{2,3},{3,0},{4,5},{5,6},{6,7},{7,4},{8,9},{9,10},{10,1... | collective-permute-start | bytes 393224 | tf_op jit(solution)/shard_map/ppermute | solution.py:426
  17.0 2.5 %copy-start.2 = (bf16[4096,512]{1,0:T(8,128)(2,1)S(1)}, bf16[4096,512]{1,0:T(8,128)(2,1)}, u32[]{:S(2)}) copy-start(bf16[4096,512]{1,0:T(8,128)(2,1)} %refs_10_.3) | copy-start | bytes 12582916
  17.0 2.5 %copy-start.5 = (bf16[4096,128]{1,0:T(8,128)(2,1)S(1)}, bf16[4096,128]{1,0:T(8,128)(2,1)}, u32[]{:S(2)}) copy-start(bf16[4096,128]{1,0:T(8,128)(2,1)} %refs_11_.3) | copy-start | bytes 3145732
  17.0 2.8 %copy-start.7 = (bf16[4096,128]{1,0:T(8,128)(2,1)S(1)}, bf16[4096,128]{1,0:T(8,128)(2,1)}, u32[]{:S(2)}) copy-start(bf16[4096,128]{1,0:T(8,128)(2,1)} %refs_12_.3) | copy-start | bytes 3145732
  23.4 19.4 %all-to-all-start = ((bf16[8,64,256]{2,1,0:T(8,128)(2,1)}), bf16[8,64,256]{2,1,0:T(8,128)(2,1)S(1)}, u32[]{:S(2)}, u32[]{:S(2)}) async-start(bf16[8,64,256]{2,1,0:T(8,128)(2,1)} %get-tuple-element.22), calls=%async_computation | async-start | bytes 524288 | tf_op jit(solution)/shard_map/all_to_all | solution.py:422
  31.8 6.9 %collective-permute-start.8 = (bf16[64,1024]{1,0:T(8,128)(2,1)S(1)}, bf16[64,1024]{1,0:T(8,128)(2,1)S(1)}, u32[]{:S(2)}, u32[]{:S(2)}) collective-permute-start(bf16[64,1024]{1,0:T(8,128)(2,1)S(1)} %get-tuple-element.25.refs_0_.refs_9_), channel_id=1, source_target_pairs={{0,24},{8,0},{16,8},{24,16},{1,25},{9,1},{17,9},{25,17},{2,26},{10... | collective-permute-start | bytes 393224 | tf_op jit(solution)/shard_map/ppermute | solution.py:426
  34.8 6.6 %collective-permute-start.7 = (bf16[64,1024]{1,0:T(8,128)(2,1)S(1)}, bf16[64,1024]{1,0:T(8,128)(2,1)S(1)}, u32[]{:S(2)}, u32[]{:S(2)}) collective-permute-start(bf16[64,1024]{1,0:T(8,128)(2,1)S(1)} %get-tuple-element.25.refs_0_.refs_9_), channel_id=1, source_target_pairs={{0,16},{8,24},{16,0},{24,8},{1,17},{9,25},{17,1},{25,9},{2,18},{10... | collective-permute-start | bytes 393224 | tf_op jit(solution)/shard_map/ppermute | solution.py:426
  35.5 7.2 %collective-permute-start.6 = (bf16[64,1024]{1,0:T(8,128)(2,1)S(1)}, bf16[64,1024]{1,0:T(8,128)(2,1)S(1)}, u32[]{:S(2)}, u32[]{:S(2)}) collective-permute-start(bf16[64,1024]{1,0:T(8,128)(2,1)S(1)} %get-tuple-element.25.refs_0_.refs_9_), channel_id=1, source_target_pairs={{0,8},{8,16},{16,24},{24,0},{1,9},{9,17},{17,25},{25,1},{2,10},{10... | collective-permute-start | bytes 393224 | tf_op jit(solution)/shard_map/ppermute | solution.py:426
  42.7 1.3 %collective-permute-start.10 = (bf16[64,1024]{1,0:T(8,128)(2,1)S(1)}, bf16[64,1024]{1,0:T(8,128)(2,1)S(1)}, u32[]{:S(2)}, u32[]{:S(2)}) collective-permute-start(bf16[64,1024]{1,0:T(8,128)(2,1)S(1)} %collective-permute-done.6.refs_1_), channel_id=1, source_target_pairs={{0,4},{4,0},{1,5},{5,1},{2,6},{6,2},{3,7},{7,3},{8,12},{12,8},{9,1... | collective-permute-start | bytes 393224 | tf_op jit(solution)/shard_map/ppermute | solution.py:426
  42.7 1.5 %collective-permute-start.11 = (bf16[64,1024]{1,0:T(8,128)(2,1)S(1)}, bf16[64,1024]{1,0:T(8,128)(2,1)S(1)}, u32[]{:S(2)}, u32[]{:S(2)}) collective-permute-start(bf16[64,1024]{1,0:T(8,128)(2,1)S(1)} %collective-permute-done.7.refs_2_), channel_id=1, source_target_pairs={{0,4},{4,0},{1,5},{5,1},{2,6},{6,2},{3,7},{7,3},{8,12},{12,8},{9,1... | collective-permute-start | bytes 393224 | tf_op jit(solution)/shard_map/ppermute | solution.py:426
  43.2 1.3 %collective-permute-start.12 = (bf16[64,1024]{1,0:T(8,128)(2,1)S(1)}, bf16[64,1024]{1,0:T(8,128)(2,1)S(1)}, u32[]{:S(2)}, u32[]{:S(2)}) collective-permute-start(bf16[64,1024]{1,0:T(8,128)(2,1)S(1)} %collective-permute-done.8.refs_3_), channel_id=1, source_target_pairs={{0,4},{4,0},{1,5},{5,1},{2,6},{6,2},{3,7},{7,3},{8,12},{12,8},{9,1... | collective-permute-start | bytes 393224 | tf_op jit(solution)/shard_map/ppermute | solution.py:426
  43.2 1.5 %collective-permute-start.9 = (bf16[64,1024]{1,0:T(8,128)(2,1)S(1)}, bf16[64,1024]{1,0:T(8,128)(2,1)S(1)}, u32[]{:S(2)}, u32[]{:S(2)}) collective-permute-start(bf16[64,1024]{1,0:T(8,128)(2,1)S(1)} %get-tuple-element.25.refs_0_.refs_9_), channel_id=1, source_target_pairs={{0,4},{4,0},{1,5},{5,1},{2,6},{6,2},{3,7},{7,3},{8,12},{12,8},{9,1... | collective-permute-start | bytes 393224 | tf_op jit(solution)/shard_map/ppermute | solution.py:426
  62.5 5.7 %collective-permute-start.13 = (bf16[4,64,1024]{2,1,0:T(8,128)(2,1)}, bf16[4,64,1024]{2,1,0:T(8,128)(2,1)}, u32[]{:S(2)}, u32[]{:S(2)}) collective-permute-start(bf16[4,64,1024]{2,1,0:T(8,128)(2,1)} %get-tuple-element.30), channel_id=1, source_target_pairs={{0,4},{4,0},{1,5},{5,1},{2,6},{6,2},{3,7},{7,3},{8,12},{12,8},{9,1... | collective-permute-start | bytes 1572872 | tf_op jit(solution)/shard_map/ppermute | solution.py:426
  62.5 18.3 %all-to-all-start.2 = ((bf16[8,64,256]{2,1,0:T(8,128)(2,1)}), bf16[8,64,256]{2,1,0:T(8,128)(2,1)S(1)}, u32[]{:S(2)}, u32[]{:S(2)}) async-start(bf16[8,64,256]{2,1,0:T(8,128)(2,1)} %bitcast.5), calls=%async_computation.2 | async-start | bytes 524288 | tf_op jit(solution)/shard_map/all_to_all | solution.py:422
  71.1 9.7 %collective-permute-start.14 = (bf16[64,1024]{1,0:T(8,128)(2,1)}, bf16[64,1024]{1,0:T(8,128)(2,1)S(1)}, u32[]{:S(2)}, u32[]{:S(2)}) collective-permute-start(bf16[64,1024]{1,0:T(8,128)(2,1)} %get-tuple-element.32), channel_id=1, source_target_pairs={{0,24},{8,0},{16,8},{24,16},{1,25},{9,1},{17,9},{25,17},{2,26},{10... | collective-permute-start | bytes 393224 | tf_op jit(solution)/shard_map/ppermute | solution.py:426
  72.3 8.5 %collective-permute-start.15 = (bf16[64,1024]{1,0:T(8,128)(2,1)}, bf16[64,1024]{1,0:T(8,128)(2,1)S(1)}, u32[]{:S(2)}, u32[]{:S(2)}) collective-permute-start(bf16[64,1024]{1,0:T(8,128)(2,1)} %get-tuple-element.33), channel_id=1, source_target_pairs={{0,16},{8,24},{16,0},{24,8},{1,17},{9,25},{17,1},{25,9},{2,18},{10... | collective-permute-start | bytes 393224 | tf_op jit(solution)/shard_map/ppermute | solution.py:426
  73.8 8.5 %collective-permute-start.16 = (bf16[64,1024]{1,0:T(8,128)(2,1)}, bf16[64,1024]{1,0:T(8,128)(2,1)}, u32[]{:S(2)}, u32[]{:S(2)}) collective-permute-start(bf16[64,1024]{1,0:T(8,128)(2,1)} %get-tuple-element.34), channel_id=1, source_target_pairs={{0,8},{8,16},{16,24},{24,0},{1,9},{9,17},{17,25},{25,1},{2,10},{10... | collective-permute-start | bytes 393224 | tf_op jit(solution)/shard_map/ppermute | solution.py:426
  86.6 20.8 %copy-start.9 = (bf16[1024,1024]{1,0:T(8,128)(2,1)S(1)}, bf16[1024,1024]{1,0:T(8,128)(2,1)}, u32[]{:S(2)}) copy-start(bf16[1024,1024]{1,0:T(8,128)(2,1)} %tokens_ref.1) | copy-start | bytes 6291460
  86.6 20.8 %copy-start.11 = (bf16[1024,1024]{1,0:T(8,128)(2,1)S(1)}, bf16[1024,1024]{1,0:T(8,128)(2,1)}, u32[]{:S(2)}) copy-start(bf16[1024,1024]{1,0:T(8,128)(2,1)} %cotangent_ref.1) | copy-start | bytes 6291460
  86.6 20.8 %copy-start.16 = (f32[64,128]{1,0:T(8,128)S(1)}, f32[64,128]{1,0:T(8,128)}, u32[]{:S(2)}) copy-start(f32[64,128]{1,0:T(8,128)} %copy-done.15) | copy-start | bytes 98308
  86.6 20.8 %copy-start.19 = (s32[64]{0:T(128)S(1)}, s32[64]{0:T(128)}, u32[]{:S(2)}) copy-start(s32[64]{0:T(128)} %param.9) | copy-start | bytes 772
  90.6 9.6 %collective-permute-start.17 = (bf16[64,2176]{1,0:T(8,128)(2,1)S(1)}, bf16[64,2176]{1,0:T(8,128)(2,1)S(1)}, u32[]{:S(2)}, u32[]{:S(2)}) collective-permute-start(bf16[64,2176]{1,0:T(8,128)(2,1)S(1)} %get-tuple-element.37), channel_id=1, source_target_pairs={{0,1},{1,2},{2,3},{3,0},{4,5},{5,6},{6,7},{7,4},{8,9},{9,10},{10,1... | collective-permute-start | bytes 835592 | tf_op jit(solution)/shard_map/ppermute | solution.py:426
  91.8 11.1 %collective-permute-start.18 = (bf16[64,2176]{1,0:T(8,128)(2,1)S(1)}, bf16[64,2176]{1,0:T(8,128)(2,1)S(1)}, u32[]{:S(2)}, u32[]{:S(2)}) collective-permute-start(bf16[64,2176]{1,0:T(8,128)(2,1)S(1)} %get-tuple-element.38), channel_id=1, source_target_pairs={{0,2},{1,3},{2,0},{3,1},{4,6},{5,7},{6,4},{7,5},{8,10},{9,11},{10,... | collective-permute-start | bytes 835592 | tf_op jit(solution)/shard_map/ppermute | solution.py:426
  94.6 12.9 %collective-permute-start.19 = (bf16[64,2176]{1,0:T(8,128)(2,1)S(1)}, bf16[64,2176]{1,0:T(8,128)(2,1)S(1)}, u32[]{:S(2)}, u32[]{:S(2)}) collective-permute-start(bf16[64,2176]{1,0:T(8,128)(2,1)S(1)} %get-tuple-element.39), channel_id=1, source_target_pairs={{0,3},{1,0},{2,1},{3,2},{4,7},{5,4},{6,5},{7,6},{8,11},{9,8},{10,9... | collective-permute-start | bytes 835592 | tf_op jit(solution)/shard_map/ppermute | solution.py:426
  (11 other events, 13.8 us)

commit v3 on v2

--- a/solution.py
+++ b/solution.py
@@ -164,23 +164,46 @@
     )(*arrays, after)
 
 
-def final_shares(pieces, kv_grads, in_pieces, own, w_query, w_key, w_value, w_out, after):
-    count, parts = len(pieces), len(in_pieces)
-    picked, part = in_pieces[0].shape
-    half = w_query.shape[1]
+def branch_share(pieces, w_out, parts, after):
+    count = len(pieces)
+    picked, both = pieces[0].shape
+    half, part = both // 2, w_out.shape[1] // parts
 
     def kernel(*refs):
-        piece_refs, in_refs = refs[:count], refs[count : count + parts]
-        kv_ref, own_ref, query_ref, key_ref, value_ref, out_w_ref, _ = refs[
-            count + parts : count + parts + 7
-        ]
-        out_refs = refs[count + parts + 7 :]
+        piece_refs, out_w_ref = refs[:count], refs[count]
+        total_ref, out_refs = refs[count + 2], refs[count + 3 :]
         tp = lax.axis_index("tp")
         total = piece_refs[0][...].astype(F32)
         for ref in piece_refs[1:]:
             total += ref[...].astype(F32)
-        total = total.astype(BF)
-        query_grad, attended = total[:, :half], total[:, half:]
+        total_ref[...] = total.astype(BF)
+        attended = total_ref[:, half:]
+        for s in range(parts):
+            columns = pl.ds(pl.multiple_of(lax.rem(tp + s, parts) * part, part), part)
+            out_refs[s][...] = mm(attended, out_w_ref[:, columns], NN).astype(BF)
+
+    return pl.pallas_call(
+        kernel,
+        in_specs=[whole()] * (count + 1) + [far()],
+        out_specs=[whole()] * (1 + parts),
+        out_shape=[like((picked, both))] + [like((picked, part))] * parts,
+        compiler_params=params(16),
+        cost_estimate=pl.CostEstimate(flops=10**9, bytes_accessed=2**22, transcendentals=0),
+        name="branch_share",
+    )(*pieces, w_out, after)
+
+
+def hidden_share(total, kv_grads, in_pieces, own, w_query, w_key, w_value):
+    parts = len(in_pieces)
+    picked, part = in_pieces[0].shape
+    half = w_query.shape[1]
+
+    def kernel(total_ref, *refs):
+        in_refs = refs[:parts]
+        kv_ref, own_ref, query_ref, key_ref, value_ref = refs[parts : parts + 5]
+        out_refs = refs[parts + 5 :]
+        tp = lax.axis_index("tp")
+        query_grad, attended = total_ref[:, :half], total_ref[:, half:]
         kv_sum = kv_ref[0].astype(F32)
         for b in range(1, kv_ref.shape[0]):
             kv_sum += kv_ref[b].astype(F32)
@@ -188,15 +211,13 @@
         key_grad, value_grad = kv_sum[:, :HEAD_DIM], kv_sum[:, HEAD_DIM:]
         stat = jnp.zeros((picked, 1), F32)
         for s in range(parts):
-            owner = lax.rem(tp + s, parts)
-            rows = pl.ds(pl.multiple_of(owner * part, part), part)
+            rows = pl.ds(pl.multiple_of(lax.rem(tp + s, parts) * part, part), part)
             hidden = mm(query_grad, query_ref[rows, :], NT)
             hidden += mm(key_grad, key_ref[rows, :], NT)
             hidden += mm(value_grad, value_ref[rows, :], NT)
             rows_in = in_refs[(parts - s) % parts][...].astype(F32)
             stat += jnp.sum(hidden * rows_in, axis=1, keepdims=True)
             out_refs[s][:, :part] = hidden.astype(BF)
-            out_refs[s][:, part : 2 * part] = mm(attended, out_w_ref[:, rows], NN).astype(BF)
         stat = stat * (1.0 / (part * parts))
         grads = own_ref[:, half:].astype(F32)
         gate_sum = jnp.sum(attended.astype(F32) * grads, axis=1, keepdims=True)
@@ -207,18 +228,18 @@
         extra = jnp.where(lane == 2, stat - stat_high, extra)
         extra = jnp.where(lane == 3, gate_sum - gate_high, extra).astype(BF)
         for s in range(parts):
-            out_refs[s][:, 2 * part :] = extra
-
-    ins = (*pieces, *in_pieces, kv_grads, own, w_query, w_key, w_value, w_out)
-    outs = [like((picked, 2 * part + 128))] * parts
-    return pl.pallas_call(
-        kernel,
-        in_specs=[whole()] * len(ins) + [far()],
+            out_refs[s][:, part:] = extra
+
+    ins = (total, *in_pieces, kv_grads, own, w_query, w_key, w_value)
+    return pl.pallas_call(
+        kernel,
+        in_specs=[whole()] * len(ins),
         out_specs=[whole()] * parts,
-        out_shape=outs,
+        out_shape=[like((picked, part + 128))] * parts,
         compiler_params=params(16),
-        name="final_shares",
-    )(*ins, after)
+        cost_estimate=pl.CostEstimate(flops=2 * 10**10, bytes_accessed=2**26, transcendentals=0),
+        name="hidden_share",
+    )(*ins)
 
 
 def put_block(base, spot, new, i, rows):
@@ -228,51 +249,67 @@
     return jnp.where(hit, mm(here.astype(BF), new, NN), base.astype(F32)).astype(BF)
 
 
-def put_rows(sizes, tokens, cotangent, chosen, rows_in, rows_grad, shares, scales, router):
-    (total, width), parts = cotangent.shape, sizes[3]
+def put_rows(sizes, base, chosen, ins, rows_of, name):
+    total, width = base.shape
     rows = min(128, total)
     steps = total // rows
-
-    def kernel(chosen_ref, in_ref, grad_ref, scales_ref, router_ref, tokens_ref, cotangent_ref, *refs):
-        share_refs = refs[:parts]
-        mixed_ref, input_grad_ref, block_ref, sems = refs[parts:]
-        tp = lax.axis_index("tp")
+    count = len(ins)
+
+    def kernel(chosen_ref, base_ref, *refs):
+        out_ref, block_ref, sems = refs[count:]
+        new = rows_of(lax.axis_index("tp"), *refs[:count]).astype(BF)
+        spot = chosen_ref[...] - my_first_row(sizes, total)
+        started = []
+        for i in range(steps):
+            part = slice(i * rows, (i + 1) * rows)
+            block_ref[part, :] = put_block(base_ref[part, :], spot, new, i, rows)
+            copy = pltpu.make_async_copy(block_ref.at[part], out_ref.at[part], sems.at[i])
+            copy.start()
+            started.append(copy)
+        for copy in started:
+            copy.wait()
+
+    return pl.pallas_call(
+        kernel,
+        in_specs=[whole()] * (2 + count),
+        out_specs=far(),
+        out_shape=like((total, width)),
+        scratch_shapes=[pltpu.VMEM((total, width), BF), pltpu.SemaphoreType.DMA((steps,))],
+        compiler_params=params(8),
+        cost_estimate=pl.CostEstimate(flops=3 * 10**9, bytes_accessed=2**23, transcendentals=0),
+        name=name,
+    )(chosen, base, *ins)
+
+
+def put_mixed(sizes, tokens, chosen, rows_in, branches, scales):
+    def rows_of(tp, in_ref, scales_ref, *branch_refs):
+        branch = branch_refs[0][...].astype(F32)
+        for ref in branch_refs[1:]:
+            branch += ref[...].astype(F32)
+        return in_ref[...].astype(F32) + scales_ref[:, 0:1] * branch
+
+    return put_rows(sizes, tokens, chosen, (rows_in, scales, *branches), rows_of, "put_mixed")
+
+
+def put_grad(sizes, cotangent, chosen, rows_in, rows_grad, shares, scales, router):
+    width = cotangent.shape[1]
+
+    def rows_of(tp, in_ref, grad_ref, scales_ref, router_ref, *share_refs):
         gating, inverse_rows = scales_ref[:, 0:1], scales_ref[:, 1:2]
         wide_in = in_ref[...].astype(F32)
         summed = share_refs[0][...].astype(F32)
         for ref in share_refs[1:]:
             summed += ref[...].astype(F32)
-        hidden, branch, extra = summed[:, :width], summed[:, width : 2 * width], summed[:, 2 * width :]
+        hidden, extra = summed[:, :width], summed[:, width:]
         row_stat = extra[:, 0:1] + extra[:, 2:3]
         logit_grad = (extra[:, 1:2] + extra[:, 3:4]) * (1.0 - gating)
         router_own = router_ref[:, pl.ds(pl.multiple_of(tp * width, width), width)].astype(F32)
         delta = inverse_rows * hidden - wide_in * (inverse_rows**3 * row_stat)
         delta = delta + logit_grad * router_own
-        grad_rows = (grad_ref[...].astype(F32) + delta).astype(BF)
-        mixed_rows = (wide_in + gating * branch).astype(BF)
-        spot = chosen_ref[...] - my_first_row(sizes, total)
-        started = []
-        pairs = ((tokens_ref, mixed_rows, mixed_ref), (cotangent_ref, grad_rows, input_grad_ref))
-        for i in range(steps):
-            part = slice(i * rows, (i + 1) * rows)
-            for a, (base_ref, new, out_ref) in enumerate(pairs):
-                block_ref[a, part, :] = put_block(base_ref[part, :], spot, new, i, rows)
-                copy = pltpu.make_async_copy(block_ref.at[a, part], out_ref.at[part], sems.at[a, i])
-                copy.start()
-                started.append(copy)
-        for copy in started:
-            copy.wait()
-
-    ins = (chosen, rows_in, rows_grad, scales, router, tokens, cotangent, *shares)
-    return pl.pallas_call(
-        kernel,
-        in_specs=[whole()] * len(ins),
-        out_specs=[far()] * 2,
-        out_shape=[like((total, width))] * 2,
-        scratch_shapes=[pltpu.VMEM((2, total, width), BF), pltpu.SemaphoreType.DMA((2, steps))],
-        compiler_params=params(16),
-        name="put_rows",
-    )(*ins)
+        return grad_ref[...].astype(F32) + delta
+
+    ins = (rows_in, rows_grad, scales, router, *shares)
+    return put_rows(sizes, cotangent, chosen, ins, rows_of, "put_grad")
 
 
 class Tiles:
@@ -426,16 +463,28 @@
     return lax.ppermute(array, axis, [(i, (i + step) % count) for i in range(count)])
 
 
+def around_ring(piece, axis, count):
+    pieces = [piece, shifted(piece, axis, count, 1)]
+    if count == 2:
+        return pieces
+    last = shifted(piece, axis, count, count - 1)
+    return pieces + [shifted(last, axis, count, count - 1), last]
+
+
+def around_tp(shares, count):
+    return [shares[0]] + [shifted(shares[s], "tp", count, s) for s in range(1, count)]
+
+
 def on_device(sizes, tokens, chosen, router, w_query, w_key, w_value, w_out, cotangent):
     planes, columns, cores, parts_tp = sizes
     picked = chosen.shape[0]
     chosen, router = chosen[None, :], router[None, :]
     tiles = Tiles(picked, planes, columns, cores, w_query.shape[1] // HEAD_DIM)
 
+    rows_grad = pick_rows(sizes, cotangent, chosen)
+    grads = around_ring(rows_grad, "tp", parts_tp)
     rows_in = pick_rows(sizes, tokens, chosen)
     inputs = [rows_in] + [shifted(rows_in, "tp", parts_tp, s) for s in range(1, parts_tp)]
-    rows_grad = pick_rows(sizes, cotangent, chosen)
-    grads = [rows_grad] + [shifted(rows_grad, "tp", parts_tp, s) for s in range(1, parts_tp)]
     near = touch((w_out, w_key, w_value), rows_in)
     key_values, mine, scales = project(
         sizes, inputs, grads, router, w_query, w_key, w_value, w_out, near
@@ -451,12 +500,13 @@
     kv_grads = exchange(kv_grads.reshape(planes, picked, 2 * HEAD_DIM), "z")
     chip = add_pieces(mine, shifted(theirs, "core", cores, 1))
     pieces = [chip[0]] + [shifted(chip[s], "y", columns, columns - s) for s in range(1, columns)]
-    shares = final_shares(
-        pieces, kv_grads, inputs, own[0], w_query, w_key, w_value, w_out, kv_grads
-    )
-    shares = [shares[0]] + [shifted(shares[s], "tp", parts_tp, s) for s in range(1, parts_tp)]
-    mixed, input_grad = put_rows(
-        sizes, tokens, cotangent, chosen, rows_in, rows_grad, shares, scales, router
+    total, *branches = branch_share(pieces, w_out, parts_tp, kv_grads)
+    shares = hidden_share(total, kv_grads, inputs, own[0], w_query, w_key, w_value)
+    branches = around_tp(branches, parts_tp)
+    shares = around_tp(shares, parts_tp)
+    mixed = put_mixed(sizes, tokens, chosen, rows_in, branches, scales)
+    input_grad = put_grad(
+        sizes, cotangent, chosen, rows_in, rows_grad, shares, scales, router
     )
     return mixed, input_grad
 

time: 112 us -> 105 us (0.938)
  waiting for transfers between devices: 30.3 us -> 23.9 us
  local copies, waits for them, and re-layouts: 14.2 us -> 10.8 us
  starting transfers between devices: 36.3 us -> 39.6 us
    ppermute x20 -> x23, waiting for transfers between devices: 23.2 us -> 15.8 us  [shifted(): lax.ppermute(array, axis, [(i, (i + step) % count) for i in range(count)])]
    unnamed x42 -> x54, local copies, waits for them, and re-layouts: 14.2 us -> 10.8 us
    ppermute x20 -> x23, starting transfers between devices: 22.1 us -> 25.4 us  [shifted(): lax.ppermute(array, axis, [(i, (i + step) % count) for i in range(count)])]
    pallas_call x2 -> x4, Pallas kernels: 6.46 us -> 6.58 us  [the longest x2 3.53 us: put_rows(): pl.pallas_call(kernel, in_specs=[whole()] * (2 + count), out_specs=far(),...]
  transfers between devices with their start and end apart: 22 -> 25, of which waited for: 14 -> 14; matrix products, arithmetic and copies ran while one was open for 0% -> 0% of each run, Pallas kernels for 2% -> 6%
where the time goes in v3:
time: 105 us; the launch traced here: 104 us
  starting transfers between devices  39.6 us (38%)
  waiting for transfers between devices  23.9 us (23%)
  Pallas kernels  18.6 us (18%)
  local copies, waits for them, and re-layouts  10.8 us (10%)
  blocking collectives  9.99 us (10%)
  between operations  1.06 us (1%)
    ppermute x23, starting transfers between devices, shifted(): lax.ppermute(array, axis, [(i, (i + step) % count) for i in range(count)])  25.4 us
    ppermute x23, waiting for transfers between devices, shifted(): lax.ppermute(array, axis, [(i, (i + step) % count) for i in range(count)])  15.8 us
    all_to_all x2, starting transfers between devices, exchange(): return lax.all_to_all(array, axis, 0, 0, tiled=True)  14.2 us
    unnamed x54, local copies, waits for them, and re-layouts  10.8 us
    all_to_all x1, blocking collectives, exchange(): return lax.all_to_all(array, axis, 0, 0, tiled=True)  9.99 us
    all_to_all x2, waiting for transfers between devices, exchange(): return lax.all_to_all(array, axis, 0, 0, tiled=True)  8.1 us
    pallas_call x1, Pallas kernels, attention_parts(): pl.pallas_call(kernel, in_specs=[whole()] * (2 + 2 * n), out_specs=[whole...  4.38 us
    pallas_call x2, Pallas kernels, put_rows(): pl.pallas_call(kernel, in_specs=[whole()] * (2 + count), out_specs=far(),...  3.53 us
  transfers between devices with their start and end apart: 25, of which 14 were waited for; matrix products, arithmetic and copies ran while one was open for 0% of the time, Pallas kernels for 6%

profile of v3, /device:TPU:2, one launch (start us, length us, event | category | flops | bytes accessed | tf_op | source)
XLA Modules:
  0.0 104.0 jit_solution(17962893058196579566)
XLA Ops:
  0.7 1.6 %copy-done.10 = bf16[1024,1024]{1,0:T(8,128)(2,1)S(1)} copy-done((bf16[1024,1024]{1,0:T(8,128)(2,1)S(1)}, bf16[1024,1024]{1,0:T(8,128)(2,1)}, u32[]{:S(2)}) %copy-start.10) | copy-done | bytes 2097176
  3.5 2.3 %collective-permute-start.4 = (bf16[64,1024]{1,0:T(8,128)(2,1)S(1)}, bf16[64,1024]{1,0:T(8,128)(2,1)S(1)}, u32[]{:S(2)}, u32[]{:S(2)}) collective-permute-start(bf16[64,1024]{1,0:T(8,128)(2,1)S(1)} %pick_rows.3.refs_4_.refs_1_), channel_id=1, source_target_pairs={{0,3},{1,0},{2,1},{3,2},{4,7},{5,4},{6,5},{7,6},{8,11},{9,8},{10,9... | collective-permute-start | bytes 393224 | tf_op jit(solution)/shard_map/ppermute | solution.py:463
  5.8 1.6 %copy-done.8 = bf16[1024,1024]{1,0:T(8,128)(2,1)S(1)} copy-done((bf16[1024,1024]{1,0:T(8,128)(2,1)S(1)}, bf16[1024,1024]{1,0:T(8,128)(2,1)}, u32[]{:S(2)}) %copy-start.8) | copy-done | bytes 2097176
  8.0 2.1 %collective-permute-start.2 = (bf16[64,1024]{1,0:T(8,128)(2,1)S(1)}, bf16[64,1024]{1,0:T(8,128)(2,1)S(1)}, u32[]{:S(2)}, u32[]{:S(2)}) collective-permute-start(bf16[64,1024]{1,0:T(8,128)(2,1)S(1)} %pick_rows.2.refs_3_.refs_0_), channel_id=1, source_target_pairs={{0,3},{1,0},{2,1},{3,2},{4,7},{5,4},{6,5},{7,6},{8,11},{9,8},{10,9... | collective-permute-start | bytes 393224 | tf_op jit(solution)/shard_map/ppermute | solution.py:463
  11.2 2.5 %collective-permute-start = (bf16[64,1024]{1,0:T(8,128)(2,1)S(1)}, bf16[64,1024]{1,0:T(8,128)(2,1)S(1)}, u32[]{:S(2)}, u32[]{:S(2)}) collective-permute-start(bf16[64,1024]{1,0:T(8,128)(2,1)S(1)} %pick_rows.2.refs_3_.refs_0_), channel_id=1, source_target_pairs={{0,1},{1,2},{2,3},{3,0},{4,5},{5,6},{6,7},{7,4},{8,9},{9,10},{10,1... | collective-permute-start | bytes 393224 | tf_op jit(solution)/shard_map/ppermute | solution.py:463
  13.8 1.2 %copy-done.4 = bf16[4096,128]{1,0:T(8,128)(2,1)S(1)} copy-done((bf16[4096,128]{1,0:T(8,128)(2,1)S(1)}, bf16[4096,128]{1,0:T(8,128)(2,1)}, u32[]{:S(2)}) %copy-start.4) | copy-done | bytes 1048600
  15.0 1.2 %copy-done.6 = bf16[4096,128]{1,0:T(8,128)(2,1)S(1)} copy-done((bf16[4096,128]{1,0:T(8,128)(2,1)S(1)}, bf16[4096,128]{1,0:T(8,128)(2,1)}, u32[]{:S(2)}) %copy-start.6) | copy-done | bytes 1048600
  16.3 2.0 %collective-permute-done.1.refs_2_ = bf16[64,1024]{1,0:T(8,128)(2,1)S(1)} collective-permute-done((bf16[64,1024]{1,0:T(8,128)(2,1)S(1)}, bf16[64,1024]{1,0:T(8,128)(2,1)S(1)}, u32[]{:S(2)}, u32[]{:S(2)}) %collective-permute-start.1) | collective-permute-done | bytes 131104 | tf_op jit(solution)/shard_map/ppermute | solution.py:463
  19.3 2.9 %project.1 = (bf16[8,64,256]{2,1,0:T(8,128)(2,1)}, bf16[64,1024]{1,0:T(8,128)(2,1)S(1)}, f32[64,128]{1,0:T(8,128)S(1)}) custom-call(bf16[64,1024]{1,0:T(8,128)(2,1)S(1)} %pick_rows.2.refs_3_.refs_0_, bf16[64,1024]{1,0:T(8,128)(2,1)S(1)} %collective-permute-done.refs_1_, bf16[64,1024]{1,0:T(8,128)(2,1)S(1)} %collective-permute-done.1.refs_2_, ...), custom_call_target="tpu_custom_call" | custom-call | tf_op jit(solution)/shard_map/project/pallas_call | solution.py:125
  22.9 8.5 %all-to-all-start = ((bf16[8,64,256]{2,1,0:T(8,128)(2,1)}), bf16[8,64,256]{2,1,0:T(8,128)(2,1)S(1)}, u32[]{:S(2)}, u32[]{:S(2)}) async-start(bf16[8,64,256]{2,1,0:T(8,128)(2,1)} %get-tuple-element.27), calls=%async_computation | async-start | bytes 524288 | tf_op jit(solution)/shard_map/all_to_all | solution.py:459
  31.3 3.0 %collective-permute-start.8 = (bf16[64,1024]{1,0:T(8,128)(2,1)S(1)}, bf16[64,1024]{1,0:T(8,128)(2,1)S(1)}, u32[]{:S(2)}, u32[]{:S(2)}) collective-permute-start(bf16[64,1024]{1,0:T(8,128)(2,1)S(1)} %get-tuple-element.30.refs_0_.refs_5_), channel_id=1, source_target_pairs={{0,24},{8,0},{16,8},{24,16},{1,25},{9,1},{17,9},{25,17},{2,26},{10... | collective-permute-start | bytes 393224 | tf_op jit(solution)/shard_map/ppermute | solution.py:463
  36.0 2.3 %collective-permute-done.8.refs_3_ = bf16[64,1024]{1,0:T(8,128)(2,1)S(1)} collective-permute-done((bf16[64,1024]{1,0:T(8,128)(2,1)S(1)}, bf16[64,1024]{1,0:T(8,128)(2,1)S(1)}, u32[]{:S(2)}, u32[]{:S(2)}) %collective-permute-start.8) | collective-permute-done | bytes 131104 | tf_op jit(solution)/shard_map/ppermute | solution.py:463
  38.3 2.6 %collective-permute-done.7.refs_2_ = bf16[64,1024]{1,0:T(8,128)(2,1)S(1)} collective-permute-done((bf16[64,1024]{1,0:T(8,128)(2,1)S(1)}, bf16[64,1024]{1,0:T(8,128)(2,1)S(1)}, u32[]{:S(2)}, u32[]{:S(2)}) %collective-permute-start.7) | collective-permute-done | bytes 131104 | tf_op jit(solution)/shard_map/ppermute | solution.py:463
  40.9 1.3 %collective-permute-done.6.refs_1_ = bf16[64,1024]{1,0:T(8,128)(2,1)S(1)} collective-permute-done((bf16[64,1024]{1,0:T(8,128)(2,1)S(1)}, bf16[64,1024]{1,0:T(8,128)(2,1)S(1)}, u32[]{:S(2)}, u32[]{:S(2)}) %collective-permute-start.6) | collective-permute-done | bytes 131104 | tf_op jit(solution)/shard_map/ppermute | solution.py:463
  44.3 1.8 %softmax_parts.1 = f32[4,2,512]{2,1,0:T(2,128)S(1)} custom-call(bf16[512,256]{1,0:T(8,128)(2,1)S(1)} %bitcast.3, bf16[64,1024]{1,0:T(8,128)(2,1)S(1)} %get-tuple-element.30.refs_0_.refs_5_, bf16[64,1024]{1,0:T(8,128)(2,1)S(1)} %collective-permute-done.6.refs_1_, bf16[64,1024]{1,0:T(8,128)(2,1)S(1)} %collective-permute-done.7.refs_2_, ...), custom_call_target="tpu_custom_call" | custom-call | tf_op jit(solution)/shard_map/softmax_parts/pallas_call | solution.py:380
  46.1 10.0 %all_to_all.15.parts_ref = f32[8,4,2,512]{3,2,1,0:T(2,128)S(1)} all-to-all(f32[8,4,2,512]{3,2,1,0:T(2,128)S(1)} %broadcast_in_dim.14), channel_id=1, replica_groups=mesh['z'=8,'y'=4,'core'=2,'tp'=4] {'y','core'}, dimensions={0} | all-to-all | bytes 262144 | tf_op jit(solution)/shard_map/all_to_all | solution.py:459
  57.0 4.4 %attention_parts.1 = (bf16[4,64,1024]{2,1,0:T(8,128)(2,1)S(1)}, bf16[4,64,1024]{2,1,0:T(8,128)(2,1)}, bf16[512,256]{1,0:T(8,128)(2,1)S(1)}) custom-call(bf16[512,256]{1,0:T(8,128)(2,1)S(1)} %bitcast.4, f32[8,4,2,512]{3,2,1,0:T(2,128)S(1)} %all_to_all.15.parts_ref, bf16[64,1024]{1,0:T(8,128)(2,1)S(1)} %get-tuple-element.30.refs_0_.refs_5_, ...), custom_call_target="tpu_custom_call" | custom-call | tf_op jit(solution)/shard_map/attention_parts/pallas_call | solution.py:443
  62.1 5.7 %all-to-all-start.2 = ((bf16[8,64,256]{2,1,0:T(8,128)(2,1)}), bf16[8,64,256]{2,1,0:T(8,128)(2,1)S(1)}, u32[]{:S(2)}, u32[]{:S(2)}) async-start(bf16[8,64,256]{2,1,0:T(8,128)(2,1)} %bitcast.5), calls=%async_computation.2 | async-start | bytes 524288 | tf_op jit(solution)/shard_map/all_to_all | solution.py:459
  67.9 1.8 %add_pieces.1 = (bf16[64,1024]{1,0:T(8,128)(2,1)S(1)}, bf16[64,1024]{1,0:T(8,128)(2,1)}, bf16[64,1024]{1,0:T(8,128)(2,1)}, bf16[64,1024]{1,0:T(8,128)(2,1)}) custom-call(bf16[4,64,1024]{2,1,0:T(8,128)(2,1)S(1)} %get-tuple-element.34.mine_ref, bf16[4,64,1024]{2,1,0:T(8,128)(2,1)} %collective-permute-done.13.received_ref), custom_call_target="tpu_custom_call" | custom-call | tf_op jit(solution)/shard_map/add_pieces/pallas_call | solution.py:143
  70.8 1.5 %collective-permute-start.15 = (bf16[64,1024]{1,0:T(8,128)(2,1)}, bf16[64,1024]{1,0:T(8,128)(2,1)S(1)}, u32[]{:S(2)}, u32[]{:S(2)}) collective-permute-start(bf16[64,1024]{1,0:T(8,128)(2,1)} %get-tuple-element.38), channel_id=1, source_target_pairs={{0,16},{8,24},{16,0},{24,8},{1,17},{9,25},{17,1},{25,9},{2,18},{10... | collective-permute-start | bytes 393224 | tf_op jit(solution)/shard_map/ppermute | solution.py:463
  72.3 8.1 %all-to-all-done.2.refs_5_.refs_4_ = bf16[8,64,256]{2,1,0:T(8,128)(2,1)S(1)} async-done(((bf16[8,64,256]{2,1,0:T(8,128)(2,1)}), bf16[8,64,256]{2,1,0:T(8,128)(2,1)S(1)}, u32[]{:S(2)}, u32[]{:S(2)}) %all-to-all-start.2) | async-done | bytes 262176 | tf_op jit(solution)/shard_map/all_to_all | solution.py:459
  80.7 2.2 %copy-done.1 = bf16[512,4096]{1,0:T(8,128)(2,1)S(1)} copy-done((bf16[512,4096]{1,0:T(8,128)(2,1)S(1)}, bf16[512,4096]{1,0:T(8,128)(2,1)}, u32[]{:S(2)}) %copy-start.1) | copy-done | bytes 4194328
  83.8 2.0 %collective-permute-start.17 = (bf16[64,1024]{1,0:T(8,128)(2,1)S(1)}, bf16[64,1024]{1,0:T(8,128)(2,1)S(1)}, u32[]{:S(2)}, u32[]{:S(2)}) collective-permute-start(bf16[64,1024]{1,0:T(8,128)(2,1)S(1)} %get-tuple-element.42), channel_id=1, source_target_pairs={{0,1},{1,2},{2,3},{3,0},{4,5},{5,6},{6,7},{7,4},{8,9},{9,10},{10,1... | collective-permute-start | bytes 393224 | tf_op jit(solution)/shard_map/ppermute | solution.py:463
  85.7 2.1 %collective-permute-start.18 = (bf16[64,1024]{1,0:T(8,128)(2,1)S(1)}, bf16[64,1024]{1,0:T(8,128)(2,1)S(1)}, u32[]{:S(2)}, u32[]{:S(2)}) collective-permute-start(bf16[64,1024]{1,0:T(8,128)(2,1)S(1)} %get-tuple-element.43), channel_id=1, source_target_pairs={{0,2},{1,3},{2,0},{3,1},{4,6},{5,7},{6,4},{7,5},{8,10},{9,11},{10,... | collective-permute-start | bytes 393224 | tf_op jit(solution)/shard_map/ppermute | solution.py:463
  87.8 2.0 %collective-permute-start.19 = (bf16[64,1024]{1,0:T(8,128)(2,1)S(1)}, bf16[64,1024]{1,0:T(8,128)(2,1)S(1)}, u32[]{:S(2)}, u32[]{:S(2)}) collective-permute-start(bf16[64,1024]{1,0:T(8,128)(2,1)S(1)} %get-tuple-element.44), channel_id=1, source_target_pairs={{0,3},{1,0},{2,1},{3,2},{4,7},{5,4},{6,5},{7,6},{8,11},{9,8},{10,9... | collective-permute-start | bytes 393224 | tf_op jit(solution)/shard_map/ppermute | solution.py:463
  89.9 2.2 %hidden_share.1 = (bf16[64,1152]{1,0:T(8,128)(2,1)S(1)}, bf16[64,1152]{1,0:T(8,128)(2,1)S(1)}, bf16[64,1152]{1,0:T(8,128)(2,1)S(1)}, bf16[64,1152]{1,0:T(8,128)(2,1)S(1)}) custom-call(bf16[64,1024]{1,0:T(8,128)(2,1)S(1)} %get-tuple-element.45.total_ref, bf16[64,1024]{1,0:T(8,128)(2,1)S(1)} %pick_rows.2.refs_3_.refs_0_, bf16[64,1024]{1,0:T(8,128)(2,1)S(1)} %copy-done.20, ...), custom_call_target="tpu_custom_call" | custom-call | flops 20000000000 | bytes 67108864 | tf_op jit(solution)/shard_map/hidden_share/pallas_call | solution.py:234
  92.4 2.6 %collective-permute-start.21 = (bf16[64,1152]{1,0:T(8,128)(2,1)S(1)}, bf16[64,1152]{1,0:T(8,128)(2,1)S(1)}, u32[]{:S(2)}, u32[]{:S(2)}) collective-permute-start(bf16[64,1152]{1,0:T(8,128)(2,1)S(1)} %get-tuple-element.48), channel_id=1, source_target_pairs={{0,2},{1,3},{2,0},{3,1},{4,6},{5,7},{6,4},{7,5},{8,10},{9,11},{10,... | collective-permute-start | bytes 442376 | tf_op jit(solution)/shard_map/ppermute | solution.py:463
  95.1 1.7 %put_mixed.1 = bf16[1024,1024]{1,0:T(8,128)(2,1)} custom-call(s32[1,64]{1,0:T(1,128)S(1)} %bitcast.8, bf16[1024,1024]{1,0:T(8,128)(2,1)S(1)} %copy-done.9, bf16[64,1024]{1,0:T(8,128)(2,1)S(1)} %pick_rows.2.refs_3_.refs_0_, f32[64,128]{1,0:T(8,128)S(1)} %copy-done.25, bf16[64,1024]{1,0:T(8,128)(2,1)S(1)} %get-tuple-element.41.refs_2_, ...), custom_call_target="tpu_custom_call" | custom-call | flops 3000000000 | bytes 8388608 | tf_op jit(solution)/shard_map/put_mixed/pallas_call | solution.py:272
  96.8 2.0 %collective-permute-done.20.refs_5_ = bf16[64,1152]{1,0:T(8,128)(2,1)S(1)} collective-permute-done((bf16[64,1152]{1,0:T(8,128)(2,1)S(1)}, bf16[64,1152]{1,0:T(8,128)(2,1)S(1)}, u32[]{:S(2)}, u32[]{:S(2)}) %collective-permute-start.20) | collective-permute-done | bytes 147488 | tf_op jit(solution)/shard_map/ppermute | solution.py:463
  98.8 1.6 %collective-permute-done.21.refs_6_ = bf16[64,1152]{1,0:T(8,128)(2,1)S(1)} collective-permute-done((bf16[64,1152]{1,0:T(8,128)(2,1)S(1)}, bf16[64,1152]{1,0:T(8,128)(2,1)S(1)}, u32[]{:S(2)}, u32[]{:S(2)}) %collective-permute-start.21) | collective-permute-done | bytes 147488 | tf_op jit(solution)/shard_map/ppermute | solution.py:463
  100.4 1.5 %collective-permute-done.22.refs_7_ = bf16[64,1152]{1,0:T(8,128)(2,1)S(1)} collective-permute-done((bf16[64,1152]{1,0:T(8,128)(2,1)S(1)}, bf16[64,1152]{1,0:T(8,128)(2,1)S(1)}, u32[]{:S(2)}, u32[]{:S(2)}) %collective-permute-start.22) | collective-permute-done | bytes 147488 | tf_op jit(solution)/shard_map/ppermute | solution.py:463
  102.0 1.8 %put_grad.1 = bf16[1024,1024]{1,0:T(8,128)(2,1)} custom-call(s32[1,64]{1,0:T(1,128)S(1)} %bitcast.9, bf16[1024,1024]{1,0:T(8,128)(2,1)S(1)} %copy-done.11, bf16[64,1024]{1,0:T(8,128)(2,1)S(1)} %pick_rows.2.refs_3_.refs_0_, bf16[64,1024]{1,0:T(8,128)(2,1)S(1)} %pick_rows.3.refs_4_.refs_1_, f32[64,128]{1,0:T(8,128)S(1)} %copy-done.25, ...), custom_call_target="tpu_custom_call" | custom-call | flops 3000000000 | bytes 8388608 | tf_op jit(solution)/shard_map/put_grad/pallas_call | solution.py:272
  (86 shorter events, 12.6 us)
Async XLA Ops:
  2.9 10.9 %copy-start = (bf16[512,4096]{1,0:T(8,128)(2,1)S(1)}, bf16[512,4096]{1,0:T(8,128)(2,1)}, u32[]{:S(2)}) copy-start(bf16[512,4096]{1,0:T(8,128)(2,1)} %refs_4_.1) | copy-start | bytes 12582916
  3.5 10.3 %collective-permute-start.4 = (bf16[64,1024]{1,0:T(8,128)(2,1)S(1)}, bf16[64,1024]{1,0:T(8,128)(2,1)S(1)}, u32[]{:S(2)}, u32[]{:S(2)}) collective-permute-start(bf16[64,1024]{1,0:T(8,128)(2,1)S(1)} %pick_rows.3.refs_4_.refs_1_), channel_id=1, source_target_pairs={{0,3},{1,0},{2,1},{3,2},{4,7},{5,4},{6,5},{7,6},{8,11},{9,8},{10,9... | collective-permute-start | bytes 393224 | tf_op jit(solution)/shard_map/ppermute | solution.py:463
  5.8 10.5 %collective-permute-start.3 = (bf16[64,1024]{1,0:T(8,128)(2,1)S(1)}, bf16[64,1024]{1,0:T(8,128)(2,1)S(1)}, u32[]{:S(2)}, u32[]{:S(2)}) collective-permute-start(bf16[64,1024]{1,0:T(8,128)(2,1)S(1)} %pick_rows.3.refs_4_.refs_1_), channel_id=1, source_target_pairs={{0,1},{1,2},{2,3},{3,0},{4,5},{5,6},{6,7},{7,4},{8,9},{9,10},{10,1... | collective-permute-start | bytes 393224 | tf_op jit(solution)/shard_map/ppermute | solution.py:463
  7.4 6.4 %copy-start.26 = (bf16[4096]{0:T(1024)(128)(2,1)S(1)}, bf16[4096]{0:T(1024)(128)(2,1)}, u32[]{:S(2)}) copy-start(bf16[4096]{0:T(1024)(128)(2,1)} %param.10) | copy-start | bytes 24580
  8.0 8.3 %collective-permute-start.2 = (bf16[64,1024]{1,0:T(8,128)(2,1)S(1)}, bf16[64,1024]{1,0:T(8,128)(2,1)S(1)}, u32[]{:S(2)}, u32[]{:S(2)}) collective-permute-start(bf16[64,1024]{1,0:T(8,128)(2,1)S(1)} %pick_rows.2.refs_3_.refs_0_), channel_id=1, source_target_pairs={{0,3},{1,0},{2,1},{3,2},{4,7},{5,4},{6,5},{7,6},{8,11},{9,8},{10,9... | collective-permute-start | bytes 393224 | tf_op jit(solution)/shard_map/ppermute | solution.py:463
  10.1 8.2 %collective-permute-start.1 = (bf16[64,1024]{1,0:T(8,128)(2,1)S(1)}, bf16[64,1024]{1,0:T(8,128)(2,1)S(1)}, u32[]{:S(2)}, u32[]{:S(2)}) collective-permute-start(bf16[64,1024]{1,0:T(8,128)(2,1)S(1)} %pick_rows.2.refs_3_.refs_0_), channel_id=1, source_target_pairs={{0,2},{1,3},{2,0},{3,1},{4,6},{5,7},{6,4},{7,5},{8,10},{9,11},{10,... | collective-permute-start | bytes 393224 | tf_op jit(solution)/shard_map/ppermute | solution.py:463
  11.2 7.1 %collective-permute-start = (bf16[64,1024]{1,0:T(8,128)(2,1)S(1)}, bf16[64,1024]{1,0:T(8,128)(2,1)S(1)}, u32[]{:S(2)}, u32[]{:S(2)}) collective-permute-start(bf16[64,1024]{1,0:T(8,128)(2,1)S(1)} %pick_rows.2.refs_3_.refs_0_), channel_id=1, source_target_pairs={{0,1},{1,2},{2,3},{3,0},{4,5},{5,6},{6,7},{7,4},{8,9},{9,10},{10,1... | collective-permute-start | bytes 393224 | tf_op jit(solution)/shard_map/ppermute | solution.py:463
  13.8 5.5 %collective-permute-start.5 = (bf16[64,1024]{1,0:T(8,128)(2,1)S(1)}, bf16[64,1024]{1,0:T(8,128)(2,1)S(1)}, u32[]{:S(2)}, u32[]{:S(2)}) collective-permute-start(bf16[64,1024]{1,0:T(8,128)(2,1)S(1)} %collective-permute-done.4.refs_7_), channel_id=1, source_target_pairs={{0,3},{1,0},{2,1},{3,2},{4,7},{5,4},{6,5},{7,6},{8,11},{9,8},{10,9... | collective-permute-start | bytes 393224 | tf_op jit(solution)/shard_map/ppermute | solution.py:463
  22.9 19.4 %all-to-all-start = ((bf16[8,64,256]{2,1,0:T(8,128)(2,1)}), bf16[8,64,256]{2,1,0:T(8,128)(2,1)S(1)}, u32[]{:S(2)}, u32[]{:S(2)}) async-start(bf16[8,64,256]{2,1,0:T(8,128)(2,1)} %get-tuple-element.27), calls=%async_computation | async-start | bytes 524288 | tf_op jit(solution)/shard_map/all_to_all | solution.py:459
  31.3 6.9 %collective-permute-start.8 = (bf16[64,1024]{1,0:T(8,128)(2,1)S(1)}, bf16[64,1024]{1,0:T(8,128)(2,1)S(1)}, u32[]{:S(2)}, u32[]{:S(2)}) collective-permute-start(bf16[64,1024]{1,0:T(8,128)(2,1)S(1)} %get-tuple-element.30.refs_0_.refs_5_), channel_id=1, source_target_pairs={{0,24},{8,0},{16,8},{24,16},{1,25},{9,1},{17,9},{25,17},{2,26},{10... | collective-permute-start | bytes 393224 | tf_op jit(solution)/shard_map/ppermute | solution.py:463
  34.4 6.6 %collective-permute-start.7 = (bf16[64,1024]{1,0:T(8,128)(2,1)S(1)}, bf16[64,1024]{1,0:T(8,128)(2,1)S(1)}, u32[]{:S(2)}, u32[]{:S(2)}) collective-permute-start(bf16[64,1024]{1,0:T(8,128)(2,1)S(1)} %get-tuple-element.30.refs_0_.refs_5_), channel_id=1, source_target_pairs={{0,16},{8,24},{16,0},{24,8},{1,17},{9,25},{17,1},{25,9},{2,18},{10... | collective-permute-start | bytes 393224 | tf_op jit(solution)/shard_map/ppermute | solution.py:463
  35.0 7.2 %collective-permute-start.6 = (bf16[64,1024]{1,0:T(8,128)(2,1)S(1)}, bf16[64,1024]{1,0:T(8,128)(2,1)S(1)}, u32[]{:S(2)}, u32[]{:S(2)}) collective-permute-start(bf16[64,1024]{1,0:T(8,128)(2,1)S(1)} %get-tuple-element.30.refs_0_.refs_5_), channel_id=1, source_target_pairs={{0,8},{8,16},{16,24},{24,0},{1,9},{9,17},{17,25},{25,1},{2,10},{10... | collective-permute-start | bytes 393224 | tf_op jit(solution)/shard_map/ppermute | solution.py:463
  42.2 1.3 %collective-permute-start.10 = (bf16[64,1024]{1,0:T(8,128)(2,1)S(1)}, bf16[64,1024]{1,0:T(8,128)(2,1)S(1)}, u32[]{:S(2)}, u32[]{:S(2)}) collective-permute-start(bf16[64,1024]{1,0:T(8,128)(2,1)S(1)} %collective-permute-done.6.refs_1_), channel_id=1, source_target_pairs={{0,4},{4,0},{1,5},{5,1},{2,6},{6,2},{3,7},{7,3},{8,12},{12,8},{9,1... | collective-permute-start | bytes 393224 | tf_op jit(solution)/shard_map/ppermute | solution.py:463
  42.2 1.5 %collective-permute-start.11 = (bf16[64,1024]{1,0:T(8,128)(2,1)S(1)}, bf16[64,1024]{1,0:T(8,128)(2,1)S(1)}, u32[]{:S(2)}, u32[]{:S(2)}) collective-permute-start(bf16[64,1024]{1,0:T(8,128)(2,1)S(1)} %collective-permute-done.7.refs_2_), channel_id=1, source_target_pairs={{0,4},{4,0},{1,5},{5,1},{2,6},{6,2},{3,7},{7,3},{8,12},{12,8},{9,1... | collective-permute-start | bytes 393224 | tf_op jit(solution)/shard_map/ppermute | solution.py:463
  42.7 1.3 %collective-permute-start.12 = (bf16[64,1024]{1,0:T(8,128)(2,1)S(1)}, bf16[64,1024]{1,0:T(8,128)(2,1)S(1)}, u32[]{:S(2)}, u32[]{:S(2)}) collective-permute-start(bf16[64,1024]{1,0:T(8,128)(2,1)S(1)} %collective-permute-done.8.refs_3_), channel_id=1, source_target_pairs={{0,4},{4,0},{1,5},{5,1},{2,6},{6,2},{3,7},{7,3},{8,12},{12,8},{9,1... | collective-permute-start | bytes 393224 | tf_op jit(solution)/shard_map/ppermute | solution.py:463
  42.8 1.4 %collective-permute-start.9 = (bf16[64,1024]{1,0:T(8,128)(2,1)S(1)}, bf16[64,1024]{1,0:T(8,128)(2,1)S(1)}, u32[]{:S(2)}, u32[]{:S(2)}) collective-permute-start(bf16[64,1024]{1,0:T(8,128)(2,1)S(1)} %get-tuple-element.30.refs_0_.refs_5_), channel_id=1, source_target_pairs={{0,4},{4,0},{1,5},{5,1},{2,6},{6,2},{3,7},{7,3},{8,12},{12,8},{9,1... | collective-permute-start | bytes 393224 | tf_op jit(solution)/shard_map/ppermute | solution.py:463
  62.1 5.7 %collective-permute-start.13 = (bf16[4,64,1024]{2,1,0:T(8,128)(2,1)}, bf16[4,64,1024]{2,1,0:T(8,128)(2,1)}, u32[]{:S(2)}, u32[]{:S(2)}) collective-permute-start(bf16[4,64,1024]{2,1,0:T(8,128)(2,1)} %get-tuple-element.35), channel_id=1, source_target_pairs={{0,4},{4,0},{1,5},{5,1},{2,6},{6,2},{3,7},{7,3},{8,12},{12,8},{9,1... | collective-permute-start | bytes 1572872 | tf_op jit(solution)/shard_map/ppermute | solution.py:463
  62.1 18.3 %all-to-all-start.2 = ((bf16[8,64,256]{2,1,0:T(8,128)(2,1)}), bf16[8,64,256]{2,1,0:T(8,128)(2,1)S(1)}, u32[]{:S(2)}, u32[]{:S(2)}) async-start(bf16[8,64,256]{2,1,0:T(8,128)(2,1)} %bitcast.5), calls=%async_computation.2 | async-start | bytes 524288 | tf_op jit(solution)/shard_map/all_to_all | solution.py:459
  69.7 10.7 %collective-permute-start.14 = (bf16[64,1024]{1,0:T(8,128)(2,1)}, bf16[64,1024]{1,0:T(8,128)(2,1)S(1)}, u32[]{:S(2)}, u32[]{:S(2)}) collective-permute-start(bf16[64,1024]{1,0:T(8,128)(2,1)} %get-tuple-element.37), channel_id=1, source_target_pairs={{0,24},{8,0},{16,8},{24,16},{1,25},{9,1},{17,9},{25,17},{2,26},{10... | collective-permute-start | bytes 393224 | tf_op jit(solution)/shard_map/ppermute | solution.py:463
  70.8 9.6 %collective-permute-start.15 = (bf16[64,1024]{1,0:T(8,128)(2,1)}, bf16[64,1024]{1,0:T(8,128)(2,1)S(1)}, u32[]{:S(2)}, u32[]{:S(2)}) collective-permute-start(bf16[64,1024]{1,0:T(8,128)(2,1)} %get-tuple-element.38), channel_id=1, source_target_pairs={{0,16},{8,24},{16,0},{24,8},{1,17},{9,25},{17,1},{25,9},{2,18},{10... | collective-permute-start | bytes 393224 | tf_op jit(solution)/shard_map/ppermute | solution.py:463
  72.3 8.4 %collective-permute-start.16 = (bf16[64,1024]{1,0:T(8,128)(2,1)}, bf16[64,1024]{1,0:T(8,128)(2,1)S(1)}, u32[]{:S(2)}, u32[]{:S(2)}) collective-permute-start(bf16[64,1024]{1,0:T(8,128)(2,1)} %get-tuple-element.39), channel_id=1, source_target_pairs={{0,8},{8,16},{16,24},{24,0},{1,9},{9,17},{17,25},{25,1},{2,10},{10... | collective-permute-start | bytes 393224 | tf_op jit(solution)/shard_map/ppermute | solution.py:463
  82.9 7.0 %copy-start.3 = (bf16[4096,512]{1,0:T(8,128)(2,1)S(1)}, bf16[4096,512]{1,0:T(8,128)(2,1)}, u32[]{:S(2)}) copy-start(bf16[4096,512]{1,0:T(8,128)(2,1)} %refs_6_.1) | copy-start | bytes 12582916
  82.9 7.0 %copy-start.16 = (bf16[64,1024]{1,0:T(8,128)(2,1)S(1)}, bf16[64,1024]{1,0:T(8,128)(2,1)}, u32[]{:S(2)}) copy-start(bf16[64,1024]{1,0:T(8,128)(2,1)} %copy-done.15) | copy-start | bytes 393220
  82.9 7.0 %copy-start.18 = (bf16[64,1024]{1,0:T(8,128)(2,1)S(1)}, bf16[64,1024]{1,0:T(8,128)(2,1)}, u32[]{:S(2)}) copy-start(bf16[64,1024]{1,0:T(8,128)(2,1)} %copy-done.17) | copy-start | bytes 393220
  82.9 7.0 %copy-start.20 = (bf16[64,1024]{1,0:T(8,128)(2,1)S(1)}, bf16[64,1024]{1,0:T(8,128)(2,1)}, u32[]{:S(2)}) copy-start(bf16[64,1024]{1,0:T(8,128)(2,1)} %copy-done.19) | copy-start | bytes 393220
  83.8 11.3 %collective-permute-start.17 = (bf16[64,1024]{1,0:T(8,128)(2,1)S(1)}, bf16[64,1024]{1,0:T(8,128)(2,1)S(1)}, u32[]{:S(2)}, u32[]{:S(2)}) collective-permute-start(bf16[64,1024]{1,0:T(8,128)(2,1)S(1)} %get-tuple-element.42), channel_id=1, source_target_pairs={{0,1},{1,2},{2,3},{3,0},{4,5},{5,6},{6,7},{7,4},{8,9},{9,10},{10,1... | collective-permute-start | bytes 393224 | tf_op jit(solution)/shard_map/ppermute | solution.py:463
  85.7 9.3 %collective-permute-start.18 = (bf16[64,1024]{1,0:T(8,128)(2,1)S(1)}, bf16[64,1024]{1,0:T(8,128)(2,1)S(1)}, u32[]{:S(2)}, u32[]{:S(2)}) collective-permute-start(bf16[64,1024]{1,0:T(8,128)(2,1)S(1)} %get-tuple-element.43), channel_id=1, source_target_pairs={{0,2},{1,3},{2,0},{3,1},{4,6},{5,7},{6,4},{7,5},{8,10},{9,11},{10,... | collective-permute-start | bytes 393224 | tf_op jit(solution)/shard_map/ppermute | solution.py:463
  87.8 7.2 %collective-permute-start.19 = (bf16[64,1024]{1,0:T(8,128)(2,1)S(1)}, bf16[64,1024]{1,0:T(8,128)(2,1)S(1)}, u32[]{:S(2)}, u32[]{:S(2)}) collective-permute-start(bf16[64,1024]{1,0:T(8,128)(2,1)S(1)} %get-tuple-element.44), channel_id=1, source_target_pairs={{0,3},{1,0},{2,1},{3,2},{4,7},{5,4},{6,5},{7,6},{8,11},{9,8},{10,9... | collective-permute-start | bytes 393224 | tf_op jit(solution)/shard_map/ppermute | solution.py:463
  92.1 6.7 %collective-permute-start.20 = (bf16[64,1152]{1,0:T(8,128)(2,1)S(1)}, bf16[64,1152]{1,0:T(8,128)(2,1)S(1)}, u32[]{:S(2)}, u32[]{:S(2)}) collective-permute-start(bf16[64,1152]{1,0:T(8,128)(2,1)S(1)} %get-tuple-element.47), channel_id=1, source_target_pairs={{0,1},{1,2},{2,3},{3,0},{4,5},{5,6},{6,7},{7,4},{8,9},{9,10},{10,1... | collective-permute-start | bytes 442376 | tf_op jit(solution)/shard_map/ppermute | solution.py:463
  92.4 8.0 %collective-permute-start.21 = (bf16[64,1152]{1,0:T(8,128)(2,1)S(1)}, bf16[64,1152]{1,0:T(8,128)(2,1)S(1)}, u32[]{:S(2)}, u32[]{:S(2)}) collective-permute-start(bf16[64,1152]{1,0:T(8,128)(2,1)S(1)} %get-tuple-element.48), channel_id=1, source_target_pairs={{0,2},{1,3},{2,0},{3,1},{4,6},{5,7},{6,4},{7,5},{8,10},{9,11},{10,... | collective-permute-start | bytes 442376 | tf_op jit(solution)/shard_map/ppermute | solution.py:463
  95.0 6.9 %collective-permute-start.22 = (bf16[64,1152]{1,0:T(8,128)(2,1)S(1)}, bf16[64,1152]{1,0:T(8,128)(2,1)S(1)}, u32[]{:S(2)}, u32[]{:S(2)}) collective-permute-start(bf16[64,1152]{1,0:T(8,128)(2,1)S(1)} %get-tuple-element.49), channel_id=1, source_target_pairs={{0,3},{1,0},{2,1},{3,2},{4,7},{5,4},{6,5},{7,6},{8,11},{9,8},{10,9... | collective-permute-start | bytes 442376 | tf_op jit(solution)/shard_map/ppermute | solution.py:463
  95.1 6.9 %copy-start.11 = (bf16[1024,1024]{1,0:T(8,128)(2,1)S(1)}, bf16[1024,1024]{1,0:T(8,128)(2,1)}, u32[]{:S(2)}) copy-start(bf16[1024,1024]{1,0:T(8,128)(2,1)} %base_ref.3) | copy-start | bytes 6291460
  (20 other events, 58.5 us)

commit v4 on v3

--- a/solution.py
+++ b/solution.py
@@ -188,7 +188,7 @@
         out_specs=[whole()] * (1 + parts),
         out_shape=[like((picked, both))] + [like((picked, part))] * parts,
         compiler_params=params(16),
-        cost_estimate=pl.CostEstimate(flops=10**9, bytes_accessed=2**22, transcendentals=0),
+        cost_estimate=pl.CostEstimate(flops=2 * 10**10, bytes_accessed=2**26, transcendentals=0),
         name="branch_share",
     )(*pieces, w_out, after)
 
@@ -500,7 +500,7 @@
     kv_grads = exchange(kv_grads.reshape(planes, picked, 2 * HEAD_DIM), "z")
     chip = add_pieces(mine, shifted(theirs, "core", cores, 1))
     pieces = [chip[0]] + [shifted(chip[s], "y", columns, columns - s) for s in range(1, columns)]
-    total, *branches = branch_share(pieces, w_out, parts_tp, kv_grads)
+    total, *branches = branch_share(pieces, w_out, parts_tp, chip[0])
     shares = hidden_share(total, kv_grads, inputs, own[0], w_query, w_key, w_value)
     branches = around_tp(branches, parts_tp)
     shares = around_tp(shares, parts_tp)

time: 105 us -> 104 us (level)
  waiting for transfers between devices: 23.9 us -> 19 us
  local copies, waits for them, and re-layouts: 10.8 us -> 13.6 us
  Pallas kernels: 18.6 us -> 19.9 us
    all_to_all x2, waiting for transfers between devices: 8.1 us -> 0.01 us  [exchange(): return lax.all_to_all(array, axis, 0, 0, tiled=True)]
    ppermute x23, waiting for transfers between devices: 15.8 us -> 19 us  [shifted(): lax.ppermute(array, axis, [(i, (i + step) % count) for i in range(count)])]
    unnamed x54 -> x42, local copies, waits for them, and re-layouts: 10.8 us -> 13.5 us
    pallas_call x1, Pallas kernels: 0.86 us -> 2.44 us  [branch_share(): pl.pallas_call(kernel, in_specs=[whole()] * (count + 1) + [far()], out_sp...]
    pallas_call x2, Pallas kernels: 3.53 us -> 4.7 us  [put_rows(): pl.pallas_call(kernel, in_specs=[whole()] * (2 + count), out_specs=far(),...]
  transfers between devices with their start and end apart: 25 -> 25, of which waited for: 14 -> 15; matrix products, arithmetic and copies ran while one was open for 0% -> 0% of each run, Pallas kernels for 6% -> 8%
where the time goes in v4:
time: 104 us; the launch traced here: 103 us
  starting transfers between devices  39.9 us (38%)
  Pallas kernels  19.9 us (19%)
  waiting for transfers between devices  19 us (18%)
  local copies, waits for them, and re-layouts  13.6 us (13%)
  blocking collectives  9.99 us (10%)
    ppermute x23, starting transfers between devices, shifted(): lax.ppermute(array, axis, [(i, (i + step) % count) for i in range(count)])  25.7 us
    ppermute x23, waiting for transfers between devices, shifted(): lax.ppermute(array, axis, [(i, (i + step) % count) for i in range(count)])  19 us
    all_to_all x2, starting transfers between devices, exchange(): return lax.all_to_all(array, axis, 0, 0, tiled=True)  14.2 us
    unnamed x42, local copies, waits for them, and re-layouts  13.5 us
    all_to_all x1, blocking collectives, exchange(): return lax.all_to_all(array, axis, 0, 0, tiled=True)  9.99 us
    pallas_call x2, Pallas kernels, put_rows(): pl.pallas_call(kernel, in_specs=[whole()] * (2 + count), out_specs=far(),...  4.7 us
    pallas_call x1, Pallas kernels, attention_parts(): pl.pallas_call(kernel, in_specs=[whole()] * (2 + 2 * n), out_specs=[whole...  3.93 us
    pallas_call x1, Pallas kernels, project(): pl.pallas_call(kernel, in_specs=[whole()] * len(ins) + [far()], out_specs...  2.94 us
  transfers between devices with their start and end apart: 25, of which 15 were waited for; matrix products, arithmetic and copies ran while one was open for 0% of the time, Pallas kernels for 8%

profile of v4, /device:TPU:2, one launch (start us, length us, event | category | flops | bytes accessed | tf_op | source)
XLA Modules:
  0.0 103.4 jit_solution(12712119365131771193)
XLA Ops:
  0.6 1.6 %copy-done.10 = bf16[1024,1024]{1,0:T(8,128)(2,1)S(1)} copy-done((bf16[1024,1024]{1,0:T(8,128)(2,1)S(1)}, bf16[1024,1024]{1,0:T(8,128)(2,1)}, u32[]{:S(2)}) %copy-start.10) | copy-done | bytes 2097176
  3.4 2.3 %collective-permute-start.4 = (bf16[64,1024]{1,0:T(8,128)(2,1)S(1)}, bf16[64,1024]{1,0:T(8,128)(2,1)S(1)}, u32[]{:S(2)}, u32[]{:S(2)}) collective-permute-start(bf16[64,1024]{1,0:T(8,128)(2,1)S(1)} %pick_rows.3.refs_4_.refs_1_), channel_id=1, source_target_pairs={{0,3},{1,0},{2,1},{3,2},{4,7},{5,4},{6,5},{7,6},{8,11},{9,8},{10,9... | collective-permute-start | bytes 393224 | tf_op jit(solution)/shard_map/ppermute | solution.py:463
  5.8 1.6 %copy-done.8 = bf16[1024,1024]{1,0:T(8,128)(2,1)S(1)} copy-done((bf16[1024,1024]{1,0:T(8,128)(2,1)S(1)}, bf16[1024,1024]{1,0:T(8,128)(2,1)}, u32[]{:S(2)}) %copy-start.8) | copy-done | bytes 2097176
  7.9 2.1 %collective-permute-start.2 = (bf16[64,1024]{1,0:T(8,128)(2,1)S(1)}, bf16[64,1024]{1,0:T(8,128)(2,1)S(1)}, u32[]{:S(2)}, u32[]{:S(2)}) collective-permute-start(bf16[64,1024]{1,0:T(8,128)(2,1)S(1)} %pick_rows.2.refs_3_.refs_0_), channel_id=1, source_target_pairs={{0,3},{1,0},{2,1},{3,2},{4,7},{5,4},{6,5},{7,6},{8,11},{9,8},{10,9... | collective-permute-start | bytes 393224 | tf_op jit(solution)/shard_map/ppermute | solution.py:463
  11.2 2.5 %collective-permute-start = (bf16[64,1024]{1,0:T(8,128)(2,1)S(1)}, bf16[64,1024]{1,0:T(8,128)(2,1)S(1)}, u32[]{:S(2)}, u32[]{:S(2)}) collective-permute-start(bf16[64,1024]{1,0:T(8,128)(2,1)S(1)} %pick_rows.2.refs_3_.refs_0_), channel_id=1, source_target_pairs={{0,1},{1,2},{2,3},{3,0},{4,5},{5,6},{6,7},{7,4},{8,9},{9,10},{10,1... | collective-permute-start | bytes 393224 | tf_op jit(solution)/shard_map/ppermute | solution.py:463
  15.0 1.2 %copy-done.6 = bf16[4096,128]{1,0:T(8,128)(2,1)S(1)} copy-done((bf16[4096,128]{1,0:T(8,128)(2,1)S(1)}, bf16[4096,128]{1,0:T(8,128)(2,1)}, u32[]{:S(2)}) %copy-start.6) | copy-done | bytes 1048600
  16.3 2.0 %collective-permute-done.1.refs_2_ = bf16[64,1024]{1,0:T(8,128)(2,1)S(1)} collective-permute-done((bf16[64,1024]{1,0:T(8,128)(2,1)S(1)}, bf16[64,1024]{1,0:T(8,128)(2,1)S(1)}, u32[]{:S(2)}, u32[]{:S(2)}) %collective-permute-start.1) | collective-permute-done | bytes 131104 | tf_op jit(solution)/shard_map/ppermute | solution.py:463
  19.3 2.9 %project.1 = (bf16[8,64,256]{2,1,0:T(8,128)(2,1)}, bf16[64,1024]{1,0:T(8,128)(2,1)S(1)}, f32[64,128]{1,0:T(8,128)S(1)}) custom-call(bf16[64,1024]{1,0:T(8,128)(2,1)S(1)} %pick_rows.2.refs_3_.refs_0_, bf16[64,1024]{1,0:T(8,128)(2,1)S(1)} %collective-permute-done.refs_1_, bf16[64,1024]{1,0:T(8,128)(2,1)S(1)} %collective-permute-done.1.refs_2_, ...), custom_call_target="tpu_custom_call" | custom-call | tf_op jit(solution)/shard_map/project/pallas_call | solution.py:125
  22.8 8.5 %all-to-all-start = ((bf16[8,64,256]{2,1,0:T(8,128)(2,1)}), bf16[8,64,256]{2,1,0:T(8,128)(2,1)S(1)}, u32[]{:S(2)}, u32[]{:S(2)}) async-start(bf16[8,64,256]{2,1,0:T(8,128)(2,1)} %get-tuple-element.27), calls=%async_computation | async-start | bytes 524288 | tf_op jit(solution)/shard_map/all_to_all | solution.py:459
  31.3 3.0 %collective-permute-start.8 = (bf16[64,1024]{1,0:T(8,128)(2,1)S(1)}, bf16[64,1024]{1,0:T(8,128)(2,1)S(1)}, u32[]{:S(2)}, u32[]{:S(2)}) collective-permute-start(bf16[64,1024]{1,0:T(8,128)(2,1)S(1)} %get-tuple-element.30.refs_0_.refs_5_), channel_id=1, source_target_pairs={{0,24},{8,0},{16,8},{24,16},{1,25},{9,1},{17,9},{25,17},{2,26},{10... | collective-permute-start | bytes 393224 | tf_op jit(solution)/shard_map/ppermute | solution.py:463
  35.9 2.3 %collective-permute-done.8.refs_3_ = bf16[64,1024]{1,0:T(8,128)(2,1)S(1)} collective-permute-done((bf16[64,1024]{1,0:T(8,128)(2,1)S(1)}, bf16[64,1024]{1,0:T(8,128)(2,1)S(1)}, u32[]{:S(2)}, u32[]{:S(2)}) %collective-permute-start.8) | collective-permute-done | bytes 131104 | tf_op jit(solution)/shard_map/ppermute | solution.py:463
  38.2 2.7 %collective-permute-done.7.refs_2_ = bf16[64,1024]{1,0:T(8,128)(2,1)S(1)} collective-permute-done((bf16[64,1024]{1,0:T(8,128)(2,1)S(1)}, bf16[64,1024]{1,0:T(8,128)(2,1)S(1)}, u32[]{:S(2)}, u32[]{:S(2)}) %collective-permute-start.7) | collective-permute-done | bytes 131104 | tf_op jit(solution)/shard_map/ppermute | solution.py:463
  40.9 1.3 %collective-permute-done.6.refs_1_ = bf16[64,1024]{1,0:T(8,128)(2,1)S(1)} collective-permute-done((bf16[64,1024]{1,0:T(8,128)(2,1)S(1)}, bf16[64,1024]{1,0:T(8,128)(2,1)S(1)}, u32[]{:S(2)}, u32[]{:S(2)}) %collective-permute-start.6) | collective-permute-done | bytes 131104 | tf_op jit(solution)/shard_map/ppermute | solution.py:463
  44.2 1.8 %softmax_parts.1 = f32[4,2,512]{2,1,0:T(2,128)S(1)} custom-call(bf16[512,256]{1,0:T(8,128)(2,1)S(1)} %bitcast.3, bf16[64,1024]{1,0:T(8,128)(2,1)S(1)} %get-tuple-element.30.refs_0_.refs_5_, bf16[64,1024]{1,0:T(8,128)(2,1)S(1)} %collective-permute-done.6.refs_1_, bf16[64,1024]{1,0:T(8,128)(2,1)S(1)} %collective-permute-done.7.refs_2_, ...), custom_call_target="tpu_custom_call" | custom-call | tf_op jit(solution)/shard_map/softmax_parts/pallas_call | solution.py:380
  46.1 10.0 %all_to_all.15.parts_ref = f32[8,4,2,512]{3,2,1,0:T(2,128)S(1)} all-to-all(f32[8,4,2,512]{3,2,1,0:T(2,128)S(1)} %broadcast_in_dim.14), channel_id=1, replica_groups=mesh['z'=8,'y'=4,'core'=2,'tp'=4] {'y','core'}, dimensions={0} | all-to-all | bytes 262144 | tf_op jit(solution)/shard_map/all_to_all | solution.py:459
  56.1 3.9 %attention_parts.1 = (bf16[4,64,1024]{2,1,0:T(8,128)(2,1)S(1)}, bf16[4,64,1024]{2,1,0:T(8,128)(2,1)S(1)}, bf16[512,256]{1,0:T(8,128)(2,1)}) custom-call(bf16[512,256]{1,0:T(8,128)(2,1)S(1)} %bitcast.4, f32[8,4,2,512]{3,2,1,0:T(2,128)S(1)} %all_to_all.15.parts_ref, bf16[64,1024]{1,0:T(8,128)(2,1)S(1)} %get-tuple-element.30.refs_0_.refs_5_, ...), custom_call_target="tpu_custom_call" | custom-call | tf_op jit(solution)/shard_map/attention_parts/pallas_call | solution.py:443
  60.0 1.9 %collective-permute-done.13.received_ref = bf16[4,64,1024]{2,1,0:T(8,128)(2,1)S(1)} collective-permute-done((bf16[4,64,1024]{2,1,0:T(8,128)(2,1)S(1)}, bf16[4,64,1024]{2,1,0:T(8,128)(2,1)S(1)}, u32[]{:S(2)}, u32[]{:S(2)}) %collective-permute-start.13) | collective-permute-done | bytes 524320 | tf_op jit(solution)/shard_map/ppermute | solution.py:463
  63.9 1.5 %collective-permute-start.15 = (bf16[64,1024]{1,0:T(8,128)(2,1)}, bf16[64,1024]{1,0:T(8,128)(2,1)S(1)}, u32[]{:S(2)}, u32[]{:S(2)}) collective-permute-start(bf16[64,1024]{1,0:T(8,128)(2,1)} %get-tuple-element.38), channel_id=1, source_target_pairs={{0,16},{8,24},{16,0},{24,8},{1,17},{9,25},{17,1},{25,9},{2,18},{10... | collective-permute-start | bytes 393224 | tf_op jit(solution)/shard_map/ppermute | solution.py:463
  65.4 5.7 %all-to-all-start.2 = ((bf16[8,64,256]{2,1,0:T(8,128)(2,1)}), bf16[8,64,256]{2,1,0:T(8,128)(2,1)S(1)}, u32[]{:S(2)}, u32[]{:S(2)}) async-start(bf16[8,64,256]{2,1,0:T(8,128)(2,1)} %bitcast.2), calls=%async_computation.2 | async-start | bytes 524288 | tf_op jit(solution)/shard_map/all_to_all | solution.py:459
  72.0 1.8 %collective-permute-done.16.refs_3_ = bf16[64,1024]{1,0:T(8,128)(2,1)} collective-permute-done((bf16[64,1024]{1,0:T(8,128)(2,1)}, bf16[64,1024]{1,0:T(8,128)(2,1)}, u32[]{:S(2)}, u32[]{:S(2)}) %collective-permute-start.16) | collective-permute-done | bytes 131104 | tf_op jit(solution)/shard_map/ppermute | solution.py:463
  73.8 2.2 %copy-done.1 = bf16[512,4096]{1,0:T(8,128)(2,1)S(1)} copy-done((bf16[512,4096]{1,0:T(8,128)(2,1)S(1)}, bf16[512,4096]{1,0:T(8,128)(2,1)}, u32[]{:S(2)}) %copy-start.1) | copy-done | bytes 4194328
  76.0 2.4 %branch_share.1 = (bf16[64,1024]{1,0:T(8,128)(2,1)S(1)}, bf16[64,1024]{1,0:T(8,128)(2,1)S(1)}, bf16[64,1024]{1,0:T(8,128)(2,1)}, bf16[64,1024]{1,0:T(8,128)(2,1)}, bf16[64,1024]{1,0:T(8,128)(2,1)}) custom-call(bf16[64,1024]{1,0:T(8,128)(2,1)S(1)} %get-tuple-element.36.refs_0_.refs_5_, bf16[64,1024]{1,0:T(8,128)(2,1)S(1)} %collective-permute-done.14.refs_1_, ...), custom_call_target="tpu_custom_call" | custom-call | flops 20000000000 | bytes 67108864 | tf_op jit(solution)/shard_map/branch_share/pallas_call | solution.py:185
  79.7 1.7 %collective-permute-start.17 = (bf16[64,1024]{1,0:T(8,128)(2,1)}, bf16[64,1024]{1,0:T(8,128)(2,1)}, u32[]{:S(2)}, u32[]{:S(2)}) collective-permute-start(bf16[64,1024]{1,0:T(8,128)(2,1)} %get-tuple-element.41), channel_id=1, source_target_pairs={{0,1},{1,2},{2,3},{3,0},{4,5},{5,6},{6,7},{7,4},{8,9},{9,10},{10,1... | collective-permute-start | bytes 393224 | tf_op jit(solution)/shard_map/ppermute | solution.py:463
  81.4 2.8 %collective-permute-start.18 = (bf16[64,1024]{1,0:T(8,128)(2,1)}, bf16[64,1024]{1,0:T(8,128)(2,1)}, u32[]{:S(2)}, u32[]{:S(2)}) collective-permute-start(bf16[64,1024]{1,0:T(8,128)(2,1)} %get-tuple-element.42), channel_id=1, source_target_pairs={{0,2},{1,3},{2,0},{3,1},{4,6},{5,7},{6,4},{7,5},{8,10},{9,11},{10,... | collective-permute-start | bytes 393224 | tf_op jit(solution)/shard_map/ppermute | solution.py:463
  84.2 2.0 %collective-permute-start.19 = (bf16[64,1024]{1,0:T(8,128)(2,1)}, bf16[64,1024]{1,0:T(8,128)(2,1)}, u32[]{:S(2)}, u32[]{:S(2)}) collective-permute-start(bf16[64,1024]{1,0:T(8,128)(2,1)} %get-tuple-element.43), channel_id=1, source_target_pairs={{0,3},{1,0},{2,1},{3,2},{4,7},{5,4},{6,5},{7,6},{8,11},{9,8},{10,9... | collective-permute-start | bytes 393224 | tf_op jit(solution)/shard_map/ppermute | solution.py:463
  86.3 2.2 %copy-done.3 = bf16[4096,512]{1,0:T(8,128)(2,1)S(1)} copy-done((bf16[4096,512]{1,0:T(8,128)(2,1)S(1)}, bf16[4096,512]{1,0:T(8,128)(2,1)}, u32[]{:S(2)}) %copy-start.3) | copy-done | bytes 4194328
  89.4 2.2 %hidden_share.1 = (bf16[64,1152]{1,0:T(8,128)(2,1)S(1)}, bf16[64,1152]{1,0:T(8,128)(2,1)S(1)}, bf16[64,1152]{1,0:T(8,128)(2,1)S(1)}, bf16[64,1152]{1,0:T(8,128)(2,1)S(1)}) custom-call(bf16[64,1024]{1,0:T(8,128)(2,1)S(1)} %copy-done.19, bf16[64,1024]{1,0:T(8,128)(2,1)S(1)} %pick_rows.2.refs_3_.refs_0_, bf16[64,1024]{1,0:T(8,128)(2,1)S(1)} %collective-permute-done.refs_1_, ...), custom_call_target="tpu_custom_call" | custom-call | flops 20000000000 | bytes 67108864 | tf_op jit(solution)/shard_map/hidden_share/pallas_call | solution.py:234
  91.9 2.1 %collective-permute-start.21 = (bf16[64,1152]{1,0:T(8,128)(2,1)S(1)}, bf16[64,1152]{1,0:T(8,128)(2,1)S(1)}, u32[]{:S(2)}, u32[]{:S(2)}) collective-permute-start(bf16[64,1152]{1,0:T(8,128)(2,1)S(1)} %get-tuple-element.48), channel_id=1, source_target_pairs={{0,2},{1,3},{2,0},{3,1},{4,6},{5,7},{6,4},{7,5},{8,10},{9,11},{10,... | collective-permute-start | bytes 442376 | tf_op jit(solution)/shard_map/ppermute | solution.py:463
  94.4 2.9 %put_mixed.1 = bf16[1024,1024]{1,0:T(8,128)(2,1)} custom-call(s32[1,64]{1,0:T(1,128)S(1)} %bitcast.7, bf16[1024,1024]{1,0:T(8,128)(2,1)S(1)} %copy-done.9, bf16[64,1024]{1,0:T(8,128)(2,1)S(1)} %pick_rows.2.refs_3_.refs_0_, f32[64,128]{1,0:T(8,128)S(1)} %copy-done.15, bf16[64,1024]{1,0:T(8,128)(2,1)S(1)} %copy-done.17, ...), custom_call_target="tpu_custom_call" | custom-call | flops 3000000000 | bytes 8388608 | tf_op jit(solution)/shard_map/put_mixed/pallas_call | solution.py:272
  98.2 1.7 %collective-permute-done.21.refs_6_ = bf16[64,1152]{1,0:T(8,128)(2,1)S(1)} collective-permute-done((bf16[64,1152]{1,0:T(8,128)(2,1)S(1)}, bf16[64,1152]{1,0:T(8,128)(2,1)S(1)}, u32[]{:S(2)}, u32[]{:S(2)}) %collective-permute-start.21) | collective-permute-done | bytes 147488 | tf_op jit(solution)/shard_map/ppermute | solution.py:463
  99.8 1.5 %collective-permute-done.22.refs_7_ = bf16[64,1152]{1,0:T(8,128)(2,1)S(1)} collective-permute-done((bf16[64,1152]{1,0:T(8,128)(2,1)S(1)}, bf16[64,1152]{1,0:T(8,128)(2,1)S(1)}, u32[]{:S(2)}, u32[]{:S(2)}) %collective-permute-start.22) | collective-permute-done | bytes 147488 | tf_op jit(solution)/shard_map/ppermute | solution.py:463
  101.4 1.8 %put_grad.1 = bf16[1024,1024]{1,0:T(8,128)(2,1)} custom-call(s32[1,64]{1,0:T(1,128)S(1)} %bitcast.8, bf16[1024,1024]{1,0:T(8,128)(2,1)S(1)} %copy-done.11, bf16[64,1024]{1,0:T(8,128)(2,1)S(1)} %pick_rows.2.refs_3_.refs_0_, bf16[64,1024]{1,0:T(8,128)(2,1)S(1)} %pick_rows.3.refs_4_.refs_1_, f32[64,128]{1,0:T(8,128)S(1)} %copy-done.15, ...), custom_call_target="tpu_custom_call" | custom-call | flops 3000000000 | bytes 8388608 | tf_op jit(solution)/shard_map/put_grad/pallas_call | solution.py:272
  (74 shorter events, 16.2 us)
Async XLA Ops:
  2.9 10.9 %copy-start = (bf16[512,4096]{1,0:T(8,128)(2,1)S(1)}, bf16[512,4096]{1,0:T(8,128)(2,1)}, u32[]{:S(2)}) copy-start(bf16[512,4096]{1,0:T(8,128)(2,1)} %refs_4_.1) | copy-start | bytes 12582916
  3.4 10.3 %collective-permute-start.4 = (bf16[64,1024]{1,0:T(8,128)(2,1)S(1)}, bf16[64,1024]{1,0:T(8,128)(2,1)S(1)}, u32[]{:S(2)}, u32[]{:S(2)}) collective-permute-start(bf16[64,1024]{1,0:T(8,128)(2,1)S(1)} %pick_rows.3.refs_4_.refs_1_), channel_id=1, source_target_pairs={{0,3},{1,0},{2,1},{3,2},{4,7},{5,4},{6,5},{7,6},{8,11},{9,8},{10,9... | collective-permute-start | bytes 393224 | tf_op jit(solution)/shard_map/ppermute | solution.py:463
  5.8 10.5 %collective-permute-start.3 = (bf16[64,1024]{1,0:T(8,128)(2,1)S(1)}, bf16[64,1024]{1,0:T(8,128)(2,1)S(1)}, u32[]{:S(2)}, u32[]{:S(2)}) collective-permute-start(bf16[64,1024]{1,0:T(8,128)(2,1)S(1)} %pick_rows.3.refs_4_.refs_1_), channel_id=1, source_target_pairs={{0,1},{1,2},{2,3},{3,0},{4,5},{5,6},{6,7},{7,4},{8,9},{9,10},{10,1... | collective-permute-start | bytes 393224 | tf_op jit(solution)/shard_map/ppermute | solution.py:463
  7.4 6.4 %copy-start.20 = (bf16[4096]{0:T(1024)(128)(2,1)S(1)}, bf16[4096]{0:T(1024)(128)(2,1)}, u32[]{:S(2)}) copy-start(bf16[4096]{0:T(1024)(128)(2,1)} %param.10) | copy-start | bytes 24580
  7.9 8.3 %collective-permute-start.2 = (bf16[64,1024]{1,0:T(8,128)(2,1)S(1)}, bf16[64,1024]{1,0:T(8,128)(2,1)S(1)}, u32[]{:S(2)}, u32[]{:S(2)}) collective-permute-start(bf16[64,1024]{1,0:T(8,128)(2,1)S(1)} %pick_rows.2.refs_3_.refs_0_), channel_id=1, source_target_pairs={{0,3},{1,0},{2,1},{3,2},{4,7},{5,4},{6,5},{7,6},{8,11},{9,8},{10,9... | collective-permute-start | bytes 393224 | tf_op jit(solution)/shard_map/ppermute | solution.py:463
  10.0 8.2 %collective-permute-start.1 = (bf16[64,1024]{1,0:T(8,128)(2,1)S(1)}, bf16[64,1024]{1,0:T(8,128)(2,1)S(1)}, u32[]{:S(2)}, u32[]{:S(2)}) collective-permute-start(bf16[64,1024]{1,0:T(8,128)(2,1)S(1)} %pick_rows.2.refs_3_.refs_0_), channel_id=1, source_target_pairs={{0,2},{1,3},{2,0},{3,1},{4,6},{5,7},{6,4},{7,5},{8,10},{9,11},{10,... | collective-permute-start | bytes 393224 | tf_op jit(solution)/shard_map/ppermute | solution.py:463
  11.2 7.1 %collective-permute-start = (bf16[64,1024]{1,0:T(8,128)(2,1)S(1)}, bf16[64,1024]{1,0:T(8,128)(2,1)S(1)}, u32[]{:S(2)}, u32[]{:S(2)}) collective-permute-start(bf16[64,1024]{1,0:T(8,128)(2,1)S(1)} %pick_rows.2.refs_3_.refs_0_), channel_id=1, source_target_pairs={{0,1},{1,2},{2,3},{3,0},{4,5},{5,6},{6,7},{7,4},{8,9},{9,10},{10,1... | collective-permute-start | bytes 393224 | tf_op jit(solution)/shard_map/ppermute | solution.py:463
  13.7 5.5 %collective-permute-start.5 = (bf16[64,1024]{1,0:T(8,128)(2,1)S(1)}, bf16[64,1024]{1,0:T(8,128)(2,1)S(1)}, u32[]{:S(2)}, u32[]{:S(2)}) collective-permute-start(bf16[64,1024]{1,0:T(8,128)(2,1)S(1)} %collective-permute-done.4.refs_7_), channel_id=1, source_target_pairs={{0,3},{1,0},{2,1},{3,2},{4,7},{5,4},{6,5},{7,6},{8,11},{9,8},{10,9... | collective-permute-start | bytes 393224 | tf_op jit(solution)/shard_map/ppermute | solution.py:463
  22.8 19.4 %all-to-all-start = ((bf16[8,64,256]{2,1,0:T(8,128)(2,1)}), bf16[8,64,256]{2,1,0:T(8,128)(2,1)S(1)}, u32[]{:S(2)}, u32[]{:S(2)}) async-start(bf16[8,64,256]{2,1,0:T(8,128)(2,1)} %get-tuple-element.27), calls=%async_computation | async-start | bytes 524288 | tf_op jit(solution)/shard_map/all_to_all | solution.py:459
  31.3 6.9 %collective-permute-start.8 = (bf16[64,1024]{1,0:T(8,128)(2,1)S(1)}, bf16[64,1024]{1,0:T(8,128)(2,1)S(1)}, u32[]{:S(2)}, u32[]{:S(2)}) collective-permute-start(bf16[64,1024]{1,0:T(8,128)(2,1)S(1)} %get-tuple-element.30.refs_0_.refs_5_), channel_id=1, source_target_pairs={{0,24},{8,0},{16,8},{24,16},{1,25},{9,1},{17,9},{25,17},{2,26},{10... | collective-permute-start | bytes 393224 | tf_op jit(solution)/shard_map/ppermute | solution.py:463
  34.3 6.6 %collective-permute-start.7 = (bf16[64,1024]{1,0:T(8,128)(2,1)S(1)}, bf16[64,1024]{1,0:T(8,128)(2,1)S(1)}, u32[]{:S(2)}, u32[]{:S(2)}) collective-permute-start(bf16[64,1024]{1,0:T(8,128)(2,1)S(1)} %get-tuple-element.30.refs_0_.refs_5_), channel_id=1, source_target_pairs={{0,16},{8,24},{16,0},{24,8},{1,17},{9,25},{17,1},{25,9},{2,18},{10... | collective-permute-start | bytes 393224 | tf_op jit(solution)/shard_map/ppermute | solution.py:463
  35.0 7.2 %collective-permute-start.6 = (bf16[64,1024]{1,0:T(8,128)(2,1)S(1)}, bf16[64,1024]{1,0:T(8,128)(2,1)S(1)}, u32[]{:S(2)}, u32[]{:S(2)}) collective-permute-start(bf16[64,1024]{1,0:T(8,128)(2,1)S(1)} %get-tuple-element.30.refs_0_.refs_5_), channel_id=1, source_target_pairs={{0,8},{8,16},{16,24},{24,0},{1,9},{9,17},{17,25},{25,1},{2,10},{10... | collective-permute-start | bytes 393224 | tf_op jit(solution)/shard_map/ppermute | solution.py:463
  42.2 1.3 %collective-permute-start.10 = (bf16[64,1024]{1,0:T(8,128)(2,1)S(1)}, bf16[64,1024]{1,0:T(8,128)(2,1)S(1)}, u32[]{:S(2)}, u32[]{:S(2)}) collective-permute-start(bf16[64,1024]{1,0:T(8,128)(2,1)S(1)} %collective-permute-done.6.refs_1_), channel_id=1, source_target_pairs={{0,4},{4,0},{1,5},{5,1},{2,6},{6,2},{3,7},{7,3},{8,12},{12,8},{9,1... | collective-permute-start | bytes 393224 | tf_op jit(solution)/shard_map/ppermute | solution.py:463
  42.2 1.5 %collective-permute-start.11 = (bf16[64,1024]{1,0:T(8,128)(2,1)S(1)}, bf16[64,1024]{1,0:T(8,128)(2,1)S(1)}, u32[]{:S(2)}, u32[]{:S(2)}) collective-permute-start(bf16[64,1024]{1,0:T(8,128)(2,1)S(1)} %collective-permute-done.7.refs_2_), channel_id=1, source_target_pairs={{0,4},{4,0},{1,5},{5,1},{2,6},{6,2},{3,7},{7,3},{8,12},{12,8},{9,1... | collective-permute-start | bytes 393224 | tf_op jit(solution)/shard_map/ppermute | solution.py:463
  42.7 1.3 %collective-permute-start.12 = (bf16[64,1024]{1,0:T(8,128)(2,1)S(1)}, bf16[64,1024]{1,0:T(8,128)(2,1)S(1)}, u32[]{:S(2)}, u32[]{:S(2)}) collective-permute-start(bf16[64,1024]{1,0:T(8,128)(2,1)S(1)} %collective-permute-done.8.refs_3_), channel_id=1, source_target_pairs={{0,4},{4,0},{1,5},{5,1},{2,6},{6,2},{3,7},{7,3},{8,12},{12,8},{9,1... | collective-permute-start | bytes 393224 | tf_op jit(solution)/shard_map/ppermute | solution.py:463
  42.7 1.5 %collective-permute-start.9 = (bf16[64,1024]{1,0:T(8,128)(2,1)S(1)}, bf16[64,1024]{1,0:T(8,128)(2,1)S(1)}, u32[]{:S(2)}, u32[]{:S(2)}) collective-permute-start(bf16[64,1024]{1,0:T(8,128)(2,1)S(1)} %get-tuple-element.30.refs_0_.refs_5_), channel_id=1, source_target_pairs={{0,4},{4,0},{1,5},{5,1},{2,6},{6,2},{3,7},{7,3},{8,12},{12,8},{9,1... | collective-permute-start | bytes 393224 | tf_op jit(solution)/shard_map/ppermute | solution.py:463
  60.0 1.9 %collective-permute-start.13 = (bf16[4,64,1024]{2,1,0:T(8,128)(2,1)S(1)}, bf16[4,64,1024]{2,1,0:T(8,128)(2,1)S(1)}, u32[]{:S(2)}, u32[]{:S(2)}) collective-permute-start(bf16[4,64,1024]{2,1,0:T(8,128)(2,1)S(1)} %get-tuple-element.35), channel_id=1, source_target_pairs={{0,4},{4,0},{1,5},{5,1},{2,6},{6,2},{3,7},{7,3},{8,12},{12,8},{9,1... | collective-permute-start | bytes 1572872 | tf_op jit(solution)/shard_map/ppermute | solution.py:463
  62.7 8.4 %collective-permute-start.14 = (bf16[64,1024]{1,0:T(8,128)(2,1)}, bf16[64,1024]{1,0:T(8,128)(2,1)S(1)}, u32[]{:S(2)}, u32[]{:S(2)}) collective-permute-start(bf16[64,1024]{1,0:T(8,128)(2,1)} %get-tuple-element.37), channel_id=1, source_target_pairs={{0,24},{8,0},{16,8},{24,16},{1,25},{9,1},{17,9},{25,17},{2,26},{10... | collective-permute-start | bytes 393224 | tf_op jit(solution)/shard_map/ppermute | solution.py:463
  63.9 8.1 %collective-permute-start.15 = (bf16[64,1024]{1,0:T(8,128)(2,1)}, bf16[64,1024]{1,0:T(8,128)(2,1)S(1)}, u32[]{:S(2)}, u32[]{:S(2)}) collective-permute-start(bf16[64,1024]{1,0:T(8,128)(2,1)} %get-tuple-element.38), channel_id=1, source_target_pairs={{0,16},{8,24},{16,0},{24,8},{1,17},{9,25},{17,1},{25,9},{2,18},{10... | collective-permute-start | bytes 393224 | tf_op jit(solution)/shard_map/ppermute | solution.py:463
  65.3 8.4 %collective-permute-start.16 = (bf16[64,1024]{1,0:T(8,128)(2,1)}, bf16[64,1024]{1,0:T(8,128)(2,1)}, u32[]{:S(2)}, u32[]{:S(2)}) collective-permute-start(bf16[64,1024]{1,0:T(8,128)(2,1)} %get-tuple-element.39), channel_id=1, source_target_pairs={{0,8},{8,16},{16,24},{24,0},{1,9},{9,17},{17,25},{25,1},{2,10},{10... | collective-permute-start | bytes 393224 | tf_op jit(solution)/shard_map/ppermute | solution.py:463
  65.4 20.9 %all-to-all-start.2 = ((bf16[8,64,256]{2,1,0:T(8,128)(2,1)}), bf16[8,64,256]{2,1,0:T(8,128)(2,1)S(1)}, u32[]{:S(2)}, u32[]{:S(2)}) async-start(bf16[8,64,256]{2,1,0:T(8,128)(2,1)} %bitcast.2), calls=%async_computation.2 | async-start | bytes 524288 | tf_op jit(solution)/shard_map/all_to_all | solution.py:459
  79.7 14.2 %collective-permute-start.17 = (bf16[64,1024]{1,0:T(8,128)(2,1)}, bf16[64,1024]{1,0:T(8,128)(2,1)}, u32[]{:S(2)}, u32[]{:S(2)}) collective-permute-start(bf16[64,1024]{1,0:T(8,128)(2,1)} %get-tuple-element.41), channel_id=1, source_target_pairs={{0,1},{1,2},{2,3},{3,0},{4,5},{5,6},{6,7},{7,4},{8,9},{9,10},{10,1... | collective-permute-start | bytes 393224 | tf_op jit(solution)/shard_map/ppermute | solution.py:463
  81.4 12.9 %collective-permute-start.18 = (bf16[64,1024]{1,0:T(8,128)(2,1)}, bf16[64,1024]{1,0:T(8,128)(2,1)}, u32[]{:S(2)}, u32[]{:S(2)}) collective-permute-start(bf16[64,1024]{1,0:T(8,128)(2,1)} %get-tuple-element.42), channel_id=1, source_target_pairs={{0,2},{1,3},{2,0},{3,1},{4,6},{5,7},{6,4},{7,5},{8,10},{9,11},{10,... | collective-permute-start | bytes 393224 | tf_op jit(solution)/shard_map/ppermute | solution.py:463
  84.2 10.1 %collective-permute-start.19 = (bf16[64,1024]{1,0:T(8,128)(2,1)}, bf16[64,1024]{1,0:T(8,128)(2,1)}, u32[]{:S(2)}, u32[]{:S(2)}) collective-permute-start(bf16[64,1024]{1,0:T(8,128)(2,1)} %get-tuple-element.43), channel_id=1, source_target_pairs={{0,3},{1,0},{2,1},{3,2},{4,7},{5,4},{6,5},{7,6},{8,11},{9,8},{10,9... | collective-permute-start | bytes 393224 | tf_op jit(solution)/shard_map/ppermute | solution.py:463
  89.4 5.0 %copy-start.9 = (bf16[1024,1024]{1,0:T(8,128)(2,1)S(1)}, bf16[1024,1024]{1,0:T(8,128)(2,1)}, u32[]{:S(2)}) copy-start(bf16[1024,1024]{1,0:T(8,128)(2,1)} %base_ref.2) | copy-start | bytes 6291460
  89.4 5.0 %copy-start.13 = (s32[64]{0:T(128)S(1)}, s32[64]{0:T(128)}, u32[]{:S(2)}) copy-start(s32[64]{0:T(128)} %param.9) | copy-start | bytes 772
  89.4 5.0 %copy-start.15 = (f32[64,128]{1,0:T(8,128)S(1)}, f32[64,128]{1,0:T(8,128)}, u32[]{:S(2)}) copy-start(f32[64,128]{1,0:T(8,128)} %copy-done.14) | copy-start | bytes 98308
  89.4 5.0 %copy-start.17 = (bf16[64,1024]{1,0:T(8,128)(2,1)S(1)}, bf16[64,1024]{1,0:T(8,128)(2,1)}, u32[]{:S(2)}) copy-start(bf16[64,1024]{1,0:T(8,128)(2,1)} %copy-done.16) | copy-start | bytes 393220
  91.6 6.6 %collective-permute-start.20 = (bf16[64,1152]{1,0:T(8,128)(2,1)S(1)}, bf16[64,1152]{1,0:T(8,128)(2,1)S(1)}, u32[]{:S(2)}, u32[]{:S(2)}) collective-permute-start(bf16[64,1152]{1,0:T(8,128)(2,1)S(1)} %get-tuple-element.47), channel_id=1, source_target_pairs={{0,1},{1,2},{2,3},{3,0},{4,5},{5,6},{6,7},{7,4},{8,9},{9,10},{10,1... | collective-permute-start | bytes 442376 | tf_op jit(solution)/shard_map/ppermute | solution.py:463
  91.9 7.9 %collective-permute-start.21 = (bf16[64,1152]{1,0:T(8,128)(2,1)S(1)}, bf16[64,1152]{1,0:T(8,128)(2,1)S(1)}, u32[]{:S(2)}, u32[]{:S(2)}) collective-permute-start(bf16[64,1152]{1,0:T(8,128)(2,1)S(1)} %get-tuple-element.48), channel_id=1, source_target_pairs={{0,2},{1,3},{2,0},{3,1},{4,6},{5,7},{6,4},{7,5},{8,10},{9,11},{10,... | collective-permute-start | bytes 442376 | tf_op jit(solution)/shard_map/ppermute | solution.py:463
  93.9 7.4 %collective-permute-start.22 = (bf16[64,1152]{1,0:T(8,128)(2,1)S(1)}, bf16[64,1152]{1,0:T(8,128)(2,1)S(1)}, u32[]{:S(2)}, u32[]{:S(2)}) collective-permute-start(bf16[64,1152]{1,0:T(8,128)(2,1)S(1)} %get-tuple-element.49), channel_id=1, source_target_pairs={{0,3},{1,0},{2,1},{3,2},{4,7},{5,4},{6,5},{7,6},{8,11},{9,8},{10,9... | collective-permute-start | bytes 442376 | tf_op jit(solution)/shard_map/ppermute | solution.py:463
  94.4 7.0 %copy-start.11 = (bf16[1024,1024]{1,0:T(8,128)(2,1)S(1)}, bf16[1024,1024]{1,0:T(8,128)(2,1)}, u32[]{:S(2)}) copy-start(bf16[1024,1024]{1,0:T(8,128)(2,1)} %base_ref.3) | copy-start | bytes 6291460
  (14 other events, 22.7 us)

commit v5 on v4

--- a/solution.py
+++ b/solution.py
@@ -171,22 +171,27 @@
 
     def kernel(*refs):
         piece_refs, out_w_ref = refs[:count], refs[count]
-        total_ref, out_refs = refs[count + 2], refs[count + 3 :]
+        total_ref, out_refs = refs[count + 2], refs[count + 2 :]
         tp = lax.axis_index("tp")
         total = piece_refs[0][...].astype(F32)
         for ref in piece_refs[1:]:
             total += ref[...].astype(F32)
-        total_ref[...] = total.astype(BF)
-        attended = total_ref[:, half:]
+        total = total.astype(BF)
+        total_ref[:, :both] = total
+        attended = total[:, half:]
         for s in range(parts):
             columns = pl.ds(pl.multiple_of(lax.rem(tp + s, parts) * part, part), part)
-            out_refs[s][...] = mm(attended, out_w_ref[:, columns], NN).astype(BF)
+            branch = mm(attended, out_w_ref[:, columns], NN).astype(BF)
+            if s == 0:
+                total_ref[:, both:] = branch
+            else:
+                out_refs[s][...] = branch
 
     return pl.pallas_call(
         kernel,
         in_specs=[whole()] * (count + 1) + [far()],
-        out_specs=[whole()] * (1 + parts),
-        out_shape=[like((picked, both))] + [like((picked, part))] * parts,
+        out_specs=[whole()] * parts,
+        out_shape=[like((picked, both + part))] + [like((picked, part))] * (parts - 1),
         compiler_params=params(16),
         cost_estimate=pl.CostEstimate(flops=2 * 10**10, bytes_accessed=2**26, transcendentals=0),
         name="branch_share",
@@ -203,7 +208,7 @@
         kv_ref, own_ref, query_ref, key_ref, value_ref = refs[parts : parts + 5]
         out_refs = refs[parts + 5 :]
         tp = lax.axis_index("tp")
-        query_grad, attended = total_ref[:, :half], total_ref[:, half:]
+        query_grad, attended = total_ref[:, :half], total_ref[:, half : 2 * half]
         kv_sum = kv_ref[0].astype(F32)
         for b in range(1, kv_ref.shape[0]):
             kv_sum += kv_ref[b].astype(F32)
@@ -283,7 +288,7 @@
 
 def put_mixed(sizes, tokens, chosen, rows_in, branches, scales):
     def rows_of(tp, in_ref, scales_ref, *branch_refs):
-        branch = branch_refs[0][...].astype(F32)
+        branch = branch_refs[0][:, branch_refs[0].shape[1] - in_ref.shape[1] :].astype(F32)
         for ref in branch_refs[1:]:
             branch += ref[...].astype(F32)
         return in_ref[...].astype(F32) + scales_ref[:, 0:1] * branch
@@ -500,8 +505,9 @@
     kv_grads = exchange(kv_grads.reshape(planes, picked, 2 * HEAD_DIM), "z")
     chip = add_pieces(mine, shifted(theirs, "core", cores, 1))
     pieces = [chip[0]] + [shifted(chip[s], "y", columns, columns - s) for s in range(1, columns)]
-    total, *branches = branch_share(pieces, w_out, parts_tp, chip[0])
-    shares = hidden_share(total, kv_grads, inputs, own[0], w_query, w_key, w_value)
+    near = touch((w_out,), chip[0])
+    branches = branch_share(pieces, w_out, parts_tp, near)
+    shares = hidden_share(branches[0], kv_grads, inputs, own[0], w_query, w_key, w_value)
     branches = around_tp(branches, parts_tp)
     shares = around_tp(shares, parts_tp)
     mixed = put_mixed(sizes, tokens, chosen, rows_in, branches, scales)

time: 104 us -> 102 us (0.981)
  waiting for transfers between devices: 19 us -> 14.7 us
  starting transfers between devices: 39.9 us -> 41 us
  local copies, waits for them, and re-layouts: 13.6 us -> 14.7 us
    ppermute x23, waiting for transfers between devices: 19 us -> 14.7 us  [shifted(): lax.ppermute(array, axis, [(i, (i + step) % count) for i in range(count)])]
    unnamed x42 -> x40, local copies, waits for them, and re-layouts: 13.5 us -> 14.6 us
  transfers between devices with their start and end apart: 25 -> 25, of which waited for: 15 -> 13; matrix products, arithmetic and copies ran while one was open for 0% -> 0% of each run, Pallas kernels for 8% -> 8%
where the time goes in v5:
time: 102 us; the launch traced here: 101 us
  starting transfers between devices  41 us (40%)
  Pallas kernels  19.9 us (20%)
  local copies, waits for them, and re-layouts  14.7 us (14%)
  waiting for transfers between devices  14.7 us (14%)
  blocking collectives  9.98 us (10%)
    ppermute x23, starting transfers between devices, shifted(): lax.ppermute(array, axis, [(i, (i + step) % count) for i in range(count)])  26.7 us
    ppermute x23, waiting for transfers between devices, shifted(): lax.ppermute(array, axis, [(i, (i + step) % count) for i in range(count)])  14.7 us
    unnamed x40, local copies, waits for them, and re-layouts  14.6 us
    all_to_all x2, starting transfers between devices, exchange(): return lax.all_to_all(array, axis, 0, 0, tiled=True)  14.2 us
    all_to_all x1, blocking collectives, exchange(): return lax.all_to_all(array, axis, 0, 0, tiled=True)  9.98 us
    pallas_call x2, Pallas kernels, put_rows(): pl.pallas_call(kernel, in_specs=[whole()] * (2 + count), out_specs=far(),...  4.7 us
    pallas_call x1, Pallas kernels, attention_parts(): pl.pallas_call(kernel, in_specs=[whole()] * (2 + 2 * n), out_specs=[whole...  3.93 us
    pallas_call x1, Pallas kernels, project(): pl.pallas_call(kernel, in_specs=[whole()] * len(ins) + [far()], out_specs...  2.94 us
  transfers between devices with their start and end apart: 25, of which 13 were waited for; matrix products, arithmetic and copies ran while one was open for 0% of the time, Pallas kernels for 8%

profile of v5, /device:TPU:2, one launch (start us, length us, event | category | flops | bytes accessed | tf_op | source)
XLA Modules:
  0.0 101.3 jit_solution(2412053707526961209)
XLA Ops:
  0.6 1.6 %copy-done.11 = bf16[1024,1024]{1,0:T(8,128)(2,1)S(1)} copy-done((bf16[1024,1024]{1,0:T(8,128)(2,1)S(1)}, bf16[1024,1024]{1,0:T(8,128)(2,1)}, u32[]{:S(2)}) %copy-start.11) | copy-done | bytes 2097176
  3.4 2.3 %collective-permute-start.4 = (bf16[64,1024]{1,0:T(8,128)(2,1)S(1)}, bf16[64,1024]{1,0:T(8,128)(2,1)S(1)}, u32[]{:S(2)}, u32[]{:S(2)}) collective-permute-start(bf16[64,1024]{1,0:T(8,128)(2,1)S(1)} %pick_rows.3.refs_4_.refs_1_), channel_id=1, source_target_pairs={{0,3},{1,0},{2,1},{3,2},{4,7},{5,4},{6,5},{7,6},{8,11},{9,8},{10,9... | collective-permute-start | bytes 393224 | tf_op jit(solution)/shard_map/ppermute | solution.py:468
  5.8 1.6 %copy-done.9 = bf16[1024,1024]{1,0:T(8,128)(2,1)S(1)} copy-done((bf16[1024,1024]{1,0:T(8,128)(2,1)S(1)}, bf16[1024,1024]{1,0:T(8,128)(2,1)}, u32[]{:S(2)}) %copy-start.9) | copy-done | bytes 2097176
  7.9 2.1 %collective-permute-start.2 = (bf16[64,1024]{1,0:T(8,128)(2,1)S(1)}, bf16[64,1024]{1,0:T(8,128)(2,1)S(1)}, u32[]{:S(2)}, u32[]{:S(2)}) collective-permute-start(bf16[64,1024]{1,0:T(8,128)(2,1)S(1)} %pick_rows.2.refs_3_.refs_0_), channel_id=1, source_target_pairs={{0,3},{1,0},{2,1},{3,2},{4,7},{5,4},{6,5},{7,6},{8,11},{9,8},{10,9... | collective-permute-start | bytes 393224 | tf_op jit(solution)/shard_map/ppermute | solution.py:468
  11.2 2.5 %collective-permute-start = (bf16[64,1024]{1,0:T(8,128)(2,1)S(1)}, bf16[64,1024]{1,0:T(8,128)(2,1)S(1)}, u32[]{:S(2)}, u32[]{:S(2)}) collective-permute-start(bf16[64,1024]{1,0:T(8,128)(2,1)S(1)} %pick_rows.2.refs_3_.refs_0_), channel_id=1, source_target_pairs={{0,1},{1,2},{2,3},{3,0},{4,5},{5,6},{6,7},{7,4},{8,9},{9,10},{10,1... | collective-permute-start | bytes 393224 | tf_op jit(solution)/shard_map/ppermute | solution.py:468
  15.0 1.2 %copy-done.7 = bf16[4096,128]{1,0:T(8,128)(2,1)S(1)} copy-done((bf16[4096,128]{1,0:T(8,128)(2,1)S(1)}, bf16[4096,128]{1,0:T(8,128)(2,1)}, u32[]{:S(2)}) %copy-start.7) | copy-done | bytes 1048600
  16.3 2.0 %collective-permute-done.1.refs_2_ = bf16[64,1024]{1,0:T(8,128)(2,1)S(1)} collective-permute-done((bf16[64,1024]{1,0:T(8,128)(2,1)S(1)}, bf16[64,1024]{1,0:T(8,128)(2,1)S(1)}, u32[]{:S(2)}, u32[]{:S(2)}) %collective-permute-start.1) | collective-permute-done | bytes 131104 | tf_op jit(solution)/shard_map/ppermute | solution.py:468
  19.3 2.9 %project.1 = (bf16[8,64,256]{2,1,0:T(8,128)(2,1)}, bf16[64,1024]{1,0:T(8,128)(2,1)S(1)}, f32[64,128]{1,0:T(8,128)S(1)}) custom-call(bf16[64,1024]{1,0:T(8,128)(2,1)S(1)} %pick_rows.2.refs_3_.refs_0_, bf16[64,1024]{1,0:T(8,128)(2,1)S(1)} %collective-permute-done.refs_1_, bf16[64,1024]{1,0:T(8,128)(2,1)S(1)} %collective-permute-done.1.refs_2_, ...), custom_call_target="tpu_custom_call" | custom-call | tf_op jit(solution)/shard_map/project/pallas_call | solution.py:125
  22.8 8.5 %all-to-all-start = ((bf16[8,64,256]{2,1,0:T(8,128)(2,1)}), bf16[8,64,256]{2,1,0:T(8,128)(2,1)S(1)}, u32[]{:S(2)}, u32[]{:S(2)}) async-start(bf16[8,64,256]{2,1,0:T(8,128)(2,1)} %get-tuple-element.26), calls=%async_computation | async-start | bytes 524288 | tf_op jit(solution)/shard_map/all_to_all | solution.py:464
  31.3 3.0 %collective-permute-start.8 = (bf16[64,1024]{1,0:T(8,128)(2,1)S(1)}, bf16[64,1024]{1,0:T(8,128)(2,1)S(1)}, u32[]{:S(2)}, u32[]{:S(2)}) collective-permute-start(bf16[64,1024]{1,0:T(8,128)(2,1)S(1)} %get-tuple-element.29.refs_0_.refs_5_), channel_id=1, source_target_pairs={{0,24},{8,0},{16,8},{24,16},{1,25},{9,1},{17,9},{25,17},{2,26},{10... | collective-permute-start | bytes 393224 | tf_op jit(solution)/shard_map/ppermute | solution.py:468
  35.9 2.3 %collective-permute-done.8.refs_3_ = bf16[64,1024]{1,0:T(8,128)(2,1)S(1)} collective-permute-done((bf16[64,1024]{1,0:T(8,128)(2,1)S(1)}, bf16[64,1024]{1,0:T(8,128)(2,1)S(1)}, u32[]{:S(2)}, u32[]{:S(2)}) %collective-permute-start.8) | collective-permute-done | bytes 131104 | tf_op jit(solution)/shard_map/ppermute | solution.py:468
  38.2 2.7 %collective-permute-done.7.refs_2_ = bf16[64,1024]{1,0:T(8,128)(2,1)S(1)} collective-permute-done((bf16[64,1024]{1,0:T(8,128)(2,1)S(1)}, bf16[64,1024]{1,0:T(8,128)(2,1)S(1)}, u32[]{:S(2)}, u32[]{:S(2)}) %collective-permute-start.7) | collective-permute-done | bytes 131104 | tf_op jit(solution)/shard_map/ppermute | solution.py:468
  40.9 1.3 %collective-permute-done.6.refs_1_ = bf16[64,1024]{1,0:T(8,128)(2,1)S(1)} collective-permute-done((bf16[64,1024]{1,0:T(8,128)(2,1)S(1)}, bf16[64,1024]{1,0:T(8,128)(2,1)S(1)}, u32[]{:S(2)}, u32[]{:S(2)}) %collective-permute-start.6) | collective-permute-done | bytes 131104 | tf_op jit(solution)/shard_map/ppermute | solution.py:468
  44.2 1.8 %softmax_parts.1 = f32[4,2,512]{2,1,0:T(2,128)S(1)} custom-call(bf16[512,256]{1,0:T(8,128)(2,1)S(1)} %bitcast.3, bf16[64,1024]{1,0:T(8,128)(2,1)S(1)} %get-tuple-element.29.refs_0_.refs_5_, bf16[64,1024]{1,0:T(8,128)(2,1)S(1)} %collective-permute-done.6.refs_1_, bf16[64,1024]{1,0:T(8,128)(2,1)S(1)} %collective-permute-done.7.refs_2_, ...), custom_call_target="tpu_custom_call" | custom-call | tf_op jit(solution)/shard_map/softmax_parts/pallas_call | solution.py:385
  46.1 10.0 %all_to_all.15.parts_ref = f32[8,4,2,512]{3,2,1,0:T(2,128)S(1)} all-to-all(f32[8,4,2,512]{3,2,1,0:T(2,128)S(1)} %broadcast_in_dim.14), channel_id=1, replica_groups=mesh['z'=8,'y'=4,'core'=2,'tp'=4] {'y','core'}, dimensions={0} | all-to-all | bytes 262144 | tf_op jit(solution)/shard_map/all_to_all | solution.py:464
  56.1 3.9 %attention_parts.1 = (bf16[4,64,1024]{2,1,0:T(8,128)(2,1)S(1)}, bf16[4,64,1024]{2,1,0:T(8,128)(2,1)S(1)}, bf16[512,256]{1,0:T(8,128)(2,1)}) custom-call(bf16[512,256]{1,0:T(8,128)(2,1)S(1)} %bitcast.4, f32[8,4,2,512]{3,2,1,0:T(2,128)S(1)} %all_to_all.15.parts_ref, bf16[64,1024]{1,0:T(8,128)(2,1)S(1)} %get-tuple-element.29.refs_0_.refs_5_, ...), custom_call_target="tpu_custom_call" | custom-call | tf_op jit(solution)/shard_map/attention_parts/pallas_call | solution.py:448
  60.0 1.9 %collective-permute-done.13.received_ref = bf16[4,64,1024]{2,1,0:T(8,128)(2,1)S(1)} collective-permute-done((bf16[4,64,1024]{2,1,0:T(8,128)(2,1)S(1)}, bf16[4,64,1024]{2,1,0:T(8,128)(2,1)S(1)}, u32[]{:S(2)}, u32[]{:S(2)}) %collective-permute-start.13) | collective-permute-done | bytes 524320 | tf_op jit(solution)/shard_map/ppermute | solution.py:468
  63.8 1.5 %collective-permute-start.15 = (bf16[64,1024]{1,0:T(8,128)(2,1)}, bf16[64,1024]{1,0:T(8,128)(2,1)}, u32[]{:S(2)}, u32[]{:S(2)}) collective-permute-start(bf16[64,1024]{1,0:T(8,128)(2,1)} %get-tuple-element.37), channel_id=1, source_target_pairs={{0,16},{8,24},{16,0},{24,8},{1,17},{9,25},{17,1},{25,9},{2,18},{10... | collective-permute-start | bytes 393224 | tf_op jit(solution)/shard_map/ppermute | solution.py:468
  65.3 5.8 %all-to-all-start.2 = ((bf16[8,64,256]{2,1,0:T(8,128)(2,1)}), bf16[8,64,256]{2,1,0:T(8,128)(2,1)S(1)}, u32[]{:S(2)}, u32[]{:S(2)}) async-start(bf16[8,64,256]{2,1,0:T(8,128)(2,1)} %bitcast.2), calls=%async_computation.2 | async-start | bytes 524288 | tf_op jit(solution)/shard_map/all_to_all | solution.py:464
  71.0 2.2 %copy-done.1 = bf16[512,4096]{1,0:T(8,128)(2,1)S(1)} copy-done((bf16[512,4096]{1,0:T(8,128)(2,1)S(1)}, bf16[512,4096]{1,0:T(8,128)(2,1)}, u32[]{:S(2)}) %copy-start.1) | copy-done | bytes 4194328
  73.7 1.7 %copy-done.2 = bf16[512,4096]{1,0:T(8,128)(2,1)S(1)} copy-done((bf16[512,4096]{1,0:T(8,128)(2,1)S(1)}, bf16[512,4096]{1,0:T(8,128)(2,1)}, u32[]{:S(2)}) %copy-start.2) | copy-done | bytes 4194328
  75.4 2.5 %branch_share.1 = (bf16[64,2048]{1,0:T(8,128)(2,1)S(1)}, bf16[64,1024]{1,0:T(8,128)(2,1)}, bf16[64,1024]{1,0:T(8,128)(2,1)}, bf16[64,1024]{1,0:T(8,128)(2,1)}) custom-call(bf16[64,1024]{1,0:T(8,128)(2,1)S(1)} %get-tuple-element.35.refs_1_.refs_0_, bf16[64,1024]{1,0:T(8,128)(2,1)S(1)} %collective-permute-done.14.refs_1_, ...), custom_call_target="tpu_custom_call" | custom-call | flops 20000000000 | bytes 67108864 | tf_op jit(solution)/shard_map/branch_share/pallas_call | solution.py:190
  78.6 1.7 %collective-permute-start.17 = (bf16[64,1024]{1,0:T(8,128)(2,1)}, bf16[64,1024]{1,0:T(8,128)(2,1)}, u32[]{:S(2)}, u32[]{:S(2)}) collective-permute-start(bf16[64,1024]{1,0:T(8,128)(2,1)} %get-tuple-element.40), channel_id=1, source_target_pairs={{0,1},{1,2},{2,3},{3,0},{4,5},{5,6},{6,7},{7,4},{8,9},{9,10},{10,1... | collective-permute-start | bytes 393224 | tf_op jit(solution)/shard_map/ppermute | solution.py:468
  80.4 2.2 %collective-permute-start.18 = (bf16[64,1024]{1,0:T(8,128)(2,1)}, bf16[64,1024]{1,0:T(8,128)(2,1)}, u32[]{:S(2)}, u32[]{:S(2)}) collective-permute-start(bf16[64,1024]{1,0:T(8,128)(2,1)} %get-tuple-element.41), channel_id=1, source_target_pairs={{0,2},{1,3},{2,0},{3,1},{4,6},{5,7},{6,4},{7,5},{8,10},{9,11},{10,... | collective-permute-start | bytes 393224 | tf_op jit(solution)/shard_map/ppermute | solution.py:468
  82.6 2.0 %collective-permute-start.19 = (bf16[64,1024]{1,0:T(8,128)(2,1)}, bf16[64,1024]{1,0:T(8,128)(2,1)}, u32[]{:S(2)}, u32[]{:S(2)}) collective-permute-start(bf16[64,1024]{1,0:T(8,128)(2,1)} %get-tuple-element.42), channel_id=1, source_target_pairs={{0,3},{1,0},{2,1},{3,2},{4,7},{5,4},{6,5},{7,6},{8,11},{9,8},{10,9... | collective-permute-start | bytes 393224 | tf_op jit(solution)/shard_map/ppermute | solution.py:468
  84.6 2.2 %copy-done.4 = bf16[4096,512]{1,0:T(8,128)(2,1)S(1)} copy-done((bf16[4096,512]{1,0:T(8,128)(2,1)S(1)}, bf16[4096,512]{1,0:T(8,128)(2,1)}, u32[]{:S(2)}) %copy-start.4) | copy-done | bytes 4194328
  87.8 2.2 %hidden_share.1 = (bf16[64,1152]{1,0:T(8,128)(2,1)S(1)}, bf16[64,1152]{1,0:T(8,128)(2,1)S(1)}, bf16[64,1152]{1,0:T(8,128)(2,1)S(1)}, bf16[64,1152]{1,0:T(8,128)(2,1)S(1)}) custom-call(bf16[64,2048]{1,0:T(8,128)(2,1)S(1)} %copy-done.18, bf16[64,1024]{1,0:T(8,128)(2,1)S(1)} %pick_rows.2.refs_3_.refs_0_, bf16[64,1024]{1,0:T(8,128)(2,1)S(1)} %collective-permute-done.refs_1_, ...), custom_call_target="tpu_custom_call" | custom-call | flops 20000000000 | bytes 67108864 | tf_op jit(solution)/shard_map/hidden_share/pallas_call | solution.py:239
  90.3 2.5 %collective-permute-start.21 = (bf16[64,1152]{1,0:T(8,128)(2,1)S(1)}, bf16[64,1152]{1,0:T(8,128)(2,1)S(1)}, u32[]{:S(2)}, u32[]{:S(2)}) collective-permute-start(bf16[64,1152]{1,0:T(8,128)(2,1)S(1)} %get-tuple-element.46), channel_id=1, source_target_pairs={{0,2},{1,3},{2,0},{3,1},{4,6},{5,7},{6,4},{7,5},{8,10},{9,11},{10,... | collective-permute-start | bytes 442376 | tf_op jit(solution)/shard_map/ppermute | solution.py:468
  92.8 1.5 %collective-permute-start.22 = (bf16[64,1152]{1,0:T(8,128)(2,1)S(1)}, bf16[64,1152]{1,0:T(8,128)(2,1)S(1)}, u32[]{:S(2)}, u32[]{:S(2)}) collective-permute-start(bf16[64,1152]{1,0:T(8,128)(2,1)S(1)} %get-tuple-element.47), channel_id=1, source_target_pairs={{0,3},{1,0},{2,1},{3,2},{4,7},{5,4},{6,5},{7,6},{8,11},{9,8},{10,9... | collective-permute-start | bytes 442376 | tf_op jit(solution)/shard_map/ppermute | solution.py:468
  94.3 2.9 %put_mixed.1 = bf16[1024,1024]{1,0:T(8,128)(2,1)} custom-call(s32[1,64]{1,0:T(1,128)S(1)} %bitcast.7, bf16[1024,1024]{1,0:T(8,128)(2,1)S(1)} %copy-done.10, bf16[64,1024]{1,0:T(8,128)(2,1)S(1)} %pick_rows.2.refs_3_.refs_0_, f32[64,128]{1,0:T(8,128)S(1)} %copy-done.16, bf16[64,2048]{1,0:T(8,128)(2,1)S(1)} %copy-done.18, ...), custom_call_target="tpu_custom_call" | custom-call | flops 3000000000 | bytes 8388608 | tf_op jit(solution)/shard_map/put_mixed/pallas_call | solution.py:277
  97.8 1.5 %collective-permute-done.22.refs_7_ = bf16[64,1152]{1,0:T(8,128)(2,1)S(1)} collective-permute-done((bf16[64,1152]{1,0:T(8,128)(2,1)S(1)}, bf16[64,1152]{1,0:T(8,128)(2,1)S(1)}, u32[]{:S(2)}, u32[]{:S(2)}) %collective-permute-start.22) | collective-permute-done | bytes 147488 | tf_op jit(solution)/shard_map/ppermute | solution.py:468
  99.2 1.8 %put_grad.1 = bf16[1024,1024]{1,0:T(8,128)(2,1)} custom-call(s32[1,64]{1,0:T(1,128)S(1)} %bitcast.8, bf16[1024,1024]{1,0:T(8,128)(2,1)S(1)} %copy-done.12, bf16[64,1024]{1,0:T(8,128)(2,1)S(1)} %pick_rows.2.refs_3_.refs_0_, bf16[64,1024]{1,0:T(8,128)(2,1)S(1)} %pick_rows.3.refs_4_.refs_1_, f32[64,128]{1,0:T(8,128)S(1)} %copy-done.16, ...), custom_call_target="tpu_custom_call" | custom-call | flops 3000000000 | bytes 8388608 | tf_op jit(solution)/shard_map/put_grad/pallas_call | solution.py:277
  (73 shorter events, 14.4 us)
Async XLA Ops:
  2.9 10.9 %copy-start = (bf16[512,4096]{1,0:T(8,128)(2,1)S(1)}, bf16[512,4096]{1,0:T(8,128)(2,1)}, u32[]{:S(2)}) copy-start(bf16[512,4096]{1,0:T(8,128)(2,1)} %refs_4_.1) | copy-start | bytes 12582916
  3.4 10.3 %collective-permute-start.4 = (bf16[64,1024]{1,0:T(8,128)(2,1)S(1)}, bf16[64,1024]{1,0:T(8,128)(2,1)S(1)}, u32[]{:S(2)}, u32[]{:S(2)}) collective-permute-start(bf16[64,1024]{1,0:T(8,128)(2,1)S(1)} %pick_rows.3.refs_4_.refs_1_), channel_id=1, source_target_pairs={{0,3},{1,0},{2,1},{3,2},{4,7},{5,4},{6,5},{7,6},{8,11},{9,8},{10,9... | collective-permute-start | bytes 393224 | tf_op jit(solution)/shard_map/ppermute | solution.py:468
  5.8 10.5 %collective-permute-start.3 = (bf16[64,1024]{1,0:T(8,128)(2,1)S(1)}, bf16[64,1024]{1,0:T(8,128)(2,1)S(1)}, u32[]{:S(2)}, u32[]{:S(2)}) collective-permute-start(bf16[64,1024]{1,0:T(8,128)(2,1)S(1)} %pick_rows.3.refs_4_.refs_1_), channel_id=1, source_target_pairs={{0,1},{1,2},{2,3},{3,0},{4,5},{5,6},{6,7},{7,4},{8,9},{9,10},{10,1... | collective-permute-start | bytes 393224 | tf_op jit(solution)/shard_map/ppermute | solution.py:468
  7.4 6.4 %copy-start.19 = (bf16[4096]{0:T(1024)(128)(2,1)S(1)}, bf16[4096]{0:T(1024)(128)(2,1)}, u32[]{:S(2)}) copy-start(bf16[4096]{0:T(1024)(128)(2,1)} %param.10) | copy-start | bytes 24580
  7.9 8.3 %collective-permute-start.2 = (bf16[64,1024]{1,0:T(8,128)(2,1)S(1)}, bf16[64,1024]{1,0:T(8,128)(2,1)S(1)}, u32[]{:S(2)}, u32[]{:S(2)}) collective-permute-start(bf16[64,1024]{1,0:T(8,128)(2,1)S(1)} %pick_rows.2.refs_3_.refs_0_), channel_id=1, source_target_pairs={{0,3},{1,0},{2,1},{3,2},{4,7},{5,4},{6,5},{7,6},{8,11},{9,8},{10,9... | collective-permute-start | bytes 393224 | tf_op jit(solution)/shard_map/ppermute | solution.py:468
  10.0 8.2 %collective-permute-start.1 = (bf16[64,1024]{1,0:T(8,128)(2,1)S(1)}, bf16[64,1024]{1,0:T(8,128)(2,1)S(1)}, u32[]{:S(2)}, u32[]{:S(2)}) collective-permute-start(bf16[64,1024]{1,0:T(8,128)(2,1)S(1)} %pick_rows.2.refs_3_.refs_0_), channel_id=1, source_target_pairs={{0,2},{1,3},{2,0},{3,1},{4,6},{5,7},{6,4},{7,5},{8,10},{9,11},{10,... | collective-permute-start | bytes 393224 | tf_op jit(solution)/shard_map/ppermute | solution.py:468
  11.2 7.1 %collective-permute-start = (bf16[64,1024]{1,0:T(8,128)(2,1)S(1)}, bf16[64,1024]{1,0:T(8,128)(2,1)S(1)}, u32[]{:S(2)}, u32[]{:S(2)}) collective-permute-start(bf16[64,1024]{1,0:T(8,128)(2,1)S(1)} %pick_rows.2.refs_3_.refs_0_), channel_id=1, source_target_pairs={{0,1},{1,2},{2,3},{3,0},{4,5},{5,6},{6,7},{7,4},{8,9},{9,10},{10,1... | collective-permute-start | bytes 393224 | tf_op jit(solution)/shard_map/ppermute | solution.py:468
  13.7 5.5 %collective-permute-start.5 = (bf16[64,1024]{1,0:T(8,128)(2,1)S(1)}, bf16[64,1024]{1,0:T(8,128)(2,1)S(1)}, u32[]{:S(2)}, u32[]{:S(2)}) collective-permute-start(bf16[64,1024]{1,0:T(8,128)(2,1)S(1)} %collective-permute-done.4.refs_7_), channel_id=1, source_target_pairs={{0,3},{1,0},{2,1},{3,2},{4,7},{5,4},{6,5},{7,6},{8,11},{9,8},{10,9... | collective-permute-start | bytes 393224 | tf_op jit(solution)/shard_map/ppermute | solution.py:468
  16.2 3.1 %copy-start.8 = (bf16[4096,128]{1,0:T(8,128)(2,1)S(1)}, bf16[4096,128]{1,0:T(8,128)(2,1)}, u32[]{:S(2)}) copy-start(bf16[4096,128]{1,0:T(8,128)(2,1)} %refs_8_.1) | copy-start | bytes 3145732
  22.8 19.4 %all-to-all-start = ((bf16[8,64,256]{2,1,0:T(8,128)(2,1)}), bf16[8,64,256]{2,1,0:T(8,128)(2,1)S(1)}, u32[]{:S(2)}, u32[]{:S(2)}) async-start(bf16[8,64,256]{2,1,0:T(8,128)(2,1)} %get-tuple-element.26), calls=%async_computation | async-start | bytes 524288 | tf_op jit(solution)/shard_map/all_to_all | solution.py:464
  31.3 6.9 %collective-permute-start.8 = (bf16[64,1024]{1,0:T(8,128)(2,1)S(1)}, bf16[64,1024]{1,0:T(8,128)(2,1)S(1)}, u32[]{:S(2)}, u32[]{:S(2)}) collective-permute-start(bf16[64,1024]{1,0:T(8,128)(2,1)S(1)} %get-tuple-element.29.refs_0_.refs_5_), channel_id=1, source_target_pairs={{0,24},{8,0},{16,8},{24,16},{1,25},{9,1},{17,9},{25,17},{2,26},{10... | collective-permute-start | bytes 393224 | tf_op jit(solution)/shard_map/ppermute | solution.py:468
  34.3 6.6 %collective-permute-start.7 = (bf16[64,1024]{1,0:T(8,128)(2,1)S(1)}, bf16[64,1024]{1,0:T(8,128)(2,1)S(1)}, u32[]{:S(2)}, u32[]{:S(2)}) collective-permute-start(bf16[64,1024]{1,0:T(8,128)(2,1)S(1)} %get-tuple-element.29.refs_0_.refs_5_), channel_id=1, source_target_pairs={{0,16},{8,24},{16,0},{24,8},{1,17},{9,25},{17,1},{25,9},{2,18},{10... | collective-permute-start | bytes 393224 | tf_op jit(solution)/shard_map/ppermute | solution.py:468
  34.9 7.2 %collective-permute-start.6 = (bf16[64,1024]{1,0:T(8,128)(2,1)S(1)}, bf16[64,1024]{1,0:T(8,128)(2,1)S(1)}, u32[]{:S(2)}, u32[]{:S(2)}) collective-permute-start(bf16[64,1024]{1,0:T(8,128)(2,1)S(1)} %get-tuple-element.29.refs_0_.refs_5_), channel_id=1, source_target_pairs={{0,8},{8,16},{16,24},{24,0},{1,9},{9,17},{17,25},{25,1},{2,10},{10... | collective-permute-start | bytes 393224 | tf_op jit(solution)/shard_map/ppermute | solution.py:468
  42.2 1.3 %collective-permute-start.10 = (bf16[64,1024]{1,0:T(8,128)(2,1)S(1)}, bf16[64,1024]{1,0:T(8,128)(2,1)S(1)}, u32[]{:S(2)}, u32[]{:S(2)}) collective-permute-start(bf16[64,1024]{1,0:T(8,128)(2,1)S(1)} %collective-permute-done.6.refs_1_), channel_id=1, source_target_pairs={{0,4},{4,0},{1,5},{5,1},{2,6},{6,2},{3,7},{7,3},{8,12},{12,8},{9,1... | collective-permute-start | bytes 393224 | tf_op jit(solution)/shard_map/ppermute | solution.py:468
  42.2 1.5 %collective-permute-start.11 = (bf16[64,1024]{1,0:T(8,128)(2,1)S(1)}, bf16[64,1024]{1,0:T(8,128)(2,1)S(1)}, u32[]{:S(2)}, u32[]{:S(2)}) collective-permute-start(bf16[64,1024]{1,0:T(8,128)(2,1)S(1)} %collective-permute-done.7.refs_2_), channel_id=1, source_target_pairs={{0,4},{4,0},{1,5},{5,1},{2,6},{6,2},{3,7},{7,3},{8,12},{12,8},{9,1... | collective-permute-start | bytes 393224 | tf_op jit(solution)/shard_map/ppermute | solution.py:468
  42.7 1.3 %collective-permute-start.12 = (bf16[64,1024]{1,0:T(8,128)(2,1)S(1)}, bf16[64,1024]{1,0:T(8,128)(2,1)S(1)}, u32[]{:S(2)}, u32[]{:S(2)}) collective-permute-start(bf16[64,1024]{1,0:T(8,128)(2,1)S(1)} %collective-permute-done.8.refs_3_), channel_id=1, source_target_pairs={{0,4},{4,0},{1,5},{5,1},{2,6},{6,2},{3,7},{7,3},{8,12},{12,8},{9,1... | collective-permute-start | bytes 393224 | tf_op jit(solution)/shard_map/ppermute | solution.py:468
  42.7 1.5 %collective-permute-start.9 = (bf16[64,1024]{1,0:T(8,128)(2,1)S(1)}, bf16[64,1024]{1,0:T(8,128)(2,1)S(1)}, u32[]{:S(2)}, u32[]{:S(2)}) collective-permute-start(bf16[64,1024]{1,0:T(8,128)(2,1)S(1)} %get-tuple-element.29.refs_0_.refs_5_), channel_id=1, source_target_pairs={{0,4},{4,0},{1,5},{5,1},{2,6},{6,2},{3,7},{7,3},{8,12},{12,8},{9,1... | collective-permute-start | bytes 393224 | tf_op jit(solution)/shard_map/ppermute | solution.py:468
  60.0 1.9 %collective-permute-start.13 = (bf16[4,64,1024]{2,1,0:T(8,128)(2,1)S(1)}, bf16[4,64,1024]{2,1,0:T(8,128)(2,1)S(1)}, u32[]{:S(2)}, u32[]{:S(2)}) collective-permute-start(bf16[4,64,1024]{2,1,0:T(8,128)(2,1)S(1)} %get-tuple-element.34), channel_id=1, source_target_pairs={{0,4},{4,0},{1,5},{5,1},{2,6},{6,2},{3,7},{7,3},{8,12},{12,8},{9,1... | collective-permute-start | bytes 1572872 | tf_op jit(solution)/shard_map/ppermute | solution.py:468
  62.7 10.6 %collective-permute-start.14 = (bf16[64,1024]{1,0:T(8,128)(2,1)}, bf16[64,1024]{1,0:T(8,128)(2,1)S(1)}, u32[]{:S(2)}, u32[]{:S(2)}) collective-permute-start(bf16[64,1024]{1,0:T(8,128)(2,1)} %get-tuple-element.36), channel_id=1, source_target_pairs={{0,24},{8,0},{16,8},{24,16},{1,25},{9,1},{17,9},{25,17},{2,26},{10... | collective-permute-start | bytes 393224 | tf_op jit(solution)/shard_map/ppermute | solution.py:468
  63.8 9.4 %collective-permute-start.15 = (bf16[64,1024]{1,0:T(8,128)(2,1)}, bf16[64,1024]{1,0:T(8,128)(2,1)}, u32[]{:S(2)}, u32[]{:S(2)}) collective-permute-start(bf16[64,1024]{1,0:T(8,128)(2,1)} %get-tuple-element.37), channel_id=1, source_target_pairs={{0,16},{8,24},{16,0},{24,8},{1,17},{9,25},{17,1},{25,9},{2,18},{10... | collective-permute-start | bytes 393224 | tf_op jit(solution)/shard_map/ppermute | solution.py:468
  65.3 8.4 %collective-permute-start.16 = (bf16[64,1024]{1,0:T(8,128)(2,1)S(1)}, bf16[64,1024]{1,0:T(8,128)(2,1)}, u32[]{:S(2)}, u32[]{:S(2)}) collective-permute-start(bf16[64,1024]{1,0:T(8,128)(2,1)S(1)} %get-tuple-element.38), channel_id=1, source_target_pairs={{0,8},{8,16},{16,24},{24,0},{1,9},{9,17},{17,25},{25,1},{2,10},{10... | collective-permute-start | bytes 393224 | tf_op jit(solution)/shard_map/ppermute | solution.py:468
  65.3 19.3 %all-to-all-start.2 = ((bf16[8,64,256]{2,1,0:T(8,128)(2,1)}), bf16[8,64,256]{2,1,0:T(8,128)(2,1)S(1)}, u32[]{:S(2)}, u32[]{:S(2)}) async-start(bf16[8,64,256]{2,1,0:T(8,128)(2,1)} %bitcast.2), calls=%async_computation.2 | async-start | bytes 524288 | tf_op jit(solution)/shard_map/all_to_all | solution.py:464
  78.6 14.2 %collective-permute-start.17 = (bf16[64,1024]{1,0:T(8,128)(2,1)}, bf16[64,1024]{1,0:T(8,128)(2,1)}, u32[]{:S(2)}, u32[]{:S(2)}) collective-permute-start(bf16[64,1024]{1,0:T(8,128)(2,1)} %get-tuple-element.40), channel_id=1, source_target_pairs={{0,1},{1,2},{2,3},{3,0},{4,5},{5,6},{6,7},{7,4},{8,9},{9,10},{10,1... | collective-permute-start | bytes 393224 | tf_op jit(solution)/shard_map/ppermute | solution.py:468
  80.4 13.9 %collective-permute-start.18 = (bf16[64,1024]{1,0:T(8,128)(2,1)}, bf16[64,1024]{1,0:T(8,128)(2,1)}, u32[]{:S(2)}, u32[]{:S(2)}) collective-permute-start(bf16[64,1024]{1,0:T(8,128)(2,1)} %get-tuple-element.41), channel_id=1, source_target_pairs={{0,2},{1,3},{2,0},{3,1},{4,6},{5,7},{6,4},{7,5},{8,10},{9,11},{10,... | collective-permute-start | bytes 393224 | tf_op jit(solution)/shard_map/ppermute | solution.py:468
  82.6 11.7 %collective-permute-start.19 = (bf16[64,1024]{1,0:T(8,128)(2,1)}, bf16[64,1024]{1,0:T(8,128)(2,1)}, u32[]{:S(2)}, u32[]{:S(2)}) collective-permute-start(bf16[64,1024]{1,0:T(8,128)(2,1)} %get-tuple-element.42), channel_id=1, source_target_pairs={{0,3},{1,0},{2,1},{3,2},{4,7},{5,4},{6,5},{7,6},{8,11},{9,8},{10,9... | collective-permute-start | bytes 393224 | tf_op jit(solution)/shard_map/ppermute | solution.py:468
  87.8 6.5 %copy-start.10 = (bf16[1024,1024]{1,0:T(8,128)(2,1)S(1)}, bf16[1024,1024]{1,0:T(8,128)(2,1)}, u32[]{:S(2)}) copy-start(bf16[1024,1024]{1,0:T(8,128)(2,1)} %base_ref.2) | copy-start | bytes 6291460
  87.8 6.6 %copy-start.14 = (s32[64]{0:T(128)S(1)}, s32[64]{0:T(128)}, u32[]{:S(2)}) copy-start(s32[64]{0:T(128)} %param.9) | copy-start | bytes 772
  87.8 6.6 %copy-start.16 = (f32[64,128]{1,0:T(8,128)S(1)}, f32[64,128]{1,0:T(8,128)}, u32[]{:S(2)}) copy-start(f32[64,128]{1,0:T(8,128)} %copy-done.15) | copy-start | bytes 98308
  90.0 7.2 %collective-permute-start.20 = (bf16[64,1152]{1,0:T(8,128)(2,1)S(1)}, bf16[64,1152]{1,0:T(8,128)(2,1)S(1)}, u32[]{:S(2)}, u32[]{:S(2)}) collective-permute-start(bf16[64,1152]{1,0:T(8,128)(2,1)S(1)} %get-tuple-element.45), channel_id=1, source_target_pairs={{0,1},{1,2},{2,3},{3,0},{4,5},{5,6},{6,7},{7,4},{8,9},{9,10},{10,1... | collective-permute-start | bytes 442376 | tf_op jit(solution)/shard_map/ppermute | solution.py:468
  90.3 7.5 %collective-permute-start.21 = (bf16[64,1152]{1,0:T(8,128)(2,1)S(1)}, bf16[64,1152]{1,0:T(8,128)(2,1)S(1)}, u32[]{:S(2)}, u32[]{:S(2)}) collective-permute-start(bf16[64,1152]{1,0:T(8,128)(2,1)S(1)} %get-tuple-element.46), channel_id=1, source_target_pairs={{0,2},{1,3},{2,0},{3,1},{4,6},{5,7},{6,4},{7,5},{8,10},{9,11},{10,... | collective-permute-start | bytes 442376 | tf_op jit(solution)/shard_map/ppermute | solution.py:468
  92.8 6.5 %collective-permute-start.22 = (bf16[64,1152]{1,0:T(8,128)(2,1)S(1)}, bf16[64,1152]{1,0:T(8,128)(2,1)S(1)}, u32[]{:S(2)}, u32[]{:S(2)}) collective-permute-start(bf16[64,1152]{1,0:T(8,128)(2,1)S(1)} %get-tuple-element.47), channel_id=1, source_target_pairs={{0,3},{1,0},{2,1},{3,2},{4,7},{5,4},{6,5},{7,6},{8,11},{9,8},{10,9... | collective-permute-start | bytes 442376 | tf_op jit(solution)/shard_map/ppermute | solution.py:468
  94.3 4.9 %copy-start.12 = (bf16[1024,1024]{1,0:T(8,128)(2,1)S(1)}, bf16[1024,1024]{1,0:T(8,128)(2,1)}, u32[]{:S(2)}) copy-start(bf16[1024,1024]{1,0:T(8,128)(2,1)} %base_ref.3) | copy-start | bytes 6291460
  (13 other events, 21.2 us)
